TPU v7x, 32 devices: a whole 2x2x4 slice. The times are simulated.
32 devices in a mesh: ep: 16 (over z, y, core), rep: 2 (over x).
Axes of the slice: x: 2, y: 2, z: 4, core: 2. Of those that a mesh axis runs over, the one named last changes fastest.
Arguments:
- residual: bfloat16 [512, 2048], P('ep'), may hold values from -6 to 6
- query_latent: bfloat16 [512, 8192], P(('ep', 'rep')), may hold values from -32.5 to 32.5
- query_rope: bfloat16 [512, 1024], P(('ep', 'rep')), may hold values from -4 to 4
- cache_latent: bfloat16 [1024, 32, 512], P(('ep', 'rep')), may hold values from -4.6 to 4.6
- cache_rope: bfloat16 [1024, 2048], P(('ep', 'rep')), may hold values from -4 to 4
- page_table: int32 [512, 9], P(('ep', 'rep')), may hold values from 0 to 31, as said below
- lengths: int32 [512], P(('ep', 'rep')), may hold values from 257 to 288, as said below
- value_up: bfloat16 [16, 512, 128], P('rep'), may hold values from -0.25 to 0.25
- out_proj: bfloat16 [2048, 2048], P('rep'), may hold values from -0.125 to 0.125
- routes: int32 [512, 6], P('ep'), may hold values from 0 to 15, all different within a row; in each aligned block of 32 rows (0 to 31, 32 to 63, ...) at most 24 rows name the same one
- route_weight: float32 [512, 6], P('ep'), may hold values from 0.05 to 0.6
- placement: int32 [16], replicated, may hold values from 0 to 15, each once
- expert_gate: bfloat16 [16, 2048, 1408], P('ep', None, 'rep'), may hold values from -0.125 to 0.125
- expert_up: bfloat16 [16, 2048, 1408], P('ep', None, 'rep'), may hold values from -0.125 to 0.125
- expert_down: bfloat16 [16, 1408, 2048], P('ep', 'rep'), may hold values from -0.15625 to 0.15625
- shared_gate: bfloat16 [2048, 1408], P(None, 'rep'), may hold values from -0.125 to 0.125
- shared_up: bfloat16 [2048, 1408], P(None, 'rep'), may hold values from -0.125 to 0.125
- shared_down: bfloat16 [1408, 2048], P('rep'), may hold values from -0.15625 to 0.15625
- norm_gain: float32 [2048], replicated, may hold values from 0.5 to 1.5
Outputs:
- normed: bfloat16 [512, 2048], P(('ep', 'rep'))
Inputs may be any that keep to these rules, and one draw needn't show every extreme that they name: `page_table`: entries number the 32 pages of the row's own device. A device's rows come in consecutive groups of 8 that share their first 8 entries; all other entries of a device are distinct. `lengths`: every row's context covers its shared prompt; the last row of every device has the greatest length. `routes`: within the 32 rows of one index of ep, no expert is named by more than 24 rows, a bound that some block reaches. `placement`: each slot holds exactly one expert.
All inputs are finite; a program needn't handle non-finite values.
Results may differ from a plain program's by a relative error of at most 0.014.
Values may be sent and summed in bfloat16 or wider, within the bound.
No kernel may reach another device: no remote copies, remote signals or barrier semaphores. Data moves between devices by JAX's collectives and lax.ppermute only.
A program may use at most 128 MiB of HBM per device.

v0:
```python
import math

import jax
import jax.numpy as jnp
from jax import lax
from jax.sharding import PartitionSpec as P

ROPE = 64
VHEAD = 128


EPSILON = 1e-06


def attend_rows(query_latent, query_rope, cache_latent, cache_rope, page_table, lengths):
    row_count = page_table.shape[0]
    page_len = cache_latent.shape[1]
    latent_width = cache_latent.shape[2]
    rope_width = cache_rope.shape[1] // page_len
    head_count = query_rope.shape[1] // rope_width
    key_span = page_table.shape[1] * page_len
    keys_lat = cache_latent[page_table].reshape(row_count, key_span, latent_width)
    keys_rope = cache_rope[page_table].reshape(row_count, key_span, rope_width)
    query_lat = query_latent.reshape(row_count, head_count, latent_width)
    query_rot = query_rope.reshape(row_count, head_count, rope_width)
    score_scale = 1.0 / math.sqrt(VHEAD + ROPE)
    scores = (
        jnp.einsum("thr,tlr->thl", query_lat, keys_lat, preferred_element_type=jnp.float32)
        + jnp.einsum("thr,tlr->thl", query_rot, keys_rope, preferred_element_type=jnp.float32)
    ) * score_scale
    live_mask = (jnp.arange(key_span, dtype=jnp.int32)[None, :] < lengths[:, None])[:, None, :]
    masked = jnp.where(live_mask, scores, -jnp.inf)
    row_peak = jnp.max(masked, axis=2, keepdims=True)
    expons = jnp.where(live_mask, jnp.exp(scores - row_peak), 0.0)
    probs = (expons / jnp.sum(expons, axis=2, keepdims=True)).astype(jnp.bfloat16)
    latent_out = jnp.einsum("thl,tlr->thr", probs, keys_lat, preferred_element_type=jnp.float32)
    return latent_out.astype(jnp.bfloat16)


def per_device(
    residual,
    query_latent,
    query_rope,
    cache_latent,
    cache_rope,
    page_table,
    lengths,
    value_up,
    out_proj,
    routes,
    route_weight,
    placement,
    expert_gate,
    expert_up,
    expert_down,
    shared_gate,
    shared_up,
    shared_down,
    norm_gain,
):
    replicas = lax.axis_size("rep")
    expert_groups = lax.axis_size("ep")
    latent_out = attend_rows(
        query_latent, query_rope, cache_latent, cache_rope, page_table, lengths
    )
    own_count = latent_out.shape[0]
    swapped = lax.all_to_all(latent_out, "rep", split_axis=1, concat_axis=0, tiled=True)
    group_rows = swapped.shape[0]
    head_out = jnp.einsum(
        "thr,hrv->thv", swapped, value_up, preferred_element_type=jnp.float32
    ).astype(jnp.bfloat16)
    attn_terms = jnp.dot(
        head_out.reshape(group_rows, -1), out_proj, preferred_element_type=jnp.float32
    )
    attended = lax.psum(attn_terms.astype(jnp.bfloat16), "rep")
    hidden = (residual.astype(jnp.float32) + attended.astype(jnp.float32)).astype(jnp.bfloat16)
    model_width = hidden.shape[1]
    shared_act = (
        jax.nn.silu(jnp.dot(hidden, shared_gate, preferred_element_type=jnp.float32))
        * jnp.dot(hidden, shared_up, preferred_element_type=jnp.float32)
    ).astype(jnp.bfloat16)
    shared_terms = jnp.dot(shared_act, shared_down, preferred_element_type=jnp.float32)
    experts = placement.shape[0]
    route_count = routes.shape[1]
    per_group = experts // expert_groups
    capacity = max(
        replicas, min(group_rows, 2 * group_rows * route_count // experts // replicas * replicas)
    )
    expert_ids = jnp.arange(experts, dtype=jnp.int32)
    slot_index = jnp.sum(jnp.where(routes[:, :, None] == expert_ids, placement, 0), axis=2).reshape(
        -1
    )
    one_hot = (slot_index[:, None] == expert_ids[None, :]).astype(jnp.int32)
    earlier = jnp.cumsum(one_hot, axis=0) - one_hot
    position = jnp.sum(earlier * one_hot, axis=1)
    assignments = slot_index.shape[0]
    source_row = (
        jnp.full((experts * capacity,), group_rows, jnp.int32)
        .at[slot_index * capacity + position]
        .set(jnp.arange(assignments, dtype=jnp.int32) // route_count)
    )
    padded = jnp.concatenate([hidden, jnp.zeros((1, model_width), jnp.bfloat16)], axis=0)
    outgoing = padded[source_row].reshape(expert_groups, per_group * capacity, model_width)
    incoming = lax.all_to_all(outgoing, "ep", split_axis=0, concat_axis=0, tiled=True).reshape(
        expert_groups, per_group, capacity, model_width
    )
    gate_values = jnp.einsum(
        "secd,edf->secf", incoming, expert_gate, preferred_element_type=jnp.float32
    )
    up_values = jnp.einsum(
        "secd,edf->secf", incoming, expert_up, preferred_element_type=jnp.float32
    )
    activated = (jax.nn.silu(gate_values) * up_values).astype(jnp.bfloat16)
    expert_terms = jnp.einsum(
        "secf,efd->secd", activated, expert_down, preferred_element_type=jnp.float32
    )
    outbound = expert_terms.astype(jnp.bfloat16).reshape(
        expert_groups, per_group * capacity, model_width
    )
    returned = lax.all_to_all(outbound, "ep", split_axis=0, concat_axis=0, tiled=True)
    picked = returned.reshape(experts * capacity, model_width)[slot_index * capacity + position]
    weight_used = route_weight.reshape(-1)
    routed = jnp.sum(
        (picked.astype(jnp.float32) * weight_used[:, None]).reshape(
            group_rows, route_count, model_width
        ),
        axis=1,
    )
    row_sums = lax.psum_scatter(
        (routed + shared_terms).astype(jnp.bfloat16), "rep", scatter_dimension=0, tiled=True
    ).astype(jnp.float32)
    own_hidden = lax.dynamic_slice_in_dim(hidden, lax.axis_index("rep") * own_count, own_count, 0)
    mixed = row_sums + own_hidden.astype(jnp.float32)
    inverse = lax.rsqrt(jnp.mean(mixed * mixed, axis=1, keepdims=True) + EPSILON)
    return (mixed * inverse * norm_gain).astype(jnp.bfloat16)


def solution(mesh):
    in_specs = (
        P("ep", None),
        P(("ep", "rep"), None),
        P(("ep", "rep"), None),
        P(("ep", "rep"), None, None),
        P(("ep", "rep"), None),
        P(("ep", "rep"), None),
        P(("ep", "rep")),
        P("rep", None, None),
        P("rep", None),
        P("ep", None),
        P("ep", None),
        P(),
        P("ep", None, "rep"),
        P("ep", None, "rep"),
        P("ep", "rep", None),
        P(None, "rep"),
        P(None, "rep"),
        P("rep", None),
        P(),
    )
    out_specs = P(("ep", "rep"), None)
    return jax.shard_map(
        per_device, mesh=mesh, in_specs=in_specs, out_specs=out_specs, check_vma=False
    )
```

profile of v0, /device:TPU:0, one launch (start us, length us, event | category | flops | bytes accessed | tf_op | source)
XLA Modules:
  0.0 202.1 jit_solution(310415517727903160)
XLA Ops:
  8.3 1.5 reshape.126
  10.8 1.8 gather_fusion.1
  12.6 3.0 %reshape.125 = bf16[16,288,64]{2,1,0:T(8,128)(2,1)} reshape(bf16[144,2048]{1,0:T(8,128)(2,1)} %gather_fusion.1) | data formatting | bytes 1179648 | tf_op jit(solution)/shard_map/reshape | solution.py:23
  15.6 8.7 %gather_fusion = bf16[144,32,512]{2,1,0:T(8,128)(2,1)} fusion(bf16[32,32,512]{2,1,0:T(8,128)(2,1)} %param.22, s32[1024]{0:T(1024)S(1)} %pad_clamp_fusion.2), kind=kCustom, calls=%fused_computation | custom fusion | bytes 9437760 | tf_op jit(solution)/shard_map/gather | solution.py:22
  24.4 3.8 %fusion.63 = f32[16,288,16]{1,2,0:T(8,128)S(1)} fusion(bf16[16,288,512]{2,1,0:T(8,128)(2,1)} %bitcast.101, bf16[16,16,512]{2,1,0:T(8,128)(2,1)S(1)} %bitcast.106), kind=kOutput, calls=%fused_computation.85 | convolution fusion | flops 75497472 | bytes 5275648 | tf_op jit(solution)/shard_map/thr,tlr->thl/dot_general | solution.py:28
  28.8 3.3 %convolution_convert_fusion.1 = bf16[16,16,512]{2,1,0:T(8,128)(2,1)S(1)} fusion(bf16[16,288,512]{2,1,0:T(8,128)(2,1)} %bitcast.102, f32[16,16]{1,0:T(8,128)S(1)} %fusion.62, f32[16,288,16]{1,2,0:T(8,128)S(1)} %fusion.28, pred[16,288]{1,0:T(8,128)(4,1)S(1)} %iota_compare_fusion.1), kind=kOutput, calls=%fused_computation.26 | convolution fusion | flops 75997728 | bytes 5281280 | tf_op jit(solution)/shard_map/thl,tlr->thr/dot_general | solution.py:36
  33.0 4.2 %all-to-all-start = ((bf16[16,16,512]{2,0,1:T(8,128)(2,1)}), bf16[16,16,512]{2,0,1:T(8,128)(2,1)S(1)}, u32[]{:S(2)}, u32[]{:S(2)}) async-start(bf16[16,16,512]{2,0,1:T(8,128)(2,1)} %copy.40), calls=%async_computation | async-start | bytes 524288 | tf_op jit(solution)/shard_map/all_to_all | solution.py:67
  40.6 2.5 %all-to-all-done = bf16[16,16,512]{2,0,1:T(8,128)(2,1)S(1)} async-done(((bf16[16,16,512]{2,0,1:T(8,128)(2,1)}), bf16[16,16,512]{2,0,1:T(8,128)(2,1)S(1)}, u32[]{:S(2)}, u32[]{:S(2)}) %all-to-all-start) | async-done | bytes 262176 | tf_op jit(solution)/shard_map/all_to_all | solution.py:67
  43.1 1.5 fusion.32
  44.6 3.7 %convolution_convert_fusion = bf16[32,2048]{1,0:T(8,128)(2,1)} fusion(bf16[1024,2048]{1,0:T(8,128)(2,1)} %param.27, bf16[8,4,8,128]{3,2,1,0:T(8,128)(2,1)S(1)} %fusion.32), kind=kOutput, calls=%fused_computation.15 | convolution fusion | flops 134283264 | bytes 4390912 | tf_op jit(solution)/shard_map/dot_general | solution.py:72
  48.4 22.1 %all-reduce.4.cloned.1.call-done = bf16[32,2048]{1,0:T(8,128)(2,1)} async-done(((bf16[32,2048]{1,0:T(8,128)(2,1)}), bf16[32,2048]{1,0:T(8,128)(2,1)}) %all-reduce.4.cloned.1.call-update) | async-done | bytes 131088 | tf_op jit(solution)/shard_map/psum | solution.py:75
  71.5 3.1 %gather_fusion.2 = bf16[384,2048]{1,0:T(8,128)(2,1)} fusion(bf16[33,2048]{1,0:T(8,128)(2,1)S(1)} %concatenate.3, s32[1024]{0:T(1024)S(1)} %pad_clamp_fusion.1), kind=kCustom, calls=%fused_computation.2 | custom fusion | bytes 3147264 | tf_op jit(solution)/shard_map/gather | solution.py:103
  74.6 42.0 %all_to_all.28 = bf16[16,24,2048]{2,1,0:T(8,128)(2,1)S(1)} all-to-all(bf16[16,24,2048]{2,1,0:T(8,128)(2,1)} %bitcast.103), channel_id=1, replica_groups=mesh['ep'=16,'rep'=2] {'ep'}, dimensions={0} | all-to-all | bytes 3145728 | tf_op jit(solution)/shard_map/all_to_all | solution.py:104
  117.7 2.5 %fusion.11 = f32[16,1,24,704]{3,2,0,1:T(8,128)} fusion(bf16[16,24,2048]{2,1,0:T(8,128)(2,1)S(1)} %all_to_all.28, bf16[1,2048,704]{1,2,0:T(8,128)(2,1)S(1)} %copy-done.8), kind=kOutput, calls=%fused_computation.17 | convolution fusion | flops 1107296256 | bytes 5537792 | tf_op jit(solution)/shard_map/secd,edf->secf/dot_general | solution.py:107
  120.3 6.9 %fusion.7 = bf16[16,24,2048]{2,1,0:T(8,128)(2,1)} fusion(bf16[1,704,2048]{2,1,0:T(8,128)(2,1)S(1)} %copy-done, bf16[16,24,2048]{2,1,0:T(8,128)(2,1)} %copy-done.3, bf16[1,2048,704]{1,2,0:T(8,128)(2,1)} %param.32, f32[16,1,24,704]{3,2,0,1:T(8,128)} %fusion.11), kind=kOutput, calls=%fused_computation.12 | convolution fusion | flops 2217000960 | bytes 9994240 | tf_op jit(solution)/shard_map/secf,efd->secd/dot_general | solution.py:114
  127.2 5.2 %all-to-all-start.2 = ((bf16[16,24,2048]{2,1,0:T(8,128)(2,1)}), bf16[16,24,2048]{2,1,0:T(8,128)(2,1)}, u32[]{:S(2)}, u32[]{:S(2)}) async-start(bf16[16,24,2048]{2,1,0:T(8,128)(2,1)} %fusion.7), calls=%async_computation.2 | async-start | bytes 3145728 | tf_op jit(solution)/shard_map/all_to_all | solution.py:120
  132.5 2.7 %fusion.64 = f32[32,704]{1,0:T(8,128)S(1)} fusion(bf16[32,2048]{1,0:T(8,128)(2,1)S(1)} %add_convert_fusion, bf16[2048,704]{0,1:T(8,128)(2,1)} %param.34), kind=kOutput, calls=%fused_computation.86 | convolution fusion | flops 92274688 | bytes 3104768 | tf_op jit(solution)/shard_map/dot_general | solution.py:79
  135.2 29.2 %all-to-all-done.2 = bf16[16,24,2048]{2,1,0:T(8,128)(2,1)} async-done(((bf16[16,24,2048]{2,1,0:T(8,128)(2,1)}), bf16[16,24,2048]{2,1,0:T(8,128)(2,1)}, u32[]{:S(2)}, u32[]{:S(2)}) %all-to-all-start.2) | async-done | bytes 1572896 | tf_op jit(solution)/shard_map/all_to_all | solution.py:120
  164.4 4.4 %gather_fusion.3 = bf16[192,2048]{1,0:T(8,128)(2,1)} fusion(bf16[384,2048]{1,0:T(8,128)(2,1)} %bitcast.25, s32[1024]{0:T(1024)S(1)} %pad_clamp_fusion), kind=kCustom, calls=%fused_computation.3 | custom fusion | bytes 1573632 | tf_op jit(solution)/shard_map/gather | solution.py:121
  168.8 2.5 %reshape.137 = f32[32,6,2048]{2,1,0:T(8,128)} reshape(bf16[192,2048]{1,0:T(8,128)(2,1)} %gather_fusion.3) | data formatting | bytes 2359296 | tf_op jit(solution)/shard_map/convert_element_type | solution.py:124
  171.3 2.3 %multiply_reduce_fusion = f32[32,2048]{1,0:T(8,128)S(1)} fusion(f32[32,6,2048]{2,1,0:T(8,128)} %reshape.137, f32[32,6]{1,0:T(8,128)S(1)} %copy.47), kind=kLoop, calls=%fused_computation.16 | loop fusion | flops 720896 | bytes 1835776 | tf_op jit(solution)/shard_map/reduce_sum | solution.py:123
  173.7 5.1 %fusion.10 = bf16[32,2048]{1,0:T(8,128)(2,1)} fusion(f32[32,2048]{1,0:T(8,128)S(1)} %multiply_reduce_fusion, bf16[704,2048]{1,0:T(8,128)(2,1)} %param.36, bf16[32,2048]{1,0:T(8,128)(2,1)S(1)} %add_convert_fusion, bf16[2048,704]{0,1:T(8,128)(2,1)} %param.35, f32[32,704]{1,0:T(8,128)S(1)} %fusion.64), kind=kOutput, calls=%fused_computation.14 | convolution fusion | flops 184815616 | bytes 6381568 | tf_op jit(solution)/shard_map/dot_general | solution.py:82
  178.8 13.9 %reduce-scatter.2.cloned.1.call-done = bf16[16,2048]{1,0:T(8,128)(2,1)} async-done(((bf16[32,2048]{1,0:T(8,128)(2,1)}), bf16[16,2048]{1,0:T(8,128)(2,1)}) %reduce-scatter.2.cloned.1.call-update) | async-done | bytes 65552 | tf_op jit(solution)/shard_map/reduce_scatter | solution.py:129
  193.7 1.6 multiply_convert_fusion
  (56 shorter events, 10.9 us)
Async XLA Ops:
  6.5 113.7 %copy-start = (bf16[1,704,2048]{2,1,0:T(8,128)(2,1)S(1)}, bf16[1,704,2048]{2,1,0:T(8,128)(2,1)}, u32[]{:S(2)}) copy-start(bf16[1,704,2048]{2,1,0:T(8,128)(2,1)} %param.33) | copy-start | bytes 8650756
  6.5 4.3 %copy-start.1 = (bf16[32,2048]{1,0:T(8,128)(2,1)S(1)}, bf16[32,2048]{1,0:T(8,128)(2,1)}, u32[]{:S(2)}) copy-start(bf16[32,2048]{1,0:T(8,128)(2,1)} %param.23) | copy-start | bytes 393220
  24.3 3.8 %copy-start.2 = (bf16[16,288,64]{2,1,0:T(8,128)(2,1)S(1)}, bf16[16,288,64]{2,1,0:T(8,128)(2,1)}, u32[]{:S(2)}) copy-start(bf16[16,288,64]{2,1,0:T(8,128)(2,1)} %reshape.125) | copy-start | bytes 1769476
  24.3 3.8 %copy-start.4 = (bf16[16,16,64]{2,1,0:T(8,128)(2,1)S(1)}, bf16[16,16,64]{2,1,0:T(8,128)(2,1)}, u32[]{:S(2)}) copy-start(bf16[16,16,64]{2,1,0:T(8,128)(2,1)} %reshape.126) | copy-start | bytes 98308
  33.0 10.1 %all-to-all-start = ((bf16[16,16,512]{2,0,1:T(8,128)(2,1)}), bf16[16,16,512]{2,0,1:T(8,128)(2,1)S(1)}, u32[]{:S(2)}, u32[]{:S(2)}) async-start(bf16[16,16,512]{2,0,1:T(8,128)(2,1)} %copy.40), calls=%async_computation | async-start | bytes 524288 | tf_op jit(solution)/shard_map/all_to_all | solution.py:67
  37.2 33.3 %all-reduce.4.cloned.1.call-start = ((), (), s32[]{:S(2)}) async-start(), calls=%async_computation.4 | async-start | bytes 262144 | tf_op jit(solution)/shard_map/psum | solution.py:75
  43.1 27.4 %copy-start.5 = (bf16[32,2048]{1,0:T(8,128)(2,1)S(1)}, bf16[32,2048]{1,0:T(8,128)(2,1)}, u32[]{:S(2)}) copy-start(bf16[32,2048]{1,0:T(8,128)(2,1)} %param.19) | copy-start | bytes 393220
  74.6 43.1 %copy-start.8 = (bf16[1,2048,704]{1,2,0:T(8,128)(2,1)S(1)}, bf16[1,2048,704]{1,2,0:T(8,128)(2,1)}, u32[]{:S(2)}) copy-start(bf16[1,2048,704]{1,2,0:T(8,128)(2,1)} %param.31) | copy-start | bytes 8650756
  116.6 1.1 copy-start.3
  127.2 5.3 %copy-start.7 = (f32[32,6]{0,1:T(8,128)S(1)}, f32[32,6]{0,1:T(8,128)}, u32[]{:S(2)}) copy-start(f32[32,6]{0,1:T(8,128)} %param.29) | copy-start | bytes 2308
  127.2 37.3 %all-to-all-start.2 = ((bf16[16,24,2048]{2,1,0:T(8,128)(2,1)}), bf16[16,24,2048]{2,1,0:T(8,128)(2,1)}, u32[]{:S(2)}, u32[]{:S(2)}) async-start(bf16[16,24,2048]{2,1,0:T(8,128)(2,1)} %fusion.7), calls=%async_computation.2 | async-start | bytes 3145728 | tf_op jit(solution)/shard_map/all_to_all | solution.py:120
  132.4 60.3 %reduce-scatter.2.cloned.1.call-start = ((), (), s32[]{:S(2)}) async-start(), calls=%async_computation.5 | async-start | bytes 196608 | tf_op jit(solution)/shard_map/reduce_scatter | solution.py:129
  173.7 20.0 %copy-start.6 = (f32[2048]{0:T(1024)S(1)}, f32[2048]{0:T(1024)}, u32[]{:S(2)}) copy-start(f32[2048]{0:T(1024)} %param.37) | copy-start | bytes 24580
Sparse Core Ops, SparseCore 0:
  48.5 21.9 all-reduce.3
  178.9 13.7 reduce-scatter.1
where the time goes:
time: 203 us; the launch traced here: 202 us
  waiting for transfers between devices  67.7 us (33%)
  blocking collectives  42 us (21%)
  local copies, waits for them, and re-layouts  30.1 us (15%)
  matrix products  30 us (15%)
  between operations  13.6 us (7%)
  starting transfers between devices  9.47 us (5%)
  other arithmetic  9.26 us (5%)
    all_to_all x1, blocking collectives, per_device(): lax.all_to_all(outgoing, 'ep', split_axis=0, concat_axis=0, tiled=True)  42 us
    all_to_all x1, waiting for transfers between devices, per_device(): lax.all_to_all(outbound, 'ep', split_axis=0, concat_axis=0, tiled=True)  29.2 us
    psum x1, waiting for transfers between devices, per_device(): attended = lax.psum(attn_terms.astype(jnp.bfloat16), 'rep')  22.1 us
    reduce_scatter x1, waiting for transfers between devices, per_device(): lax.psum_scatter((routed + shared_terms).astype(jnp.bfloat16), 'rep', sca...  13.9 us
    gather x1, local copies, waits for them, and re-layouts, attend_rows(): cache_latent[page_table].reshape(row_count, key_span, latent_width)  8.73 us
    dot_general x1, matrix products, per_device(): jnp.einsum('secf,efd->secd', activated, expert_down, preferred_element_ty...  6.89 us
    all_to_all x1, starting transfers between devices, per_device(): lax.all_to_all(outbound, 'ep', split_axis=0, concat_axis=0, tiled=True)  5.21 us
    dot_general x1, matrix products, per_device(): jnp.dot(shared_act, shared_down, preferred_element_type=jnp.float32)  5.09 us
  transfers between devices with their start and end apart: 4, of which 4 were waited for; matrix products, arithmetic and copies ran while one was open for 3% of the time, Pallas kernels for 0%

commit v1 on v0

v1 whole, which is shorter than its diff:
```python
import functools
import math

import jax
import jax.numpy as jnp
from jax import lax
from jax.experimental import pallas as pl
from jax.experimental.pallas import tpu as pltpu
from jax.sharding import PartitionSpec as P

ROPE = 64
VHEAD = 128
LANES = 128
EPSILON = 1e-06
AXES = ("ep", "rep")
MIB = 1024 * 1024
NT = (((1,), (1,)), ((), ()))


def attend_kernel(
    block_ref, table_ref, lengths_ref, query_ref, rot_ref, pages_ref, rope_ref, out_ref, keys_rope
):
    del block_ref
    rows, span = table_ref.shape
    pages, page_len, latent = pages_ref.shape
    keys = pages * page_len
    heads = out_ref.shape[0] // rows
    for pair in range(page_len // 2):
        both = rope_ref[:, pair * LANES : (pair + 1) * LANES].astype(jnp.float32)
        keys_rope[pl.ds(2 * pair, pages, stride=page_len), :] = both
        keys_rope[pl.ds(2 * pair + 1, pages, stride=page_len), :] = pltpu.roll(both, ROPE, 1)
    key_ids = lax.broadcasted_iota(jnp.int32, (rows, keys), 1)
    page_of, slot_of = key_ids // page_len, key_ids % page_len
    lengths = lengths_ref[...]
    count = jnp.zeros((rows, keys), jnp.float32)
    for step in range(span):
        live = (table_ref[:, step : step + 1] == page_of) & (slot_of + step * page_len < lengths)
        count = count + jnp.where(live, 1.0, 0.0)
    low = lax.broadcasted_iota(jnp.int32, (rows, LANES), 1) < ROPE
    lat_parts, rot_parts = [], []
    for head in range(heads):
        lat_parts.append(query_ref[:, head * latent : (head + 1) * latent])
        pair = rot_ref[:, head // 2 * LANES : (head // 2 + 1) * LANES].astype(jnp.float32)
        if head % 2:
            pair = pltpu.roll(pair, ROPE, 1)
        rot_parts.append(jnp.where(low, pair, 0.0).astype(jnp.bfloat16))
    query = jnp.concatenate(lat_parts, axis=0)
    rot = jnp.concatenate(rot_parts, axis=0)
    key_lat = pages_ref[...].reshape(keys, latent)
    key_rot = keys_rope[...].astype(jnp.bfloat16)
    scores = (
        lax.dot_general(query, key_lat, NT, preferred_element_type=jnp.float32)
        + lax.dot_general(rot, key_rot, NT, preferred_element_type=jnp.float32)
    ) * (1.0 / math.sqrt(VHEAD + ROPE))
    scores = scores.reshape(heads, rows, keys)
    masked = jnp.where(count[None] > 0.0, scores, -jnp.inf)
    peak = jnp.max(masked, axis=2, keepdims=True)
    expons = jnp.exp(masked - peak) * count[None]
    probs = (expons / jnp.sum(expons, axis=2, keepdims=True)).astype(jnp.bfloat16)
    out_ref[...] = jnp.dot(
        probs.reshape(heads * rows, keys), key_lat, preferred_element_type=jnp.float32
    ).astype(jnp.bfloat16)


def attend(block, heads, query_latent, query_rope, cache_latent, cache_rope, page_table, lengths):
    rows = page_table.shape[0]
    pages, page_len, latent = cache_latent.shape
    whole = lambda *shape: pl.BlockSpec(shape, lambda i, s: (0,) * len(shape))
    return pl.pallas_call(
        attend_kernel,
        grid_spec=pltpu.PrefetchScalarGridSpec(
            num_scalar_prefetch=1,
            grid=(1,),
            in_specs=[
                whole(*page_table.shape),
                whole(rows, 1),
                pl.BlockSpec((rows, heads * latent), lambda i, s: (0, s[0])),
                pl.BlockSpec((rows, heads * ROPE), lambda i, s: (0, s[0])),
                whole(*cache_latent.shape),
                whole(*cache_rope.shape),
            ],
            out_specs=whole(heads * rows, latent),
            scratch_shapes=[pltpu.VMEM((pages * page_len, LANES), jnp.float32)],
        ),
        out_shape=jax.ShapeDtypeStruct((heads * rows, latent), jnp.bfloat16),
        compiler_params=pltpu.CompilerParams(vmem_limit_bytes=24 * MIB),
        name="attend",
    )(
        block.reshape(1).astype(jnp.int32),
        page_table,
        lengths.reshape(rows, 1),
        query_latent,
        query_rope,
        cache_latent,
        cache_rope,
    )


def project_kernel(parts, value_ref, proj_ref, *refs):
    latents, (out_refs, scratch) = refs[:parts], (refs[parts : 2 * parts], refs[2 * parts :])
    value, proj, value_sem, proj_sem = scratch
    heads, latent, width = value_ref.shape
    rows = latents[0].shape[0] // heads
    chunks, chunk = proj.shape[0], proj.shape[2]
    value_copy = pltpu.make_async_copy(value_ref, value, value_sem)
    value_copy.start()
    copies = []
    for step in range(chunks):
        copies.append(
            pltpu.make_async_copy(
                proj_ref.at[:, pl.ds(step * chunk, chunk)], proj.at[step], proj_sem.at[step]
            )
        )
        copies[-1].start()
    value_copy.wait()
    outs = []
    for head in range(heads):
        both = jnp.concatenate(
            [ref[head * rows : (head + 1) * rows, :] for ref in latents], axis=0
        )
        outs.append(
            jnp.dot(both, value[head], preferred_element_type=jnp.float32).astype(jnp.bfloat16)
        )
    head_out = jnp.concatenate(outs, axis=1)
    for step in range(chunks):
        copies[step].wait()
        terms = jnp.dot(head_out, proj[step], preferred_element_type=jnp.float32)
        for part, out in enumerate(out_refs):
            out[:, step * chunk : (step + 1) * chunk] = terms[
                part * rows : (part + 1) * rows
            ].astype(out.dtype)


def project(latents, out_types, value_up, out_proj):
    heads, latent, width = value_up.shape
    rows = latents[0].shape[0] // heads
    model = out_proj.shape[1]
    chunks = 4
    vmem = pl.BlockSpec(memory_space=pltpu.VMEM)
    hbm = pl.BlockSpec(memory_space=pl.ANY)
    return pl.pallas_call(
        functools.partial(project_kernel, len(latents)),
        in_specs=[hbm, hbm] + [vmem] * len(latents),
        out_specs=[vmem] * len(latents),
        out_shape=[jax.ShapeDtypeStruct((rows, model), kind) for kind in out_types],
        scratch_shapes=[
            pltpu.VMEM(value_up.shape, jnp.bfloat16),
            pltpu.VMEM((chunks, out_proj.shape[0], model // chunks), jnp.bfloat16),
            pltpu.SemaphoreType.DMA,
            pltpu.SemaphoreType.DMA((chunks,)),
        ],
        compiler_params=pltpu.CompilerParams(vmem_limit_bytes=24 * MIB),
        name="project",
    )(value_up, out_proj, *latents)


def expert_kernel(blocks, slot_ref, gate_ref, up_ref, down_ref, *refs):
    inputs, outs, scratch = refs[:blocks], refs[blocks : 2 * blocks], refs[2 * blocks :]
    gate, up, down, act, sems = scratch
    hidden_units, model = gate.shape
    lots = [(0, 256), (256, 256), (512, hidden_units - 512)] if hidden_units > 512 else [
        (0, hidden_units)
    ]
    columns = 512
    copies = []
    for number, (begin, size) in enumerate(lots):
        for kind, (source, target) in enumerate(((gate_ref, gate), (up_ref, up))):
            where = pl.ds(begin, size)
            copies.append(
                pltpu.make_async_copy(source.at[where], target.at[where], sems.at[kind, number])
            )
            copies[-1].start()
    down_copy = pltpu.make_async_copy(down_ref, down, sems.at[2, 0])
    down_copy.start()
    rows = jnp.concatenate([ref[:, :model] for ref in inputs], axis=0)
    tails = jnp.concatenate([ref[:, model:] for ref in inputs], axis=0).astype(jnp.float32)
    lane = lax.broadcasted_iota(jnp.int32, tails.shape, 1)
    half = tails.shape[1] // 2
    slot = slot_ref[0]
    mine = (lane == slot) | (lane == slot + half)
    weight = jnp.sum(jnp.where(mine, tails, 0.0), axis=1, keepdims=True)
    for number, (begin, size) in enumerate(lots):
        copies[2 * number].wait()
        gate_values = lax.dot_general(
            rows, gate[begin : begin + size], NT, preferred_element_type=jnp.float32
        )
        copies[2 * number + 1].wait()
        up_values = lax.dot_general(
            rows, up[begin : begin + size], NT, preferred_element_type=jnp.float32
        )
        act[:, begin : begin + size] = (
            gate_values / (1.0 + jnp.exp(-gate_values)) * up_values
        ).astype(jnp.bfloat16)
    down_copy.wait()
    active = act[...]
    for begin in range(0, model, columns):
        terms = jnp.dot(
            active, down[:, begin : begin + columns], preferred_element_type=jnp.float32
        )
        terms = terms * weight
        at = 0
        for out in outs:
            out[:, begin : begin + columns] = terms[at : at + out.shape[0]].astype(out.dtype)
            at += out.shape[0]


def run_experts(slot, gate, up, down, inputs, out_types):
    hidden_units, model = gate.shape
    total = sum(block.shape[0] for block in inputs)
    vmem = pl.BlockSpec(memory_space=pltpu.VMEM)
    hbm = pl.BlockSpec(memory_space=pl.ANY)
    return pl.pallas_call(
        functools.partial(expert_kernel, len(inputs)),
        in_specs=[pl.BlockSpec(memory_space=pltpu.SMEM), hbm, hbm, hbm] + [vmem] * len(inputs),
        out_specs=[vmem] * len(inputs),
        out_shape=[
            jax.ShapeDtypeStruct((block.shape[0], model), kind)
            for block, kind in zip(inputs, out_types)
        ],
        scratch_shapes=[
            pltpu.VMEM(gate.shape, jnp.bfloat16),
            pltpu.VMEM(up.shape, jnp.bfloat16),
            pltpu.VMEM(down.shape, jnp.bfloat16),
            pltpu.VMEM((total, hidden_units), jnp.bfloat16),
            pltpu.SemaphoreType.DMA((3, 3)),
        ],
        compiler_params=pltpu.CompilerParams(vmem_limit_bytes=40 * MIB),
        name="experts",
    )(slot.reshape(1).astype(jnp.int32), gate, up, down, *inputs)


def shared_terms(rows, shared_gate, shared_up, shared_down):
    act = (
        jax.nn.silu(jnp.dot(rows, shared_gate, preferred_element_type=jnp.float32))
        * jnp.dot(rows, shared_up, preferred_element_type=jnp.float32)
    ).astype(jnp.bfloat16)
    return jnp.dot(act, shared_down, preferred_element_type=jnp.float32)


def exchanges(groups, replicas):
    lines = replicas

    def flip(dz=0, dy=0, dc=0, dx=0):
        pairs = []
        for group in range(groups):
            z, y, core = group // (2 * lines), group // 2 % lines, group % 2
            other = ((z ^ dz) * lines + (y ^ dy)) * 2 + (core ^ dc)
            for rep in range(replicas):
                pairs.append((group * replicas + rep, other * replicas + (rep ^ dx)))
        return pairs

    return lambda value, **by: lax.ppermute(value, AXES, flip(**by))


def route_columns(routes, route_weight, placement):
    experts = placement.shape[0]
    ids = jnp.arange(experts, dtype=jnp.int32)
    slots = jnp.sum(jnp.where(routes[:, :, None] == ids, placement, 0), axis=2)
    table = jnp.sum(jnp.where(slots[:, :, None] == ids, route_weight[:, :, None], 0.0), axis=1)
    half = -(-experts // 64) * 64
    table = jnp.pad(table, ((0, 0), (0, half - experts)))
    high = table.astype(jnp.bfloat16)
    low = (table - high.astype(jnp.float32)).astype(jnp.bfloat16)
    return jnp.concatenate([high, low], axis=1)


def finish(mixed, norm_gain):
    inverse = lax.rsqrt(jnp.mean(mixed * mixed, axis=1, keepdims=True) + EPSILON)
    return (mixed * inverse * norm_gain).astype(jnp.bfloat16)


def per_device(
    residual,
    query_latent,
    query_rope,
    cache_latent,
    cache_rope,
    page_table,
    lengths,
    value_up,
    out_proj,
    routes,
    route_weight,
    placement,
    expert_gate,
    expert_up,
    expert_down,
    shared_gate,
    shared_up,
    shared_down,
    norm_gain,
):
    replicas = lax.axis_size("rep")
    groups = lax.axis_size("ep")
    rep = lax.axis_index("rep")
    slot = lax.axis_index("ep")
    own = page_table.shape[0]
    heads = value_up.shape[0]
    own_rows = lambda value: lax.dynamic_slice_in_dim(value, rep * own, own, 0)
    caches = (query_latent, query_rope, cache_latent, cache_rope, page_table, lengths)
    columns = route_columns(own_rows(routes), own_rows(route_weight), placement)
    own_residual = own_rows(residual)
    gate = expert_gate[0].T
    up = expert_up[0].T
    down = expert_down[0]
    small = replicas == 2 and groups == 16

    if small:
        swap = exchanges(groups, replicas)
        away = attend(1 - rep, heads, *caches)
        arrived = swap(away, dx=1)
        kept = attend(rep, heads, *caches)
        send, keep = project([arrived, kept], [jnp.bfloat16, jnp.float32], value_up, out_proj)
        attended = (keep + swap(send, dx=1).astype(jnp.float32)).astype(jnp.bfloat16)
    else:
        latents = attend(jnp.int32(0), heads * replicas, *caches)
        latents = lax.all_to_all(latents, "rep", 0, 0, tiled=True).reshape(replicas, -1, latents.shape[1])
        terms = project(
            [latents[i] for i in range(replicas)], [jnp.bfloat16] * replicas, value_up, out_proj
        )
        attended = lax.psum_scatter(
            jnp.concatenate(terms, axis=0), "rep", scatter_dimension=0, tiled=True
        )
    hidden = (own_residual.astype(jnp.float32) + attended.astype(jnp.float32)).astype(jnp.bfloat16)
    model = hidden.shape[1]
    block = jnp.concatenate([hidden, columns], axis=1)

    if not small:
        every = lax.all_gather(block, AXES, axis=0, tiled=True)
        inputs = [every[at : at + 512] for at in range(0, every.shape[0], 512)]
        terms = []
        for piece in inputs:
            terms += run_experts(slot, gate, up, down, [piece], [jnp.bfloat16])
        mine = lax.dynamic_slice_in_dim(every, slot * replicas * own, replicas * own, 0)[:, :model]
        shared = shared_terms(mine, shared_gate, shared_up, shared_down).astype(jnp.bfloat16)
        total = lax.psum_scatter(
            jnp.concatenate(terms, axis=0), AXES, scatter_dimension=0, tiled=True
        ).astype(jnp.float32)
        total = total + lax.psum_scatter(
            shared, "rep", scatter_dimension=0, tiled=True
        ).astype(jnp.float32)
        return finish(hidden.astype(jnp.float32) + total, norm_gain)

    line = [block] + [swap(block, dz=step) for step in (1, 2, 3)]
    column = jnp.concatenate(line, axis=0)
    planes = [column, swap(column, dx=1), swap(column, dy=1), swap(column, dx=1, dy=1)]
    others = [swap(plane, dc=1) for plane in planes]
    terms = run_experts(
        slot, gate, up, down, others + planes, [jnp.bfloat16] * 4 + [jnp.bfloat16] * 4
    )
    pair = jnp.concatenate([planes[1][:own, :model], hidden], axis=0)
    shared = shared_terms(pair, shared_gate, shared_up, shared_down)
    crossed = [swap(term, dc=1) for term in terms[:4]]
    sums = [
        mine.astype(jnp.float32) + other.astype(jnp.float32)
        for mine, other in zip(terms[4:], crossed)
    ]
    sums[1] = sums[1] + jnp.pad(shared[:own], ((0, 3 * own), (0, 0)))
    total = sums[0]
    for value, by in zip(sums[1:], (dict(dx=1), dict(dy=1), dict(dx=1, dy=1))):
        total = total + swap(value.astype(jnp.bfloat16), **by).astype(jnp.float32)
    mixed = hidden.astype(jnp.float32) + shared[own:] + total[:own]
    for step in (1, 2, 3):
        piece = total[step * own : (step + 1) * own].astype(jnp.bfloat16)
        mixed = mixed + swap(piece, dz=step).astype(jnp.float32)
    return finish(mixed, norm_gain)


def solution(mesh):
    in_specs = (
        P("ep", None),
        P(("ep", "rep"), None),
        P(("ep", "rep"), None),
        P(("ep", "rep"), None, None),
        P(("ep", "rep"), None),
        P(("ep", "rep"), None),
        P(("ep", "rep")),
        P("rep", None, None),
        P("rep", None),
        P("ep", None),
        P("ep", None),
        P(),
        P("ep", None, "rep"),
        P("ep", None, "rep"),
        P("ep", "rep", None),
        P(None, "rep"),
        P(None, "rep"),
        P("rep", None),
        P(),
    )
    out_specs = P(("ep", "rep"), None)
    return jax.shard_map(
        per_device, mesh=mesh, in_specs=in_specs, out_specs=out_specs, check_vma=False
    )
```

time: 203 us -> 109 us (0.54)
  blocking collectives: 42 us -> 0 us
  waiting for transfers between devices: 67.7 us -> 35.4 us
  matrix products: 30 us -> 7.64 us
  Pallas kernels: 0 us -> 17 us
  between operations: 13.6 us -> 0.24 us
  starting transfers between devices: 9.47 us -> 20.3 us
  other arithmetic: 9.26 us -> 3.35 us
  local copies, waits for them, and re-layouts: 30.1 us -> 24.6 us
    all_to_all x1 -> x0, blocking collectives: 42 us -> none  [per_device(): lax.all_to_all(outgoing, 'ep', split_axis=0, concat_axis=0, tiled=True)]
    ppermute x0 -> x22, waiting for transfers between devices: none -> 35.4 us  [exchanges(): return lambda value, **by: lax.ppermute(value, AXES, flip(**by))]
    all_to_all x2 -> x0, waiting for transfers between devices: 31.7 us -> none  [the longest x1 29.2 us: per_device(): lax.all_to_all(outbound, 'ep', split_axis=0, concat_axis=0, tiled=True)]
    dot_general x9 -> x2, matrix products: 30 us -> 7.64 us  [the longest x1 4.27 us: shared_terms(): return jnp.dot(act, shared_down, preferred_element_type=jnp.float32)]
    psum x1 -> x0, waiting for transfers between devices: 22.1 us -> none  [per_device(): attended = lax.psum(attn_terms.astype(jnp.bfloat16), 'rep')]
    ppermute x0 -> x22, starting transfers between devices: none -> 20.3 us  [exchanges(): return lambda value, **by: lax.ppermute(value, AXES, flip(**by))]
    unnamed x20 -> x60, local copies, waits for them, and re-layouts: 2.3 us -> 21.1 us
    gather x4 -> x0, local copies, waits for them, and re-layouts: 18.1 us -> none  [the longest x1 8.73 us: attend_rows(): cache_latent[page_table].reshape(row_count, key_span, latent_width)]
  transfers between devices with their start and end apart: 4 -> 22, of which waited for: 4 -> 10; matrix products, arithmetic and copies ran while one was open for 3% -> 11% of each run, Pallas kernels for 0% -> 1%
where the time goes in v1:
time: 109 us
  waiting for transfers between devices  35.4 us (32%)
  local copies, waits for them, and re-layouts  24.6 us (23%)
  starting transfers between devices  20.3 us (19%)
  Pallas kernels  17 us (16%)
  matrix products  7.64 us (7%)
  other arithmetic  3.35 us (3%)
    ppermute x22, waiting for transfers between devices, exchanges(): return lambda value, **by: lax.ppermute(value, AXES, flip(**by))  35.4 us
    unnamed x60, local copies, waits for them, and re-layouts  21.1 us
    ppermute x22, starting transfers between devices, exchanges(): return lambda value, **by: lax.ppermute(value, AXES, flip(**by))  20.3 us
    pallas_call x1, Pallas kernels, run_experts(): pl.pallas_call(functools.partial(expert_kernel, len(inputs)), in_specs=[p...  11.9 us
    dot_general x1, matrix products, shared_terms(): return jnp.dot(act, shared_down, preferred_element_type=jnp.float32)  4.27 us
    dot_general x1, matrix products, shared_terms(): jnp.dot(rows, shared_gate, preferred_element_type=jnp.float32)  3.37 us
    pallas_call x2, Pallas kernels, attend(): pl.pallas_call(attend_kernel, grid_spec=pltpu.PrefetchScalarGridSpec(num_...  2.94 us
    pallas_call x1, Pallas kernels, project(): pl.pallas_call(functools.partial(project_kernel, len(latents)), in_specs=...  2.2 us
  transfers between devices with their start and end apart: 22, of which 10 were waited for; matrix products, arithmetic and copies ran while one was open for 11% of the time, Pallas kernels for 1%

profile of v1, /device:TPU:0, one launch (start us, length us, event | category | flops | bytes accessed | tf_op | source)
XLA Modules:
  0.0 108.5 jit_solution(12152695078373525701)
XLA Ops:
  5.4 1.5 %attend.2 = bf16[128,512]{1,0:T(8,128)(2,1)S(1)} custom-call(s32[1]{0:T(128)} %bitcast.block_ref, s32[16,9]{1,0:T(8,128)S(1)} %copy-done.21, s32[16,1]{1,0:T(8,128)S(1)} %copy.24.lengths_ref, bf16[16,8192]{1,0:T(8,128)(2,1)S(1)} %copy-done.8, bf16[16,1024]{1,0:T(8,128)(2,1)S(1)} %copy-done.19, bf16[32,32,512]{2,1,0:T(8,128)(2,1)S(1)} %copy-done.1, ...), custom_call_target="tpu_custom_call" | custom-call | tf_op jit(solution)/shard_map/attend/pallas_call | solution.py:69
  6.9 3.0 %collective-permute-start = (bf16[128,512]{1,0:T(8,128)(2,1)S(1)}, bf16[128,512]{1,0:T(8,128)(2,1)S(1)}, u32[]{:S(2)}, u32[]{:S(2)}) collective-permute-start(bf16[128,512]{1,0:T(8,128)(2,1)S(1)} %attend.2), channel_id=1, source_target_pairs={{0,1},{1,0},{2,3},{3,2},{4,5},{5,4},{6,7},{7,6},{8,9},{9,8},{10,11... | collective-permute-start | bytes 393224 | tf_op jit(solution)/shard_map/ppermute | solution.py:252
  17.0 1.5 %attend.3.refs_1_ = bf16[128,512]{1,0:T(8,128)(2,1)S(1)} custom-call(s32[1]{0:T(128)} %bitcast.2.block_ref, s32[16,9]{1,0:T(8,128)S(1)} %copy-done.22, s32[16,1]{1,0:T(8,128)S(1)} %copy.24.lengths_ref, bf16[16,8192]{1,0:T(8,128)(2,1)S(1)} %copy-done.9, bf16[16,1024]{1,0:T(8,128)(2,1)S(1)} %copy-done.20, bf16[32,32,512]{2,1,0:T(8,128)(2,1)S(1)} %copy-done.2, ...), custom_call_target="tpu_custom_call" | custom-call | tf_op jit(solution)/shard_map/attend/pallas_call | solution.py:69
  18.5 2.2 %copy-done.3 = bf16[1024,2048]{1,0:T(8,128)(2,1)S(1)} copy-done((bf16[1024,2048]{1,0:T(8,128)(2,1)S(1)}, bf16[1024,2048]{1,0:T(8,128)(2,1)}, u32[]{:S(2)}) %copy-start.3) | copy-done | bytes 4194328
  21.9 2.2 %project.1 = (bf16[16,2048]{1,0:T(8,128)(2,1)S(1)}, f32[16,2048]{1,0:T(8,128)S(1)}) custom-call(bf16[8,512,128]{2,1,0:T(8,128)(2,1)S(1)} %copy-done.7, bf16[1024,2048]{1,0:T(8,128)(2,1)S(1)} %copy-done.3, bf16[128,512]{1,0:T(8,128)(2,1)S(1)} %collective-permute-done.refs_0_, bf16[128,512]{1,0:T(8,128)(2,1)S(1)} %attend.3.refs_1_), custom_call_target="tpu_custom_call" | custom-call | tf_op jit(solution)/shard_map/project/pallas_call | solution.py:141
  24.2 4.2 %collective-permute-done.1 = bf16[16,2048]{1,0:T(8,128)(2,1)S(1)} collective-permute-done((bf16[16,2048]{1,0:T(8,128)(2,1)S(1)}, bf16[16,2048]{1,0:T(8,128)(2,1)S(1)}, u32[]{:S(2)}, u32[]{:S(2)}) %collective-permute-start.1) | collective-permute-done | bytes 65568 | tf_op jit(solution)/shard_map/ppermute | solution.py:252
  28.5 1.6 %collective-permute-start.2 = (bf16[16,2176]{1,0:T(8,128)(2,1)S(1)}, bf16[16,2176]{1,0:T(8,128)(2,1)S(1)}, u32[]{:S(2)}, u32[]{:S(2)}) collective-permute-start(bf16[16,2176]{1,0:T(8,128)(2,1)S(1)} %concatenate.9), channel_id=1, source_target_pairs={{0,8},{1,9},{2,10},{3,11},{4,12},{5,13},{6,14},{7,15},{8,0},{9,1},... | collective-permute-start | bytes 208904 | tf_op jit(solution)/shard_map/ppermute | solution.py:252
  30.1 2.6 %collective-permute-start.3 = (bf16[16,2176]{1,0:T(8,128)(2,1)S(1)}, bf16[16,2176]{1,0:T(8,128)(2,1)S(1)}, u32[]{:S(2)}, u32[]{:S(2)}) collective-permute-start(bf16[16,2176]{1,0:T(8,128)(2,1)S(1)} %concatenate.9), channel_id=1, source_target_pairs={{0,16},{1,17},{2,18},{3,19},{4,20},{5,21},{6,22},{7,23},{8,24},{9,... | collective-permute-start | bytes 208904 | tf_op jit(solution)/shard_map/ppermute | solution.py:252
  33.2 3.7 %collective-permute-done.3 = bf16[16,2176]{1,0:T(8,128)(2,1)S(1)} collective-permute-done((bf16[16,2176]{1,0:T(8,128)(2,1)S(1)}, bf16[16,2176]{1,0:T(8,128)(2,1)S(1)}, u32[]{:S(2)}, u32[]{:S(2)}) %collective-permute-start.3) | collective-permute-done | bytes 69664 | tf_op jit(solution)/shard_map/ppermute | solution.py:252
  36.8 2.0 %collective-permute-done.4 = bf16[16,2176]{1,0:T(8,128)(2,1)S(1)} collective-permute-done((bf16[16,2176]{1,0:T(8,128)(2,1)S(1)}, bf16[16,2176]{1,0:T(8,128)(2,1)S(1)}, u32[]{:S(2)}, u32[]{:S(2)}) %collective-permute-start.4) | collective-permute-done | bytes 69664 | tf_op jit(solution)/shard_map/ppermute | solution.py:252
  39.4 2.4 %collective-permute-start.10 = (bf16[64,2176]{1,0:T(8,128)(2,1)S(1)}, bf16[64,2176]{1,0:T(8,128)(2,1)}, u32[]{:S(2)}, u32[]{:S(2)}) collective-permute-start(bf16[64,2176]{1,0:T(8,128)(2,1)S(1)} %pad_maximum_fusion.refs_4_), channel_id=1, source_target_pairs={{0,5},{1,4},{2,7},{3,6},{4,1},{5,0},{6,3},{7,2},{8,13},{9,12},{10,... | collective-permute-start | bytes 835592 | tf_op jit(solution)/shard_map/ppermute | solution.py:252
  42.4 5.5 %collective-permute-done.5.refs_5_ = bf16[64,2176]{1,0:T(8,128)(2,1)S(1)} collective-permute-done((bf16[64,2176]{1,0:T(8,128)(2,1)S(1)}, bf16[64,2176]{1,0:T(8,128)(2,1)S(1)}, u32[]{:S(2)}, u32[]{:S(2)}) %collective-permute-start.5) | collective-permute-done | bytes 278560 | tf_op jit(solution)/shard_map/ppermute | solution.py:252
  47.9 4.1 %collective-permute-done.10.refs_7_ = bf16[64,2176]{1,0:T(8,128)(2,1)} collective-permute-done((bf16[64,2176]{1,0:T(8,128)(2,1)S(1)}, bf16[64,2176]{1,0:T(8,128)(2,1)}, u32[]{:S(2)}, u32[]{:S(2)}) %collective-permute-start.10) | collective-permute-done | bytes 278560 | tf_op jit(solution)/shard_map/ppermute | solution.py:252
  53.5 3.4 %fusion.4 = f32[32,704]{1,0:T(8,128)} fusion(bf16[2048,704]{0,1:T(8,128)(2,1)} %param.34, bf16[16,2048]{1,0:T(8,128)(2,1)S(1)} %add_convert_fusion.3, bf16[16,2048]{1,0:T(8,128)(2,1)S(1)} %slice.31), kind=kOutput, calls=%fused_computation.17 | convolution fusion | flops 92536832 | bytes 3104768 | tf_op jit(solution)/shard_map/dot_general | solution.py:234
  56.9 1.8 %copy-done.5 = bf16[1,2048,704]{1,2,0:T(8,128)(2,1)S(1)} copy-done((bf16[1,2048,704]{1,2,0:T(8,128)(2,1)S(1)}, bf16[1,2048,704]{1,2,0:T(8,128)(2,1)}, u32[]{:S(2)}) %copy-start.5) | copy-done | bytes 2883608
  58.7 1.8 %copy-done.6 = bf16[1,704,2048]{2,1,0:T(8,128)(2,1)S(1)} copy-done((bf16[1,704,2048]{2,1,0:T(8,128)(2,1)S(1)}, bf16[1,704,2048]{2,1,0:T(8,128)(2,1)}, u32[]{:S(2)}) %copy-start.6) | copy-done | bytes 2883608
  60.5 11.9 %experts.1 = (bf16[64,2048]{1,0:T(8,128)(2,1)S(1)}, bf16[64,2048]{1,0:T(8,128)(2,1)}, bf16[64,2048]{1,0:T(8,128)(2,1)S(1)}, bf16[64,2048]{1,0:T(8,128)(2,1)S(1)}...) custom-call(s32[1]{0:T(128)} %bitcast.3.slot_ref, ...), custom_call_target="tpu_custom_call" | custom-call | tf_op jit(solution)/shard_map/experts/pallas_call | solution.py:212
  77.9 4.3 %fusion.5 = f32[32,2048]{1,0:T(8,128)} fusion(bf16[704,2048]{1,0:T(8,128)(2,1)S(1)} %copy-done, f32[32,704]{1,0:T(8,128)} %fusion.4, bf16[2048,704]{0,1:T(8,128)(2,1)} %param.35, bf16[16,2048]{1,0:T(8,128)(2,1)S(1)} %add_convert_fusion.3, bf16[16,2048]{1,0:T(8,128)(2,1)} %copy-done.27), kind=kOutput, calls=%fused_computation.18 | convolution fusion | flops 184946688 | bytes 6250496 | tf_op jit(solution)/shard_map/dot_general | solution.py:237
  86.2 2.5 %collective-permute-start.18 = (bf16[64,2048]{1,0:T(8,128)(2,1)S(1)}, bf16[64,2048]{1,0:T(8,128)(2,1)S(1)}, u32[]{:S(2)}, u32[]{:S(2)}) collective-permute-start(bf16[64,2048]{1,0:T(8,128)(2,1)S(1)} %add_convert_fusion), channel_id=1, source_target_pairs={{0,5},{1,4},{2,7},{3,6},{4,1},{5,0},{6,3},{7,2},{8,13},{9,12},{10,... | collective-permute-start | bytes 786440 | tf_op jit(solution)/shard_map/ppermute | solution.py:252
  88.7 5.3 %collective-permute-done.14 = bf16[64,2048]{1,0:T(8,128)(2,1)S(1)} collective-permute-done((bf16[64,2048]{1,0:T(8,128)(2,1)S(1)}, bf16[64,2048]{1,0:T(8,128)(2,1)S(1)}, u32[]{:S(2)}, u32[]{:S(2)}) %collective-permute-start.14) | collective-permute-done | bytes 262176 | tf_op jit(solution)/shard_map/ppermute | solution.py:252
  94.1 5.6 %collective-permute-done.16 = bf16[64,2048]{1,0:T(8,128)(2,1)S(1)} collective-permute-done((bf16[64,2048]{1,0:T(8,128)(2,1)S(1)}, bf16[64,2048]{1,0:T(8,128)(2,1)S(1)}, u32[]{:S(2)}, u32[]{:S(2)}) %collective-permute-start.16) | collective-permute-done | bytes 262176 | tf_op jit(solution)/shard_map/ppermute | solution.py:252
  99.9 1.6 %collective-permute-start.20 = (bf16[16,2048]{1,0:T(8,128)(2,1)S(1)}, bf16[16,2048]{1,0:T(8,128)(2,1)S(1)}, u32[]{:S(2)}, u32[]{:S(2)}) collective-permute-start(bf16[16,2048]{1,0:T(8,128)(2,1)S(1)} %get-tuple-element.31), channel_id=1, source_target_pairs={{0,16},{1,17},{2,18},{3,19},{4,20},{5,21},{6,22},{7,23},{8,24},{9,... | collective-permute-start | bytes 196616 | tf_op jit(solution)/shard_map/ppermute | solution.py:252
  101.5 2.8 %collective-permute-start.21 = (bf16[16,2048]{1,0:T(8,128)(2,1)S(1)}, bf16[16,2048]{1,0:T(8,128)(2,1)S(1)}, u32[]{:S(2)}, u32[]{:S(2)}) collective-permute-start(bf16[16,2048]{1,0:T(8,128)(2,1)S(1)} %get-tuple-element.30), channel_id=1, source_target_pairs={{0,24},{1,25},{2,26},{3,27},{4,28},{5,29},{6,30},{7,31},{8,16},{9,... | collective-permute-start | bytes 196616 | tf_op jit(solution)/shard_map/ppermute | solution.py:252
  104.3 3.3 %collective-permute-done.20 = bf16[16,2048]{1,0:T(8,128)(2,1)S(1)} collective-permute-done((bf16[16,2048]{1,0:T(8,128)(2,1)S(1)}, bf16[16,2048]{1,0:T(8,128)(2,1)S(1)}, u32[]{:S(2)}, u32[]{:S(2)}) %collective-permute-start.20) | collective-permute-done | bytes 65568 | tf_op jit(solution)/shard_map/ppermute | solution.py:252
  (106 shorter events, 27.6 us)
Async XLA Ops:
  0.0 77.9 %copy-start = (bf16[704,2048]{1,0:T(8,128)(2,1)S(1)}, bf16[704,2048]{1,0:T(8,128)(2,1)}, u32[]{:S(2)}) copy-start(bf16[704,2048]{1,0:T(8,128)(2,1)} %param.36) | copy-start | bytes 8650756
  6.9 11.5 %collective-permute-start = (bf16[128,512]{1,0:T(8,128)(2,1)S(1)}, bf16[128,512]{1,0:T(8,128)(2,1)S(1)}, u32[]{:S(2)}, u32[]{:S(2)}) collective-permute-start(bf16[128,512]{1,0:T(8,128)(2,1)S(1)} %attend.2), channel_id=1, source_target_pairs={{0,1},{1,0},{2,3},{3,2},{4,5},{5,4},{6,7},{7,6},{8,9},{9,8},{10,11... | collective-permute-start | bytes 393224 | tf_op jit(solution)/shard_map/ppermute | solution.py:252
  24.1 4.3 %collective-permute-start.1 = (bf16[16,2048]{1,0:T(8,128)(2,1)S(1)}, bf16[16,2048]{1,0:T(8,128)(2,1)S(1)}, u32[]{:S(2)}, u32[]{:S(2)}) collective-permute-start(bf16[16,2048]{1,0:T(8,128)(2,1)S(1)} %get-tuple-element.16), channel_id=1, source_target_pairs={{0,1},{1,0},{2,3},{3,2},{4,5},{5,4},{6,7},{7,6},{8,9},{9,8},{10,11... | collective-permute-start | bytes 196616 | tf_op jit(solution)/shard_map/ppermute | solution.py:252
  28.5 4.6 %collective-permute-start.2 = (bf16[16,2176]{1,0:T(8,128)(2,1)S(1)}, bf16[16,2176]{1,0:T(8,128)(2,1)S(1)}, u32[]{:S(2)}, u32[]{:S(2)}) collective-permute-start(bf16[16,2176]{1,0:T(8,128)(2,1)S(1)} %concatenate.9), channel_id=1, source_target_pairs={{0,8},{1,9},{2,10},{3,11},{4,12},{5,13},{6,14},{7,15},{8,0},{9,1},... | collective-permute-start | bytes 208904 | tf_op jit(solution)/shard_map/ppermute | solution.py:252
  30.1 6.7 %collective-permute-start.3 = (bf16[16,2176]{1,0:T(8,128)(2,1)S(1)}, bf16[16,2176]{1,0:T(8,128)(2,1)S(1)}, u32[]{:S(2)}, u32[]{:S(2)}) collective-permute-start(bf16[16,2176]{1,0:T(8,128)(2,1)S(1)} %concatenate.9), channel_id=1, source_target_pairs={{0,16},{1,17},{2,18},{3,19},{4,20},{5,21},{6,22},{7,23},{8,24},{9,... | collective-permute-start | bytes 208904 | tf_op jit(solution)/shard_map/ppermute | solution.py:252
  32.7 6.1 %collective-permute-start.4 = (bf16[16,2176]{1,0:T(8,128)(2,1)S(1)}, bf16[16,2176]{1,0:T(8,128)(2,1)S(1)}, u32[]{:S(2)}, u32[]{:S(2)}) collective-permute-start(bf16[16,2176]{1,0:T(8,128)(2,1)S(1)} %concatenate.9), channel_id=1, source_target_pairs={{0,24},{1,25},{2,26},{3,27},{4,28},{5,29},{6,30},{7,31},{8,16},{9,... | collective-permute-start | bytes 208904 | tf_op jit(solution)/shard_map/ppermute | solution.py:252
  38.8 9.1 %collective-permute-start.5 = (bf16[64,2176]{1,0:T(8,128)(2,1)S(1)}, bf16[64,2176]{1,0:T(8,128)(2,1)S(1)}, u32[]{:S(2)}, u32[]{:S(2)}) collective-permute-start(bf16[64,2176]{1,0:T(8,128)(2,1)S(1)} %pad_maximum_fusion.refs_4_), channel_id=1, source_target_pairs={{0,1},{1,0},{2,3},{3,2},{4,5},{5,4},{6,7},{7,6},{8,9},{9,8},{10,11... | collective-permute-start | bytes 835592 | tf_op jit(solution)/shard_map/ppermute | solution.py:252
  39.4 12.6 %collective-permute-start.10 = (bf16[64,2176]{1,0:T(8,128)(2,1)S(1)}, bf16[64,2176]{1,0:T(8,128)(2,1)}, u32[]{:S(2)}, u32[]{:S(2)}) collective-permute-start(bf16[64,2176]{1,0:T(8,128)(2,1)S(1)} %pad_maximum_fusion.refs_4_), channel_id=1, source_target_pairs={{0,5},{1,4},{2,7},{3,6},{4,1},{5,0},{6,3},{7,2},{8,13},{9,12},{10,... | collective-permute-start | bytes 835592 | tf_op jit(solution)/shard_map/ppermute | solution.py:252
  41.9 11.6 %collective-permute-start.8 = (bf16[64,2176]{1,0:T(8,128)(2,1)S(1)}, bf16[64,2176]{1,0:T(8,128)(2,1)}, u32[]{:S(2)}, u32[]{:S(2)}) collective-permute-start(bf16[64,2176]{1,0:T(8,128)(2,1)S(1)} %pad_maximum_fusion.refs_4_), channel_id=1, source_target_pairs={{0,4},{1,5},{2,6},{3,7},{4,0},{5,1},{6,2},{7,3},{8,12},{9,13},{10,... | collective-permute-start | bytes 835592 | tf_op jit(solution)/shard_map/ppermute | solution.py:252
  42.4 14.4 %collective-permute-start.6 = (bf16[64,2176]{1,0:T(8,128)(2,1)S(1)}, bf16[64,2176]{1,0:T(8,128)(2,1)S(1)}, u32[]{:S(2)}, u32[]{:S(2)}) collective-permute-start(bf16[64,2176]{1,0:T(8,128)(2,1)S(1)} %pad_maximum_fusion.refs_4_), channel_id=1, source_target_pairs={{0,2},{1,3},{2,0},{3,1},{4,6},{5,7},{6,4},{7,5},{8,10},{9,11},{10,... | collective-permute-start | bytes 835592 | tf_op jit(solution)/shard_map/ppermute | solution.py:252
  47.9 8.9 %collective-permute-start.7 = (bf16[64,2176]{1,0:T(8,128)(2,1)S(1)}, bf16[64,2176]{1,0:T(8,128)(2,1)S(1)}, u32[]{:S(2)}, u32[]{:S(2)}) collective-permute-start(bf16[64,2176]{1,0:T(8,128)(2,1)S(1)} %collective-permute-done.5.refs_5_), channel_id=1, source_target_pairs={{0,2},{1,3},{2,0},{3,1},{4,6},{5,7},{6,4},{7,5},{8,10},{9,11},{10,... | collective-permute-start | bytes 835592 | tf_op jit(solution)/shard_map/ppermute | solution.py:252
  52.1 4.7 %collective-permute-start.11 = (bf16[64,2176]{1,0:T(8,128)(2,1)}, bf16[64,2176]{1,0:T(8,128)(2,1)S(1)}, u32[]{:S(2)}, u32[]{:S(2)}) collective-permute-start(bf16[64,2176]{1,0:T(8,128)(2,1)} %collective-permute-done.10.refs_7_), channel_id=1, source_target_pairs={{0,2},{1,3},{2,0},{3,1},{4,6},{5,7},{6,4},{7,5},{8,10},{9,11},{10,... | collective-permute-start | bytes 835592 | tf_op jit(solution)/shard_map/ppermute | solution.py:252
  53.4 3.4 %collective-permute-start.9 = (bf16[64,2176]{1,0:T(8,128)(2,1)}, bf16[64,2176]{1,0:T(8,128)(2,1)S(1)}, u32[]{:S(2)}, u32[]{:S(2)}) collective-permute-start(bf16[64,2176]{1,0:T(8,128)(2,1)} %collective-permute-done.8.refs_6_), channel_id=1, source_target_pairs={{0,2},{1,3},{2,0},{3,1},{4,6},{5,7},{6,4},{7,5},{8,10},{9,11},{10,... | collective-permute-start | bytes 835592 | tf_op jit(solution)/shard_map/ppermute | solution.py:252
  77.3 6.4 %collective-permute-start.13 = (bf16[64,2048]{1,0:T(8,128)(2,1)}, bf16[64,2048]{1,0:T(8,128)(2,1)}, u32[]{:S(2)}, u32[]{:S(2)}) collective-permute-start(bf16[64,2048]{1,0:T(8,128)(2,1)} %get-tuple-element.20), channel_id=1, source_target_pairs={{0,2},{1,3},{2,0},{3,1},{4,6},{5,7},{6,4},{7,5},{8,10},{9,11},{10,... | collective-permute-start | bytes 786440 | tf_op jit(solution)/shard_map/ppermute | solution.py:252
  82.1 25.5 %copy-start.26 = (f32[32,2048]{1,0:T(8,128)S(1)}, f32[32,2048]{1,0:T(8,128)}, u32[]{:S(2)}) copy-start(f32[32,2048]{1,0:T(8,128)} %fusion.5) | copy-start | bytes 786436
  83.1 2.4 %collective-permute-start.15 = (bf16[64,2048]{1,0:T(8,128)(2,1)}, bf16[64,2048]{1,0:T(8,128)(2,1)S(1)}, u32[]{:S(2)}, u32[]{:S(2)}) collective-permute-start(bf16[64,2048]{1,0:T(8,128)(2,1)} %copy-done.25), channel_id=1, source_target_pairs={{0,2},{1,3},{2,0},{3,1},{4,6},{5,7},{6,4},{7,5},{8,10},{9,11},{10,... | collective-permute-start | bytes 786440 | tf_op jit(solution)/shard_map/ppermute | solution.py:252
  83.3 2.9 %collective-permute-start.17 = (bf16[64,2048]{1,0:T(8,128)(2,1)}, bf16[64,2048]{1,0:T(8,128)(2,1)S(1)}, u32[]{:S(2)}, u32[]{:S(2)}) collective-permute-start(bf16[64,2048]{1,0:T(8,128)(2,1)} %copy-done.24), channel_id=1, source_target_pairs={{0,2},{1,3},{2,0},{3,1},{4,6},{5,7},{6,4},{7,5},{8,10},{9,11},{10,... | collective-permute-start | bytes 786440 | tf_op jit(solution)/shard_map/ppermute | solution.py:252
  83.7 5.0 %collective-permute-start.12 = (bf16[64,2048]{1,0:T(8,128)(2,1)}, bf16[64,2048]{1,0:T(8,128)(2,1)S(1)}, u32[]{:S(2)}, u32[]{:S(2)}) collective-permute-start(bf16[64,2048]{1,0:T(8,128)(2,1)} %copy-done.23), channel_id=1, source_target_pairs={{0,2},{1,3},{2,0},{3,1},{4,6},{5,7},{6,4},{7,5},{8,10},{9,11},{10,... | collective-permute-start | bytes 786440 | tf_op jit(solution)/shard_map/ppermute | solution.py:252
  84.9 9.2 %collective-permute-start.14 = (bf16[64,2048]{1,0:T(8,128)(2,1)S(1)}, bf16[64,2048]{1,0:T(8,128)(2,1)S(1)}, u32[]{:S(2)}, u32[]{:S(2)}) collective-permute-start(bf16[64,2048]{1,0:T(8,128)(2,1)S(1)} %add_convert_fusion.2), channel_id=1, source_target_pairs={{0,1},{1,0},{2,3},{3,2},{4,5},{5,4},{6,7},{7,6},{8,9},{9,8},{10,11... | collective-permute-start | bytes 786440 | tf_op jit(solution)/shard_map/ppermute | solution.py:252
  85.6 14.1 %collective-permute-start.16 = (bf16[64,2048]{1,0:T(8,128)(2,1)S(1)}, bf16[64,2048]{1,0:T(8,128)(2,1)S(1)}, u32[]{:S(2)}, u32[]{:S(2)}) collective-permute-start(bf16[64,2048]{1,0:T(8,128)(2,1)S(1)} %add_convert_fusion.1), channel_id=1, source_target_pairs={{0,4},{1,5},{2,6},{3,7},{4,0},{5,1},{6,2},{7,3},{8,12},{9,13},{10,... | collective-permute-start | bytes 786440 | tf_op jit(solution)/shard_map/ppermute | solution.py:252
  86.2 13.4 %collective-permute-start.18 = (bf16[64,2048]{1,0:T(8,128)(2,1)S(1)}, bf16[64,2048]{1,0:T(8,128)(2,1)S(1)}, u32[]{:S(2)}, u32[]{:S(2)}) collective-permute-start(bf16[64,2048]{1,0:T(8,128)(2,1)S(1)} %add_convert_fusion), channel_id=1, source_target_pairs={{0,5},{1,4},{2,7},{3,6},{4,1},{5,0},{6,3},{7,2},{8,13},{9,12},{10,... | collective-permute-start | bytes 786440 | tf_op jit(solution)/shard_map/ppermute | solution.py:252
  99.8 4.5 %collective-permute-start.19 = (bf16[16,2048]{1,0:T(8,128)(2,1)S(1)}, bf16[16,2048]{1,0:T(8,128)(2,1)S(1)}, u32[]{:S(2)}, u32[]{:S(2)}) collective-permute-start(bf16[16,2048]{1,0:T(8,128)(2,1)S(1)} %get-tuple-element.29), channel_id=1, source_target_pairs={{0,8},{1,9},{2,10},{3,11},{4,12},{5,13},{6,14},{7,15},{8,0},{9,1},... | collective-permute-start | bytes 196616 | tf_op jit(solution)/shard_map/ppermute | solution.py:252
  99.9 7.7 %collective-permute-start.20 = (bf16[16,2048]{1,0:T(8,128)(2,1)S(1)}, bf16[16,2048]{1,0:T(8,128)(2,1)S(1)}, u32[]{:S(2)}, u32[]{:S(2)}) collective-permute-start(bf16[16,2048]{1,0:T(8,128)(2,1)S(1)} %get-tuple-element.31), channel_id=1, source_target_pairs={{0,16},{1,17},{2,18},{3,19},{4,20},{5,21},{6,22},{7,23},{8,24},{9,... | collective-permute-start | bytes 196616 | tf_op jit(solution)/shard_map/ppermute | solution.py:252
  101.5 6.2 %collective-permute-start.21 = (bf16[16,2048]{1,0:T(8,128)(2,1)S(1)}, bf16[16,2048]{1,0:T(8,128)(2,1)S(1)}, u32[]{:S(2)}, u32[]{:S(2)}) collective-permute-start(bf16[16,2048]{1,0:T(8,128)(2,1)S(1)} %get-tuple-element.30), channel_id=1, source_target_pairs={{0,24},{1,25},{2,26},{3,27},{4,28},{5,29},{6,30},{7,31},{8,16},{9,... | collective-permute-start | bytes 196616 | tf_op jit(solution)/shard_map/ppermute | solution.py:252
  (28 other events, 115.1 us)

commit v2 on v0

v2 whole, which is shorter than its diff:
```python
import functools
import math

import jax
import jax.numpy as jnp
from jax import lax
from jax.experimental import pallas as pl
from jax.experimental.pallas import tpu as pltpu
from jax.sharding import PartitionSpec as P

ROPE = 64
VHEAD = 128
LANES = 128
EPSILON = 1e-06
AXES = ("ep", "rep")
MIB = 1024 * 1024
NT = (((1,), (1,)), ((), ()))


def in_hbm(value):
    return pltpu.with_memory_space_constraint(value, pltpu.HBM)


def attend_heads(query_ref, rot_ref, key_lat, key_rot, count, out_ref, before_latent, before_keys):
    rows, keys = count.shape
    latent = key_lat.shape[1]
    heads = out_ref.shape[0] // rows
    low = lax.broadcasted_iota(jnp.int32, (rows, LANES), 1) < ROPE
    rot_parts = []
    for head in range(heads):
        pair = rot_ref[:, head // 2 * LANES : (head // 2 + 1) * LANES].astype(jnp.float32)
        if head % 2:
            pair = pltpu.roll(pair, ROPE, 1)
        rot_parts.append(jnp.where(low, pair, 0.0).astype(jnp.bfloat16))
    rot = jnp.concatenate(rot_parts, axis=0)
    scores = lax.dot_general(rot, key_rot[...], NT, preferred_element_type=jnp.float32)
    before_latent()
    query = jnp.concatenate(
        [query_ref[:, head * latent : (head + 1) * latent] for head in range(heads)], axis=0
    )
    before_keys()
    scores = (
        lax.dot_general(query, key_lat[...], NT, preferred_element_type=jnp.float32) + scores
    ) * (1.0 / math.sqrt(VHEAD + ROPE))
    scores = scores.reshape(heads, rows, keys)
    counts = count[...][None]
    masked = jnp.where(counts > 0.0, scores, -jnp.inf)
    peak = jnp.max(masked, axis=2, keepdims=True)
    expons = jnp.exp(masked - peak) * counts
    probs = (expons / jnp.sum(expons, axis=2, keepdims=True)).astype(jnp.bfloat16)
    out_ref[...] = jnp.dot(
        probs.reshape(heads * rows, keys), key_lat[...], preferred_element_type=jnp.float32
    ).astype(jnp.bfloat16)


def head_columns(ref, head_block, width):
    return ref.at[:, pl.ds(pl.multiple_of(head_block * width, LANES), width)]


def attend_kernel(
    block_ref,
    lengths_hbm,
    table_hbm,
    query_hbm,
    rot_hbm,
    pages_hbm,
    rope_hbm,
    out_ref,
    key_lat,
    key_rot,
    count,
    lengths_ref,
    table_ref,
    query_ref,
    rot_ref,
    rope_ref,
    keys_rope,
    sems,
):
    rows, span = table_ref.shape
    pages, page_len, latent = pages_hbm.shape
    keys = pages * page_len
    copies = [
        pltpu.make_async_copy(source, target, sems.at[number])
        for number, (source, target) in enumerate(
            (
                (rope_hbm, rope_ref),
                (table_hbm, table_ref),
                (lengths_hbm, lengths_ref),
                (head_columns(rot_hbm, block_ref[0], rot_ref.shape[1]), rot_ref),
                (head_columns(query_hbm, block_ref[0], query_ref.shape[1]), query_ref),
                (pages_hbm, key_lat.reshape(pages, page_len, latent)),
            )
        )
    ]
    for copy in copies:
        copy.start()
    copies[0].wait()
    for pair in range(page_len // 2):
        both = rope_ref[:, pair * LANES : (pair + 1) * LANES].astype(jnp.float32)
        keys_rope[pl.ds(2 * pair, pages, stride=page_len), :] = both
        keys_rope[pl.ds(2 * pair + 1, pages, stride=page_len), :] = pltpu.roll(both, ROPE, 1)
    key_rot[...] = keys_rope[...].astype(jnp.bfloat16)
    copies[1].wait()
    copies[2].wait()
    row_ids = lax.broadcasted_iota(jnp.int32, (rows, LANES), 0)
    lengths = jnp.zeros((rows, LANES), jnp.int32)
    for row in range(rows):
        lengths = jnp.where(row_ids == row, lengths_ref[row], lengths)
    lengths = lengths[:, :1]
    key_ids = lax.broadcasted_iota(jnp.int32, (rows, keys), 1)
    page_of, slot_of = key_ids // page_len, key_ids % page_len
    total = jnp.zeros((rows, keys), jnp.float32)
    for step in range(span):
        live = (table_ref[:, step : step + 1] == page_of) & (slot_of + step * page_len < lengths)
        total = total + jnp.where(live, 1.0, 0.0)
    count[...] = total
    copies[3].wait()
    attend_heads(
        query_ref, rot_ref, key_lat, key_rot, count, out_ref, copies[4].wait, copies[5].wait
    )


def attend(block, heads, query_latent, query_rope, cache_latent, cache_rope, page_table, lengths):
    rows = page_table.shape[0]
    pages, page_len, latent = cache_latent.shape
    keys = pages * page_len
    operands = (lengths, page_table, query_latent, query_rope, cache_latent, cache_rope)
    out, *prepared = pl.pallas_call(
        attend_kernel,
        in_specs=[pl.BlockSpec(memory_space=pltpu.SMEM)]
        + [pl.BlockSpec(memory_space=pl.ANY)] * len(operands),
        out_specs=[pl.BlockSpec(memory_space=pltpu.VMEM)] * 4,
        out_shape=[
            pltpu.VMEM((heads * rows, latent), jnp.bfloat16),
            pltpu.VMEM((keys, latent), jnp.bfloat16),
            pltpu.VMEM((keys, LANES), jnp.bfloat16),
            pltpu.VMEM((rows, keys), jnp.float32),
        ],
        scratch_shapes=[
            pltpu.SMEM(lengths.shape, jnp.int32),
            pltpu.VMEM(page_table.shape, jnp.int32),
            pltpu.VMEM((rows, heads * latent), jnp.bfloat16),
            pltpu.VMEM((rows, heads * ROPE), jnp.bfloat16),
            pltpu.VMEM(cache_rope.shape, jnp.bfloat16),
            pltpu.VMEM((keys, LANES), jnp.float32),
            pltpu.SemaphoreType.DMA((len(operands),)),
        ],
        compiler_params=pltpu.CompilerParams(vmem_limit_bytes=16 * MIB),
        cost_estimate=pl.CostEstimate(
            flops=4 * heads * rows * keys * latent,
            bytes_accessed=4 * MIB,
            transcendentals=heads * rows * keys,
        ),
        name="attend",
    )(block.reshape(1).astype(jnp.int32), *[in_hbm(value) for value in operands])
    return out, prepared


def attend_more_kernel(
    staged, block_ref, key_lat, key_rot, count, query_hbm, rot_hbm, *refs
):
    sources, (out_ref, *targets) = refs[:staged], refs[staged : 2 * staged + 1]
    query_ref, rot_ref, sems = refs[2 * staged + 1 :]
    copies = [
        pltpu.make_async_copy(source, target, sems.at[number])
        for number, (source, target) in enumerate(
            (
                (head_columns(rot_hbm, block_ref[0], rot_ref.shape[1]), rot_ref),
                (head_columns(query_hbm, block_ref[0], query_ref.shape[1]), query_ref),
                *zip(sources, targets),
            )
        )
    ]
    for copy in copies:
        copy.start()
    copies[0].wait()
    attend_heads(
        query_ref, rot_ref, key_lat, key_rot, count, out_ref, copies[1].wait, lambda: None
    )
    for copy in copies[2:]:
        copy.wait()


def attend_more(block, heads, prepared, query_latent, query_rope, values):
    key_lat, key_rot, count = prepared
    rows, keys = count.shape
    latent = key_lat.shape[1]
    vmem = pl.BlockSpec(memory_space=pltpu.VMEM)
    anywhere = pl.BlockSpec(memory_space=pl.ANY)
    return pl.pallas_call(
        functools.partial(attend_more_kernel, len(values)),
        in_specs=[pl.BlockSpec(memory_space=pltpu.SMEM)] + [vmem] * 3 + [anywhere] * (2 + len(values)),
        out_specs=[vmem] * (1 + len(values)),
        out_shape=[pltpu.VMEM((heads * rows, latent), jnp.bfloat16)]
        + [pltpu.VMEM(value.shape, value.dtype) for value in values],
        scratch_shapes=[
            pltpu.VMEM((rows, heads * latent), jnp.bfloat16),
            pltpu.VMEM((rows, heads * ROPE), jnp.bfloat16),
            pltpu.SemaphoreType.DMA((2 + len(values),)),
        ],
        compiler_params=pltpu.CompilerParams(vmem_limit_bytes=16 * MIB),
        cost_estimate=pl.CostEstimate(
            flops=4 * heads * rows * keys * latent,
            bytes_accessed=8 * MIB,
            transcendentals=heads * rows * keys,
        ),
        name="attend_more",
    )(
        block.reshape(1).astype(jnp.int32),
        *prepared,
        *[in_hbm(value) for value in (query_latent, query_rope, *values)],
    )


def project_kernel(parts, value_ref, proj_ref, *refs):
    latents, out_refs = refs[:parts], refs[parts : 2 * parts]
    heads, latent, width = value_ref.shape
    rows = latents[0].shape[0] // heads
    outs = []
    for head in range(heads):
        both = jnp.concatenate(
            [ref[head * rows : (head + 1) * rows, :] for ref in latents], axis=0
        )
        outs.append(
            jnp.dot(both, value_ref[head], preferred_element_type=jnp.float32).astype(jnp.bfloat16)
        )
    head_out = jnp.concatenate(outs, axis=1)
    chunk = 512
    for begin in range(0, proj_ref.shape[1], chunk):
        terms = jnp.dot(
            head_out, proj_ref[:, begin : begin + chunk], preferred_element_type=jnp.float32
        )
        for part, out in enumerate(out_refs):
            out[:, begin : begin + chunk] = terms[part * rows : (part + 1) * rows].astype(out.dtype)


def project(latents, out_types, value_up, out_proj):
    heads, latent, width = value_up.shape
    rows = latents[0].shape[0] // heads
    model = out_proj.shape[1]
    vmem = pl.BlockSpec(memory_space=pltpu.VMEM)
    return pl.pallas_call(
        functools.partial(project_kernel, len(latents)),
        in_specs=[vmem] * (2 + len(latents)),
        out_specs=[vmem] * len(latents),
        out_shape=[pltpu.VMEM((rows, model), kind) for kind in out_types],
        compiler_params=pltpu.CompilerParams(vmem_limit_bytes=16 * MIB),
        cost_estimate=pl.CostEstimate(
            flops=2 * len(latents) * rows * out_proj.size,
            bytes_accessed=2 * (value_up.size + out_proj.size),
            transcendentals=0,
        ),
        name="project",
    )(value_up, out_proj, *latents)


def stage_kernel(count, after_ref, *refs):
    del after_ref
    sources, targets, (token, sems) = refs[:count], refs[count : 2 * count], refs[2 * count :]
    copies = [
        pltpu.make_async_copy(source, target, sems.at[number])
        for number, (source, target) in enumerate(zip(sources, targets))
    ]
    for copy in copies:
        copy.start()
    token[...] = jnp.zeros_like(token)
    for copy in copies:
        copy.wait()


def stage(after, values):
    anywhere = pl.BlockSpec(memory_space=pl.ANY)
    *staged, token = pl.pallas_call(
        functools.partial(stage_kernel, len(values)),
        in_specs=[anywhere] * (1 + len(values)),
        out_specs=[pl.BlockSpec(memory_space=pltpu.VMEM)] * (1 + len(values)),
        out_shape=[pltpu.VMEM(value.shape, value.dtype) for value in values]
        + [jax.ShapeDtypeStruct((8, LANES), jnp.float32)],
        scratch_shapes=[pltpu.SemaphoreType.DMA((len(values),))],
        compiler_params=pltpu.CompilerParams(vmem_limit_bytes=16 * MIB),
        cost_estimate=pl.CostEstimate(
            flops=0,
            bytes_accessed=2 * sum(value.size * value.dtype.itemsize for value in values),
            transcendentals=0,
        ),
        name="stage",
    )(after, *[in_hbm(value) for value in values])
    return staged, token


def lots_of(units):
    return [(begin, min(256, units - begin)) for begin in range(0, units, 256)]


def activate(rows, gate, up):
    gate_values = lax.dot_general(rows, gate, NT, preferred_element_type=jnp.float32)
    up_values = lax.dot_general(rows, up, NT, preferred_element_type=jnp.float32)
    return (gate_values / (1.0 + jnp.exp(-gate_values)) * up_values).astype(jnp.bfloat16)


def expert_kernel(blocks, slot_ref, after_ref, gate_ref, up_ref, down_ref, *refs):
    del after_ref
    inputs, outs, (rows, act) = refs[:blocks], refs[blocks : 2 * blocks], refs[2 * blocks :]
    units, model = gate_ref.shape
    columns = 512
    slot = slot_ref[0]
    weights, at = [], 0
    for ref in inputs:
        rows[at : at + ref.shape[0], :] = ref[:, :model]
        at += ref.shape[0]
        tail = ref[:, model:].astype(jnp.float32)
        lane = lax.broadcasted_iota(jnp.int32, tail.shape, 1)
        mine = (lane == slot) | (lane == slot + tail.shape[1] // 2)
        weights.append(jnp.sum(jnp.where(mine, tail, 0.0), axis=1, keepdims=True))
    weight = jnp.concatenate(weights, axis=0)
    for begin, size in lots_of(units):
        lot = pl.ds(begin, size)
        act[:, begin : begin + size] = activate(rows[...], gate_ref[lot, :], up_ref[lot, :])
    for begin in range(0, model, columns):
        terms = weight * jnp.dot(
            act[...], down_ref[:, begin : begin + columns], preferred_element_type=jnp.float32
        )
        at = 0
        for out in outs:
            out[:, begin : begin + columns] = terms[at : at + out.shape[0]].astype(out.dtype)
            at += out.shape[0]


def run_experts(slot, after, gate, up, down, inputs):
    units, model = gate.shape
    total = sum(block.shape[0] for block in inputs)
    vmem = pl.BlockSpec(memory_space=pltpu.VMEM)
    return pl.pallas_call(
        functools.partial(expert_kernel, len(inputs)),
        in_specs=[pl.BlockSpec(memory_space=pltpu.SMEM), pl.BlockSpec(memory_space=pl.ANY)]
        + [vmem] * (3 + len(inputs)),
        out_specs=[vmem] * len(inputs),
        out_shape=[pltpu.VMEM((block.shape[0], model), jnp.bfloat16) for block in inputs],
        scratch_shapes=[
            pltpu.VMEM((total, model), jnp.bfloat16),
            pltpu.VMEM((total, units), jnp.bfloat16),
        ],
        compiler_params=pltpu.CompilerParams(vmem_limit_bytes=28 * MIB),
        cost_estimate=pl.CostEstimate(
            flops=6 * total * units * model,
            bytes_accessed=6 * units * model + 4 * total * model,
            transcendentals=total * units,
        ),
        name="experts",
    )(slot, after, gate, up, down, *inputs)


def shared_kernel(gate_hbm, up_hbm, down_hbm, after_ref, rows_ref, out_ref, gate, up, down, act, sems):
    del after_ref
    units, model = gate.shape
    lots, columns = lots_of(units), 1024
    copies = []
    for number, (begin, size) in enumerate(lots):
        for kind, (source, target) in enumerate(((gate_hbm, gate), (up_hbm, up))):
            lot = pl.ds(begin, size)
            copies.append(
                pltpu.make_async_copy(source.at[lot], target.at[lot], sems.at[kind, number])
            )
    copies.append(pltpu.make_async_copy(down_hbm, down, sems.at[2, 0]))
    for copy in copies:
        copy.start()
    for number, (begin, size) in enumerate(lots):
        copies[2 * number].wait()
        copies[2 * number + 1].wait()
        lot = pl.ds(begin, size)
        act[:, begin : begin + size] = activate(rows_ref[...], gate[lot, :], up[lot, :])
    copies[-1].wait()
    for begin in range(0, model, columns):
        out_ref[:, begin : begin + columns] = jnp.dot(
            act[...], down[:, begin : begin + columns], preferred_element_type=jnp.float32
        )


def run_shared(after, rows, gate, up, down):
    units, model = gate.shape
    vmem = pl.BlockSpec(memory_space=pltpu.VMEM)
    anywhere = pl.BlockSpec(memory_space=pl.ANY)
    return pl.pallas_call(
        shared_kernel,
        in_specs=[anywhere] * 4 + [vmem],
        out_specs=vmem,
        out_shape=pltpu.VMEM((rows.shape[0], model), jnp.float32),
        scratch_shapes=[
            pltpu.VMEM(gate.shape, jnp.bfloat16),
            pltpu.VMEM(up.shape, jnp.bfloat16),
            pltpu.VMEM(down.shape, jnp.bfloat16),
            pltpu.VMEM((rows.shape[0], units), jnp.bfloat16),
            pltpu.SemaphoreType.DMA((3, len(lots_of(units)))),
        ],
        compiler_params=pltpu.CompilerParams(vmem_limit_bytes=24 * MIB),
        cost_estimate=pl.CostEstimate(
            flops=6 * rows.shape[0] * units * model,
            bytes_accessed=12 * units * model,
            transcendentals=rows.shape[0] * units,
        ),
        name="shared",
    )(*[in_hbm(value) for value in (gate, up, down)], after, rows)


def exchanges(groups, replicas):
    lines, depth = replicas, groups // (2 * replicas)

    def moves(dz=0, dy=0, dc=0, dx=0):
        pairs = []
        for group in range(groups):
            z, y, core = group // (2 * lines), group // 2 % lines, group % 2
            other = ((z + dz) % depth * lines + (y ^ dy)) * 2 + (core ^ dc)
            for rep in range(replicas):
                pairs.append((group * replicas + rep, other * replicas + (rep ^ dx)))
        return pairs

    return lambda value, **by: lax.ppermute(value, AXES, moves(**by))


def route_columns(routes, route_weight, placement):
    experts = placement.shape[0]
    ids = jnp.arange(experts, dtype=jnp.int32)
    slots = jnp.sum(jnp.where(routes[:, :, None] == ids, placement, 0), axis=2)
    table = jnp.sum(jnp.where(slots[:, :, None] == ids, route_weight[:, :, None], 0.0), axis=1)
    half = -(-experts // 64) * 64
    table = jnp.pad(table, ((0, 0), (0, half - experts)))
    high = table.astype(jnp.bfloat16)
    low = (table - high.astype(jnp.float32)).astype(jnp.bfloat16)
    return jnp.concatenate([high, low], axis=1)


def enter(attended, own_rows, routes, route_weight, placement, residual):
    attended = attended.astype(jnp.bfloat16).astype(jnp.float32)
    hidden = (own_rows(residual).astype(jnp.float32) + attended).astype(jnp.bfloat16)
    columns = route_columns(own_rows(routes), own_rows(route_weight), placement)
    return jnp.concatenate([hidden, columns], axis=1), hidden


def exchange_experts(swap, block, hidden, slot, weights, shared):
    own, model = hidden.shape
    directions = (dict(dx=1), dict(dy=1), dict(dx=1, dy=1))
    line = [block] + [swap(block, dz=step) for step in (1, 2, 3)]
    column = jnp.concatenate(line, axis=0)
    column, slot = lax.optimization_barrier((column, slot))
    planes = [swap(column, **by) for by in directions]
    other = swap(column, dc=1)
    weights, token = stage(column, weights)
    planes, other, token = lax.optimization_barrier((planes, other, token))
    first = run_experts(slot, token, *weights, [column, *planes[:2], other])
    others = [swap(plane, dc=1) for plane in planes]
    last = run_experts(slot, token, *weights, [*others[:2], planes[2], others[2]])
    kept = [*first[:3], last[2]]
    crossed = [swap(term, dc=1) for term in (first[3], last[0], last[1], last[3])]
    sums = [
        mine.astype(jnp.float32) + term.astype(jnp.float32) for mine, term in zip(kept, crossed)
    ]
    returned = [
        swap(value.astype(jnp.bfloat16), **by) for value, by in zip(sums[1:], directions)
    ]
    pair = jnp.concatenate([planes[0][:own, :model], hidden], axis=0)
    own_terms = run_shared(last[0], pair, *shared)
    away = swap(own_terms[:own].astype(jnp.bfloat16), dx=1)
    total = sums[0]
    for value in returned:
        total = total + value.astype(jnp.float32)
    mixed = hidden.astype(jnp.float32) + own_terms[own:] + total[:own]
    for step in (1, 2, 3):
        piece = total[step * own : (step + 1) * own].astype(jnp.bfloat16)
        mixed = mixed + swap(piece, dz=-step).astype(jnp.float32)
    return mixed, away.astype(jnp.float32)


def finish(mixed, norm_gain):
    inverse = lax.rsqrt(jnp.mean(mixed * mixed, axis=1, keepdims=True) + EPSILON)
    return (mixed * inverse * norm_gain).astype(jnp.bfloat16)


def per_device(
    residual,
    query_latent,
    query_rope,
    cache_latent,
    cache_rope,
    page_table,
    lengths,
    value_up,
    out_proj,
    routes,
    route_weight,
    placement,
    expert_gate,
    expert_up,
    expert_down,
    shared_gate,
    shared_up,
    shared_down,
    norm_gain,
):
    replicas = lax.axis_size("rep")
    groups = lax.axis_size("ep")
    rep = lax.axis_index("rep")
    slot = lax.axis_index("ep").reshape(1).astype(jnp.int32)
    own = page_table.shape[0]
    heads = value_up.shape[0]
    own_rows = lambda value: lax.dynamic_slice_in_dim(value, rep * own, own, 0)
    caches = (query_latent, query_rope, cache_latent, cache_rope, page_table, lengths)
    gate = expert_gate[0].T
    up = expert_up[0].T
    down = expert_down[0]
    shared = (shared_gate.T, shared_up.T, shared_down)
    routing = (routes, route_weight, placement, residual)

    if replicas == 2 and groups == 16:
        swap = exchanges(groups, replicas)
        away, prepared = attend(1 - rep, heads, *caches)
        arrived = swap(away, dx=1)
        kept, value_up, out_proj = attend_more(
            rep, heads, prepared, query_latent, query_rope, (value_up, out_proj)
        )
        send, keep = project([arrived, kept], [jnp.bfloat16, jnp.float32], value_up, out_proj)
        send, routing = lax.optimization_barrier((send, routing))
        block, hidden = enter(keep + swap(send, dx=1).astype(jnp.float32), own_rows, *routing)
        total, mixed_shared = exchange_experts(
            swap, block, hidden, slot, (gate, up, down), shared
        )
        return finish(total + mixed_shared, norm_gain)

    latents, _ = attend(jnp.int32(0), heads * replicas, *caches)
    latents = lax.all_to_all(latents, "rep", 0, 0, tiled=True)
    latents = latents.reshape(replicas, -1, latents.shape[1])
    terms = project(
        [latents[i] for i in range(replicas)], [jnp.bfloat16] * replicas, value_up, out_proj
    )
    attended = lax.psum_scatter(
        jnp.concatenate(terms, axis=0), "rep", scatter_dimension=0, tiled=True
    )
    block, hidden = enter(attended, own_rows, *routing)
    model = hidden.shape[1]
    every = lax.all_gather(block, AXES, axis=0, tiled=True)
    lot = min(512, every.shape[0])
    terms = [
        run_experts(slot, slot, gate, up, down, [every[at : at + lot]])[0]
        for at in range(0, every.shape[0], lot)
    ]
    mine = lax.dynamic_slice_in_dim(every, slot[0] * replicas * own, replicas * own, 0)[:, :model]
    own_terms = run_shared(mine, mine, *shared).astype(jnp.bfloat16)
    total = lax.psum_scatter(
        jnp.concatenate(terms, axis=0), AXES, scatter_dimension=0, tiled=True
    ).astype(jnp.float32)
    total = total + lax.psum_scatter(
        own_terms, "rep", scatter_dimension=0, tiled=True
    ).astype(jnp.float32)
    return finish(hidden.astype(jnp.float32) + total, norm_gain)


def solution(mesh):
    in_specs = (
        P("ep", None),
        P(("ep", "rep"), None),
        P(("ep", "rep"), None),
        P(("ep", "rep"), None, None),
        P(("ep", "rep"), None),
        P(("ep", "rep"), None),
        P(("ep", "rep")),
        P("rep", None, None),
        P("rep", None),
        P("ep", None),
        P("ep", None),
        P(),
        P("ep", None, "rep"),
        P("ep", None, "rep"),
        P("ep", "rep", None),
        P(None, "rep"),
        P(None, "rep"),
        P("rep", None),
        P(),
    )
    out_specs = P(("ep", "rep"), None)
    return jax.shard_map(
        per_device, mesh=mesh, in_specs=in_specs, out_specs=out_specs, check_vma=False
    )
```

time: 203 us -> 71.4 us (0.35)
  waiting for transfers between devices: 67.7 us -> 25.6 us
  blocking collectives: 42 us -> 0 us
  matrix products: 30 us -> 0 us
  local copies, waits for them, and re-layouts: 30.1 us -> 0.3 us
  Pallas kernels: 0 us -> 19.7 us
  starting transfers between devices: 9.47 us -> 23.8 us
  between operations: 13.6 us -> 0.19 us
  other arithmetic: 9.26 us -> 1.67 us
    all_to_all x1 -> x0, blocking collectives: 42 us -> none  [per_device(): lax.all_to_all(outgoing, 'ep', split_axis=0, concat_axis=0, tiled=True)]
    all_to_all x2 -> x0, waiting for transfers between devices: 31.7 us -> none  [the longest x1 29.2 us: per_device(): lax.all_to_all(outbound, 'ep', split_axis=0, concat_axis=0, tiled=True)]
    dot_general x9 -> x0, matrix products: 30 us -> none  [the longest x1 6.89 us: per_device(): jnp.einsum('secf,efd->secd', activated, expert_down, preferred_element_ty...]
    ppermute x0 -> x23, waiting for transfers between devices: none -> 25.6 us  [exchanges(): return lambda value, **by: lax.ppermute(value, AXES, moves(**by))]
    ppermute x0 -> x23, starting transfers between devices: none -> 23.8 us  [exchanges(): return lambda value, **by: lax.ppermute(value, AXES, moves(**by))]
    psum x1 -> x0, waiting for transfers between devices: 22.1 us -> none  [per_device(): attended = lax.psum(attn_terms.astype(jnp.bfloat16), 'rep')]
    pallas_call x0 -> x7, Pallas kernels: none -> 19.7 us  [the longest x2 5.46 us: run_experts(): pl.pallas_call(functools.partial(expert_kernel, len(inputs)), in_specs=[p...]
    gather x4 -> x0, local copies, waits for them, and re-layouts: 18.1 us -> none  [the longest x1 8.73 us: attend_rows(): cache_latent[page_table].reshape(row_count, key_span, latent_width)]
  transfers between devices with their start and end apart: 4 -> 23, of which waited for: 4 -> 15; matrix products, arithmetic and copies ran while one was open for 3% -> 1% of each run, Pallas kernels for 0% -> 19%
where the time goes in v2:
time: 71.4 us; the launch traced here: 71.2 us
  waiting for transfers between devices  25.6 us (36%)
  starting transfers between devices  23.8 us (33%)
  Pallas kernels  19.7 us (28%)
  other arithmetic  1.67 us (2%)
    ppermute x23, waiting for transfers between devices, exchanges(): return lambda value, **by: lax.ppermute(value, AXES, moves(**by))  25.6 us
    ppermute x23, starting transfers between devices, exchanges(): return lambda value, **by: lax.ppermute(value, AXES, moves(**by))  23.8 us
    pallas_call x2, Pallas kernels, run_experts(): pl.pallas_call(functools.partial(expert_kernel, len(inputs)), in_specs=[p...  5.46 us
    pallas_call x1, Pallas kernels, run_shared(): pl.pallas_call(shared_kernel, in_specs=[anywhere] * 4 + [vmem], out_specs...  4.34 us
    pallas_call x1, Pallas kernels, stage(): pl.pallas_call(functools.partial(stage_kernel, len(values)), in_specs=[an...  3.56 us
    pallas_call x1, Pallas kernels, attend(): pl.pallas_call(attend_kernel, in_specs=[pl.BlockSpec(memory_space=pltpu.S...  2.71 us
    pallas_call x1, Pallas kernels, attend_more(): pl.pallas_call(functools.partial(attend_more_kernel, len(values)), in_spe...  2.63 us
  transfers between devices with their start and end apart: 23, of which 15 were waited for; matrix products, arithmetic and copies ran while one was open for 1% of the time, Pallas kernels for 19%

profile of v2, /device:TPU:0, one launch (start us, length us, event | category | flops | bytes accessed | tf_op | source)
XLA Modules:
  0.0 71.2 jit_solution(11515841612259183704)
XLA Ops:
  0.0 2.7 %attend.1 = (bf16[128,512]{1,0:T(8,128)(2,1)S(1)}, bf16[1024,512]{1,0:T(8,128)(2,1)S(1)}, bf16[1024,128]{1,0:T(8,128)(2,1)S(1)}, f32[16,1024]{1,0:T(8,128)S(1)}) custom-call(s32[1]{0:T(128)} %bitcast.1.block_ref, s32[16]{0:T(128)} %lengths_hbm.1, s32[16,9]{1,0:T(8,128)} %table_hbm.1, bf16[16,8192]{1,0:T(8,128)(2,1)} %query_hbm.3, bf16[16,1024]{1,0:T(8,128)(2,1)} %rot_hbm.3, ...), custom_call_target="tpu_custom_call" | custom-call | flops 268435456 | bytes 4194304 | tf_op jit(solution)/shard_map/attend/pallas_call | solution.py:129
  2.7 3.0 %collective-permute-start = (bf16[128,512]{1,0:T(8,128)(2,1)S(1)}, bf16[128,512]{1,0:T(8,128)(2,1)S(1)}, u32[]{:S(2)}, u32[]{:S(2)}) collective-permute-start(bf16[128,512]{1,0:T(8,128)(2,1)S(1)} %get-tuple-element.43), channel_id=1, source_target_pairs={{0,1},{1,0},{2,3},{3,2},{4,5},{5,4},{6,7},{7,6},{8,9},{9,8},{10,11... | collective-permute-start | bytes 393224 | tf_op jit(solution)/shard_map/ppermute | solution.py:418
  5.7 2.6 %attend_more.1 = (bf16[128,512]{1,0:T(8,128)(2,1)S(1)}, bf16[8,512,128]{2,1,0:T(8,128)(2,1)S(1)}, bf16[1024,2048]{1,0:T(8,128)(2,1)S(1)}) custom-call(s32[1]{0:T(128)} %bitcast.block_ref, bf16[1024,512]{1,0:T(8,128)(2,1)S(1)} %get-tuple-element.38.key_lat, bf16[1024,128]{1,0:T(8,128)(2,1)S(1)} %get-tuple-element.39.key_rot, ...), custom_call_target="tpu_custom_call" | custom-call | flops 268435456 | bytes 8388608 | tf_op jit(solution)/shard_map/attend_more/pallas_call | solution.py:191
  10.2 1.8 %collective-permute-start.1 = (bf16[16,2048]{1,0:T(8,128)(2,1)S(1)}, bf16[16,2048]{1,0:T(8,128)(2,1)S(1)}, u32[]{:S(2)}, u32[]{:S(2)}) collective-permute-start(bf16[16,2048]{1,0:T(8,128)(2,1)S(1)} %get-tuple-element.48), channel_id=1, source_target_pairs={{0,1},{1,0},{2,3},{3,2},{4,5},{5,4},{6,7},{7,6},{8,9},{9,8},{10,11... | collective-permute-start | bytes 196616 | tf_op jit(solution)/shard_map/ppermute | solution.py:418
  12.5 2.0 %collective-permute-done.1 = bf16[16,2048]{1,0:T(8,128)(2,1)S(1)} collective-permute-done((bf16[16,2048]{1,0:T(8,128)(2,1)S(1)}, bf16[16,2048]{1,0:T(8,128)(2,1)S(1)}, u32[]{:S(2)}, u32[]{:S(2)}) %collective-permute-start.1) | collective-permute-done | bytes 65568 | tf_op jit(solution)/shard_map/ppermute | solution.py:418
  14.6 3.9 %collective-permute-start.4 = (bf16[16,2176]{1,0:T(8,128)(2,1)S(1)}, bf16[16,2176]{1,0:T(8,128)(2,1)S(1)}, u32[]{:S(2)}, u32[]{:S(2)}) collective-permute-start(bf16[16,2176]{1,0:T(8,128)(2,1)S(1)} %concatenate.9), channel_id=1, source_target_pairs={{0,24},{1,25},{2,26},{3,27},{4,28},{5,29},{6,30},{7,31},{8,0},{9,1... | collective-permute-start | bytes 208904 | tf_op jit(solution)/shard_map/ppermute | solution.py:418
  18.5 1.0 %collective-permute-start.2 = (bf16[16,2176]{1,0:T(8,128)(2,1)S(1)}, bf16[16,2176]{1,0:T(8,128)(2,1)S(1)}, u32[]{:S(2)}, u32[]{:S(2)}) collective-permute-start(bf16[16,2176]{1,0:T(8,128)(2,1)S(1)} %concatenate.9), channel_id=1, source_target_pairs={{0,8},{1,9},{2,10},{3,11},{4,12},{5,13},{6,14},{7,15},{8,16},{9,17... | collective-permute-start | bytes 208904 | tf_op jit(solution)/shard_map/ppermute | solution.py:418
  20.4 3.3 %collective-permute-done.3 = bf16[16,2176]{1,0:T(8,128)(2,1)S(1)} collective-permute-done((bf16[16,2176]{1,0:T(8,128)(2,1)S(1)}, bf16[16,2176]{1,0:T(8,128)(2,1)S(1)}, u32[]{:S(2)}, u32[]{:S(2)}) %collective-permute-start.3) | collective-permute-done | bytes 69664 | tf_op jit(solution)/shard_map/ppermute | solution.py:418
  24.6 1.6 %collective-permute-start.5 = (bf16[64,2176]{1,0:T(8,128)(2,1)S(1)}, bf16[64,2176]{1,0:T(8,128)(2,1)S(1)}, u32[]{:S(2)}, u32[]{:S(2)}) collective-permute-start(bf16[64,2176]{1,0:T(8,128)(2,1)S(1)} %pad_maximum_fusion.after_ref.refs_0_), channel_id=1, source_target_pairs={{0,1},{1,0},{2,3},{3,2},{4,5},{5,4},{6,7},{7,6},{8,9},{9,8},{10,11... | collective-permute-start | bytes 835592 | tf_op jit(solution)/shard_map/ppermute | solution.py:418
  26.2 1.5 %collective-permute-start.6 = (bf16[64,2176]{1,0:T(8,128)(2,1)S(1)}, bf16[64,2176]{1,0:T(8,128)(2,1)S(1)}, u32[]{:S(2)}, u32[]{:S(2)}) collective-permute-start(bf16[64,2176]{1,0:T(8,128)(2,1)S(1)} %pad_maximum_fusion.after_ref.refs_0_), channel_id=1, source_target_pairs={{0,4},{1,5},{2,6},{3,7},{4,0},{5,1},{6,2},{7,3},{8,12},{9,13},{10,... | collective-permute-start | bytes 835592 | tf_op jit(solution)/shard_map/ppermute | solution.py:418
  28.2 3.6 %stage.1 = (bf16[704,2048]{1,0:T(8,128)(2,1)S(1)}, bf16[704,2048]{1,0:T(8,128)(2,1)S(1)}, bf16[704,2048]{1,0:T(8,128)(2,1)S(1)}, f32[8,128]{1,0:T(8,128)S(1)}) custom-call(bf16[64,2176]{1,0:T(8,128)(2,1)S(1)} %pad_maximum_fusion.after_ref.refs_0_, bf16[704,2048]{1,0:T(8,128)(2,1)} %bitcast.12, bf16[704,2048]{1,0:T(8,128)(2,1)} %bitcast.13, ...), custom_call_target="tpu_custom_call" | custom-call | bytes 17301504 | tf_op jit(solution)/shard_map/stage/pallas_call | solution.py:274
  31.7 1.6 %collective-permute-done.5.refs_1_ = bf16[64,2176]{1,0:T(8,128)(2,1)S(1)} collective-permute-done((bf16[64,2176]{1,0:T(8,128)(2,1)S(1)}, bf16[64,2176]{1,0:T(8,128)(2,1)S(1)}, u32[]{:S(2)}, u32[]{:S(2)}) %collective-permute-start.5) | collective-permute-done | bytes 278560 | tf_op jit(solution)/shard_map/ppermute | solution.py:418
  33.3 4.2 %collective-permute-done.6.refs_2_ = bf16[64,2176]{1,0:T(8,128)(2,1)S(1)} collective-permute-done((bf16[64,2176]{1,0:T(8,128)(2,1)S(1)}, bf16[64,2176]{1,0:T(8,128)(2,1)S(1)}, u32[]{:S(2)}, u32[]{:S(2)}) %collective-permute-start.6) | collective-permute-done | bytes 278560 | tf_op jit(solution)/shard_map/ppermute | solution.py:418
  38.1 1.0 %collective-permute-done.9.refs_0_ = bf16[64,2176]{1,0:T(8,128)(2,1)S(1)} collective-permute-done((bf16[64,2176]{1,0:T(8,128)(2,1)S(1)}, bf16[64,2176]{1,0:T(8,128)(2,1)S(1)}, u32[]{:S(2)}, u32[]{:S(2)}) %collective-permute-start.9) | collective-permute-done | bytes 278560 | tf_op jit(solution)/shard_map/ppermute | solution.py:418
  39.9 2.7 %experts.2 = (bf16[64,2048]{1,0:T(8,128)(2,1)S(1)}, bf16[64,2048]{1,0:T(8,128)(2,1)S(1)}, bf16[64,2048]{1,0:T(8,128)(2,1)S(1)}, bf16[64,2048]{1,0:T(8,128)(2,1)S(1)}) custom-call(s32[1]{0:T(128)} %bitcast.4.slot_ref, f32[8,128]{1,0:T(8,128)S(1)} %get-tuple-element.55.after_ref, bf16[704,2048]{1,0:T(8,128)(2,1)S(1)} %get-tuple-element.56.gate_ref, ...), custom_call_target="tpu_custom_call" | custom-call | flops 2214592512 | bytes 10747904 | tf_op jit(solution)/shard_map/experts/pallas_call | solution.py:334
  42.8 2.7 %experts.3 = (bf16[64,2048]{1,0:T(8,128)(2,1)S(1)}, bf16[64,2048]{1,0:T(8,128)(2,1)S(1)}, bf16[64,2048]{1,0:T(8,128)(2,1)S(1)}, bf16[64,2048]{1,0:T(8,128)(2,1)S(1)}) custom-call(s32[1]{0:T(128)} %bitcast.4.slot_ref, f32[8,128]{1,0:T(8,128)S(1)} %get-tuple-element.55.after_ref, bf16[704,2048]{1,0:T(8,128)(2,1)S(1)} %get-tuple-element.56.gate_ref, ...), custom_call_target="tpu_custom_call" | custom-call | flops 2214592512 | bytes 10747904 | tf_op jit(solution)/shard_map/experts/pallas_call | solution.py:334
  46.6 1.5 %collective-permute-start.18 = (bf16[64,2048]{1,0:T(8,128)(2,1)S(1)}, bf16[64,2048]{1,0:T(8,128)(2,1)S(1)}, u32[]{:S(2)}, u32[]{:S(2)}) collective-permute-start(bf16[64,2048]{1,0:T(8,128)(2,1)S(1)} %add_convert_fusion), channel_id=1, source_target_pairs={{0,5},{1,4},{2,7},{3,6},{4,1},{5,0},{6,3},{7,2},{8,13},{9,12},{10,... | collective-permute-start | bytes 786440 | tf_op jit(solution)/shard_map/ppermute | solution.py:418
  48.2 1.3 %collective-permute-start.16 = (bf16[64,2048]{1,0:T(8,128)(2,1)S(1)}, bf16[64,2048]{1,0:T(8,128)(2,1)S(1)}, u32[]{:S(2)}, u32[]{:S(2)}) collective-permute-start(bf16[64,2048]{1,0:T(8,128)(2,1)S(1)} %add_convert_fusion.1), channel_id=1, source_target_pairs={{0,4},{1,5},{2,6},{3,7},{4,0},{5,1},{6,2},{7,3},{8,12},{9,13},{10,... | collective-permute-start | bytes 786440 | tf_op jit(solution)/shard_map/ppermute | solution.py:418
  50.4 4.3 %shared.1 = f32[32,2048]{1,0:T(8,128)S(1)} custom-call(bf16[704,2048]{1,0:T(8,128)(2,1)} %bitcast.15, bf16[704,2048]{1,0:T(8,128)(2,1)} %bitcast.16, bf16[704,2048]{1,0:T(8,128)(2,1)} %down_hbm.1, bf16[64,2048]{1,0:T(8,128)(2,1)S(1)} %get-tuple-element.62.after_ref, bf16[32,2048]{1,0:T(8,128)(2,1)S(1)} %pad_maximum_fusion.1.rows_ref), custom_call_target="tpu_custom_call" | custom-call | flops 276824064 | bytes 17301504 | tf_op jit(solution)/shard_map/shared/pallas_call | solution.py:384
  54.8 1.3 %collective-permute-start.22 = (bf16[16,2048]{1,0:T(8,128)(2,1)S(1)}, bf16[16,2048]{1,0:T(8,128)(2,1)S(1)}, u32[]{:S(2)}, u32[]{:S(2)}) collective-permute-start(bf16[16,2048]{1,0:T(8,128)(2,1)S(1)} %slice.51), channel_id=1, source_target_pairs={{0,1},{1,0},{2,3},{3,2},{4,5},{5,4},{6,7},{7,6},{8,9},{9,8},{10,11... | collective-permute-start | bytes 196616 | tf_op jit(solution)/shard_map/ppermute | solution.py:418
  56.7 4.8 %collective-permute-done.16 = bf16[64,2048]{1,0:T(8,128)(2,1)S(1)} collective-permute-done((bf16[64,2048]{1,0:T(8,128)(2,1)S(1)}, bf16[64,2048]{1,0:T(8,128)(2,1)S(1)}, u32[]{:S(2)}, u32[]{:S(2)}) %collective-permute-start.16) | collective-permute-done | bytes 262176 | tf_op jit(solution)/shard_map/ppermute | solution.py:418
  63.4 2.9 %collective-permute-start.19 = (bf16[16,2048]{1,0:T(8,128)(2,1)S(1)}, bf16[16,2048]{1,0:T(8,128)(2,1)S(1)}, u32[]{:S(2)}, u32[]{:S(2)}) collective-permute-start(bf16[16,2048]{1,0:T(8,128)(2,1)S(1)} %get-tuple-element.75), channel_id=1, source_target_pairs={{0,24},{1,25},{2,26},{3,27},{4,28},{5,29},{6,30},{7,31},{8,0},{9,1... | collective-permute-start | bytes 196616 | tf_op jit(solution)/shard_map/ppermute | solution.py:418
  66.4 2.6 %collective-permute-done.21 = bf16[16,2048]{1,0:T(8,128)(2,1)S(1)} collective-permute-done((bf16[16,2048]{1,0:T(8,128)(2,1)S(1)}, bf16[16,2048]{1,0:T(8,128)(2,1)S(1)}, u32[]{:S(2)}, u32[]{:S(2)}) %collective-permute-start.21) | collective-permute-done | bytes 65568 | tf_op jit(solution)/shard_map/ppermute | solution.py:418
  69.0 1.3 %collective-permute-done.20 = bf16[16,2048]{1,0:T(8,128)(2,1)S(1)} collective-permute-done((bf16[16,2048]{1,0:T(8,128)(2,1)S(1)}, bf16[16,2048]{1,0:T(8,128)(2,1)S(1)}, u32[]{:S(2)}, u32[]{:S(2)}) %collective-permute-start.20) | collective-permute-done | bytes 65568 | tf_op jit(solution)/shard_map/ppermute | solution.py:418
  (59 shorter events, 11.9 us)
Async XLA Ops:
  2.7 6.5 %collective-permute-start = (bf16[128,512]{1,0:T(8,128)(2,1)S(1)}, bf16[128,512]{1,0:T(8,128)(2,1)S(1)}, u32[]{:S(2)}, u32[]{:S(2)}) collective-permute-start(bf16[128,512]{1,0:T(8,128)(2,1)S(1)} %get-tuple-element.43), channel_id=1, source_target_pairs={{0,1},{1,0},{2,3},{3,2},{4,5},{5,4},{6,7},{7,6},{8,9},{9,8},{10,11... | collective-permute-start | bytes 393224 | tf_op jit(solution)/shard_map/ppermute | solution.py:418
  10.2 4.3 %collective-permute-start.1 = (bf16[16,2048]{1,0:T(8,128)(2,1)S(1)}, bf16[16,2048]{1,0:T(8,128)(2,1)S(1)}, u32[]{:S(2)}, u32[]{:S(2)}) collective-permute-start(bf16[16,2048]{1,0:T(8,128)(2,1)S(1)} %get-tuple-element.48), channel_id=1, source_target_pairs={{0,1},{1,0},{2,3},{3,2},{4,5},{5,4},{6,7},{7,6},{8,9},{9,8},{10,11... | collective-permute-start | bytes 196616 | tf_op jit(solution)/shard_map/ppermute | solution.py:418
  14.6 5.8 %collective-permute-start.4 = (bf16[16,2176]{1,0:T(8,128)(2,1)S(1)}, bf16[16,2176]{1,0:T(8,128)(2,1)S(1)}, u32[]{:S(2)}, u32[]{:S(2)}) collective-permute-start(bf16[16,2176]{1,0:T(8,128)(2,1)S(1)} %concatenate.9), channel_id=1, source_target_pairs={{0,24},{1,25},{2,26},{3,27},{4,28},{5,29},{6,30},{7,31},{8,0},{9,1... | collective-permute-start | bytes 208904 | tf_op jit(solution)/shard_map/ppermute | solution.py:418
  18.5 5.2 %collective-permute-start.3 = (bf16[16,2176]{1,0:T(8,128)(2,1)S(1)}, bf16[16,2176]{1,0:T(8,128)(2,1)S(1)}, u32[]{:S(2)}, u32[]{:S(2)}) collective-permute-start(bf16[16,2176]{1,0:T(8,128)(2,1)S(1)} %concatenate.9), channel_id=1, source_target_pairs={{0,16},{1,17},{2,18},{3,19},{4,20},{5,21},{6,22},{7,23},{8,24},{9,... | collective-permute-start | bytes 208904 | tf_op jit(solution)/shard_map/ppermute | solution.py:418
  18.5 6.1 %collective-permute-start.2 = (bf16[16,2176]{1,0:T(8,128)(2,1)S(1)}, bf16[16,2176]{1,0:T(8,128)(2,1)S(1)}, u32[]{:S(2)}, u32[]{:S(2)}) collective-permute-start(bf16[16,2176]{1,0:T(8,128)(2,1)S(1)} %concatenate.9), channel_id=1, source_target_pairs={{0,8},{1,9},{2,10},{3,11},{4,12},{5,13},{6,14},{7,15},{8,16},{9,17... | collective-permute-start | bytes 208904 | tf_op jit(solution)/shard_map/ppermute | solution.py:418
  24.6 8.7 %collective-permute-start.5 = (bf16[64,2176]{1,0:T(8,128)(2,1)S(1)}, bf16[64,2176]{1,0:T(8,128)(2,1)S(1)}, u32[]{:S(2)}, u32[]{:S(2)}) collective-permute-start(bf16[64,2176]{1,0:T(8,128)(2,1)S(1)} %pad_maximum_fusion.after_ref.refs_0_), channel_id=1, source_target_pairs={{0,1},{1,0},{2,3},{3,2},{4,5},{5,4},{6,7},{7,6},{8,9},{9,8},{10,11... | collective-permute-start | bytes 835592 | tf_op jit(solution)/shard_map/ppermute | solution.py:418
  26.2 11.3 %collective-permute-start.6 = (bf16[64,2176]{1,0:T(8,128)(2,1)S(1)}, bf16[64,2176]{1,0:T(8,128)(2,1)S(1)}, u32[]{:S(2)}, u32[]{:S(2)}) collective-permute-start(bf16[64,2176]{1,0:T(8,128)(2,1)S(1)} %pad_maximum_fusion.after_ref.refs_0_), channel_id=1, source_target_pairs={{0,4},{1,5},{2,6},{3,7},{4,0},{5,1},{6,2},{7,3},{8,12},{9,13},{10,... | collective-permute-start | bytes 835592 | tf_op jit(solution)/shard_map/ppermute | solution.py:418
  27.7 9.8 %collective-permute-start.7 = (bf16[64,2176]{1,0:T(8,128)(2,1)S(1)}, bf16[64,2176]{1,0:T(8,128)(2,1)S(1)}, u32[]{:S(2)}, u32[]{:S(2)}) collective-permute-start(bf16[64,2176]{1,0:T(8,128)(2,1)S(1)} %pad_maximum_fusion.after_ref.refs_0_), channel_id=1, source_target_pairs={{0,5},{1,4},{2,7},{3,6},{4,1},{5,0},{6,3},{7,2},{8,13},{9,12},{10,... | collective-permute-start | bytes 835592 | tf_op jit(solution)/shard_map/ppermute | solution.py:418
  28.2 9.4 %collective-permute-start.8 = (bf16[64,2176]{1,0:T(8,128)(2,1)S(1)}, bf16[64,2176]{1,0:T(8,128)(2,1)S(1)}, u32[]{:S(2)}, u32[]{:S(2)}) collective-permute-start(bf16[64,2176]{1,0:T(8,128)(2,1)S(1)} %pad_maximum_fusion.after_ref.refs_0_), channel_id=1, source_target_pairs={{0,2},{1,3},{2,0},{3,1},{4,6},{5,7},{6,4},{7,5},{8,10},{9,11},{10,... | collective-permute-start | bytes 835592 | tf_op jit(solution)/shard_map/ppermute | solution.py:418
  37.5 1.6 %collective-permute-start.9 = (bf16[64,2176]{1,0:T(8,128)(2,1)S(1)}, bf16[64,2176]{1,0:T(8,128)(2,1)S(1)}, u32[]{:S(2)}, u32[]{:S(2)}) collective-permute-start(bf16[64,2176]{1,0:T(8,128)(2,1)S(1)} %collective-permute-done.5.refs_1_), channel_id=1, source_target_pairs={{0,2},{1,3},{2,0},{3,1},{4,6},{5,7},{6,4},{7,5},{8,10},{9,11},{10,... | collective-permute-start | bytes 835592 | tf_op jit(solution)/shard_map/ppermute | solution.py:418
  37.5 1.9 %collective-permute-start.10 = (bf16[64,2176]{1,0:T(8,128)(2,1)S(1)}, bf16[64,2176]{1,0:T(8,128)(2,1)S(1)}, u32[]{:S(2)}, u32[]{:S(2)}) collective-permute-start(bf16[64,2176]{1,0:T(8,128)(2,1)S(1)} %collective-permute-done.6.refs_2_), channel_id=1, source_target_pairs={{0,2},{1,3},{2,0},{3,1},{4,6},{5,7},{6,4},{7,5},{8,10},{9,11},{10,... | collective-permute-start | bytes 835592 | tf_op jit(solution)/shard_map/ppermute | solution.py:418
  38.0 1.8 %collective-permute-start.11 = (bf16[64,2176]{1,0:T(8,128)(2,1)S(1)}, bf16[64,2176]{1,0:T(8,128)(2,1)S(1)}, u32[]{:S(2)}, u32[]{:S(2)}) collective-permute-start(bf16[64,2176]{1,0:T(8,128)(2,1)S(1)} %collective-permute-done.7.refs_2_), channel_id=1, source_target_pairs={{0,2},{1,3},{2,0},{3,1},{4,6},{5,7},{6,4},{7,5},{8,10},{9,11},{10,... | collective-permute-start | bytes 835592 | tf_op jit(solution)/shard_map/ppermute | solution.py:418
  42.6 3.9 %collective-permute-start.17 = (bf16[64,2048]{1,0:T(8,128)(2,1)S(1)}, bf16[64,2048]{1,0:T(8,128)(2,1)S(1)}, u32[]{:S(2)}, u32[]{:S(2)}) collective-permute-start(bf16[64,2048]{1,0:T(8,128)(2,1)S(1)} %get-tuple-element.70), channel_id=1, source_target_pairs={{0,2},{1,3},{2,0},{3,1},{4,6},{5,7},{6,4},{7,5},{8,10},{9,11},{10,... | collective-permute-start | bytes 786440 | tf_op jit(solution)/shard_map/ppermute | solution.py:418
  45.5 10.5 %collective-permute-start.12 = (bf16[64,2048]{1,0:T(8,128)(2,1)S(1)}, bf16[64,2048]{1,0:T(8,128)(2,1)S(1)}, u32[]{:S(2)}, u32[]{:S(2)}) collective-permute-start(bf16[64,2048]{1,0:T(8,128)(2,1)S(1)} %get-tuple-element.65), channel_id=1, source_target_pairs={{0,2},{1,3},{2,0},{3,1},{4,6},{5,7},{6,4},{7,5},{8,10},{9,11},{10,... | collective-permute-start | bytes 786440 | tf_op jit(solution)/shard_map/ppermute | solution.py:418
  46.0 2.1 %collective-permute-start.15 = (bf16[64,2048]{1,0:T(8,128)(2,1)S(1)}, bf16[64,2048]{1,0:T(8,128)(2,1)S(1)}, u32[]{:S(2)}, u32[]{:S(2)}) collective-permute-start(bf16[64,2048]{1,0:T(8,128)(2,1)S(1)} %get-tuple-element.68), channel_id=1, source_target_pairs={{0,2},{1,3},{2,0},{3,1},{4,6},{5,7},{6,4},{7,5},{8,10},{9,11},{10,... | collective-permute-start | bytes 786440 | tf_op jit(solution)/shard_map/ppermute | solution.py:418
  46.1 3.3 %collective-permute-start.13 = (bf16[64,2048]{1,0:T(8,128)(2,1)S(1)}, bf16[64,2048]{1,0:T(8,128)(2,1)S(1)}, u32[]{:S(2)}, u32[]{:S(2)}) collective-permute-start(bf16[64,2048]{1,0:T(8,128)(2,1)S(1)} %get-tuple-element.62.after_ref), channel_id=1, source_target_pairs={{0,2},{1,3},{2,0},{3,1},{4,6},{5,7},{6,4},{7,5},{8,10},{9,11},{10,... | collective-permute-start | bytes 786440 | tf_op jit(solution)/shard_map/ppermute | solution.py:418
  46.6 10.2 %collective-permute-start.18 = (bf16[64,2048]{1,0:T(8,128)(2,1)S(1)}, bf16[64,2048]{1,0:T(8,128)(2,1)S(1)}, u32[]{:S(2)}, u32[]{:S(2)}) collective-permute-start(bf16[64,2048]{1,0:T(8,128)(2,1)S(1)} %add_convert_fusion), channel_id=1, source_target_pairs={{0,5},{1,4},{2,7},{3,6},{4,1},{5,0},{6,3},{7,2},{8,13},{9,12},{10,... | collective-permute-start | bytes 786440 | tf_op jit(solution)/shard_map/ppermute | solution.py:418
  48.2 13.3 %collective-permute-start.16 = (bf16[64,2048]{1,0:T(8,128)(2,1)S(1)}, bf16[64,2048]{1,0:T(8,128)(2,1)S(1)}, u32[]{:S(2)}, u32[]{:S(2)}) collective-permute-start(bf16[64,2048]{1,0:T(8,128)(2,1)S(1)} %add_convert_fusion.1), channel_id=1, source_target_pairs={{0,4},{1,5},{2,6},{3,7},{4,0},{5,1},{6,2},{7,3},{8,12},{9,13},{10,... | collective-permute-start | bytes 786440 | tf_op jit(solution)/shard_map/ppermute | solution.py:418
  49.5 12.8 %collective-permute-start.14 = (bf16[64,2048]{1,0:T(8,128)(2,1)S(1)}, bf16[64,2048]{1,0:T(8,128)(2,1)S(1)}, u32[]{:S(2)}, u32[]{:S(2)}) collective-permute-start(bf16[64,2048]{1,0:T(8,128)(2,1)S(1)} %add_convert_fusion.2), channel_id=1, source_target_pairs={{0,1},{1,0},{2,3},{3,2},{4,5},{5,4},{6,7},{7,6},{8,9},{9,8},{10,11... | collective-permute-start | bytes 786440 | tf_op jit(solution)/shard_map/ppermute | solution.py:418
  54.8 15.7 %copy-start.2 = (f32[2048]{0:T(1024)S(1)}, f32[2048]{0:T(1024)}, u32[]{:S(2)}) copy-start(f32[2048]{0:T(1024)} %param.37) | copy-start | bytes 24580
  54.8 11.6 %collective-permute-start.22 = (bf16[16,2048]{1,0:T(8,128)(2,1)S(1)}, bf16[16,2048]{1,0:T(8,128)(2,1)S(1)}, u32[]{:S(2)}, u32[]{:S(2)}) collective-permute-start(bf16[16,2048]{1,0:T(8,128)(2,1)S(1)} %slice.51), channel_id=1, source_target_pairs={{0,1},{1,0},{2,3},{3,2},{4,5},{5,4},{6,7},{7,6},{8,9},{9,8},{10,11... | collective-permute-start | bytes 196616 | tf_op jit(solution)/shard_map/ppermute | solution.py:418
  62.5 6.5 %collective-permute-start.21 = (bf16[16,2048]{1,0:T(8,128)(2,1)S(1)}, bf16[16,2048]{1,0:T(8,128)(2,1)S(1)}, u32[]{:S(2)}, u32[]{:S(2)}) collective-permute-start(bf16[16,2048]{1,0:T(8,128)(2,1)S(1)} %get-tuple-element.76), channel_id=1, source_target_pairs={{0,8},{1,9},{2,10},{3,11},{4,12},{5,13},{6,14},{7,15},{8,16},{9,17... | collective-permute-start | bytes 196616 | tf_op jit(solution)/shard_map/ppermute | solution.py:418
  62.5 7.8 %collective-permute-start.20 = (bf16[16,2048]{1,0:T(8,128)(2,1)S(1)}, bf16[16,2048]{1,0:T(8,128)(2,1)S(1)}, u32[]{:S(2)}, u32[]{:S(2)}) collective-permute-start(bf16[16,2048]{1,0:T(8,128)(2,1)S(1)} %get-tuple-element.77), channel_id=1, source_target_pairs={{0,16},{1,17},{2,18},{3,19},{4,20},{5,21},{6,22},{7,23},{8,24},{9,... | collective-permute-start | bytes 196616 | tf_op jit(solution)/shard_map/ppermute | solution.py:418
  63.4 6.9 %collective-permute-start.19 = (bf16[16,2048]{1,0:T(8,128)(2,1)S(1)}, bf16[16,2048]{1,0:T(8,128)(2,1)S(1)}, u32[]{:S(2)}, u32[]{:S(2)}) collective-permute-start(bf16[16,2048]{1,0:T(8,128)(2,1)S(1)} %get-tuple-element.75), channel_id=1, source_target_pairs={{0,24},{1,25},{2,26},{3,27},{4,28},{5,29},{6,30},{7,31},{8,0},{9,1... | collective-permute-start | bytes 196616 | tf_op jit(solution)/shard_map/ppermute | solution.py:418
  (4 other events, 25.4 us)

commit v3 on v2

--- a/solution.py
+++ b/solution.py
@@ -213,8 +213,8 @@
     )
 
 
-def project_kernel(parts, value_ref, proj_ref, *refs):
-    latents, out_refs = refs[:parts], refs[parts : 2 * parts]
+def project_kernel(value_ref, proj_ref, *refs):
+    latents, out_ref = refs[:-1], refs[-1]
     heads, latent, width = value_ref.shape
     rows = latents[0].shape[0] // heads
     outs = []
@@ -228,23 +228,21 @@
     head_out = jnp.concatenate(outs, axis=1)
     chunk = 512
     for begin in range(0, proj_ref.shape[1], chunk):
-        terms = jnp.dot(
+        out_ref[:, begin : begin + chunk] = jnp.dot(
             head_out, proj_ref[:, begin : begin + chunk], preferred_element_type=jnp.float32
-        )
-        for part, out in enumerate(out_refs):
-            out[:, begin : begin + chunk] = terms[part * rows : (part + 1) * rows].astype(out.dtype)
-
-
-def project(latents, out_types, value_up, out_proj):
+        ).astype(out_ref.dtype)
+
+
+def project(latents, value_up, out_proj):
     heads, latent, width = value_up.shape
     rows = latents[0].shape[0] // heads
     model = out_proj.shape[1]
     vmem = pl.BlockSpec(memory_space=pltpu.VMEM)
     return pl.pallas_call(
-        functools.partial(project_kernel, len(latents)),
+        project_kernel,
         in_specs=[vmem] * (2 + len(latents)),
-        out_specs=[vmem] * len(latents),
-        out_shape=[pltpu.VMEM((rows, model), kind) for kind in out_types],
+        out_specs=vmem,
+        out_shape=pltpu.VMEM((len(latents) * rows, model), jnp.bfloat16),
         compiler_params=pltpu.CompilerParams(vmem_limit_bytes=16 * MIB),
         cost_estimate=pl.CostEstimate(
             flops=2 * len(latents) * rows * out_proj.size,
@@ -301,7 +299,7 @@
 
 def expert_kernel(blocks, slot_ref, after_ref, gate_ref, up_ref, down_ref, *refs):
     del after_ref
-    inputs, outs, (rows, act) = refs[:blocks], refs[blocks : 2 * blocks], refs[2 * blocks :]
+    inputs, outs, (rows, act) = refs[:blocks], refs[blocks:-2], refs[-2:]
     units, model = gate_ref.shape
     columns = 512
     slot = slot_ref[0]
@@ -327,7 +325,7 @@
             at += out.shape[0]
 
 
-def run_experts(slot, after, gate, up, down, inputs):
+def run_experts(slot, after, gate, up, down, inputs, sizes):
     units, model = gate.shape
     total = sum(block.shape[0] for block in inputs)
     vmem = pl.BlockSpec(memory_space=pltpu.VMEM)
@@ -335,24 +333,67 @@
         functools.partial(expert_kernel, len(inputs)),
         in_specs=[pl.BlockSpec(memory_space=pltpu.SMEM), pl.BlockSpec(memory_space=pl.ANY)]
         + [vmem] * (3 + len(inputs)),
-        out_specs=[vmem] * len(inputs),
-        out_shape=[pltpu.VMEM((block.shape[0], model), jnp.bfloat16) for block in inputs],
+        out_specs=[vmem] * len(sizes),
+        out_shape=[pltpu.VMEM((size, model), jnp.bfloat16) for size in sizes],
         scratch_shapes=[
             pltpu.VMEM((total, model), jnp.bfloat16),
             pltpu.VMEM((total, units), jnp.bfloat16),
         ],
         compiler_params=pltpu.CompilerParams(vmem_limit_bytes=28 * MIB),
-        cost_estimate=pl.CostEstimate(
-            flops=6 * total * units * model,
-            bytes_accessed=6 * units * model + 4 * total * model,
-            transcendentals=total * units,
-        ),
+        cost_estimate=pl.CostEstimate(flops=1, bytes_accessed=1, transcendentals=0),
         name="experts",
     )(slot, after, gate, up, down, *inputs)
 
 
-def shared_kernel(gate_hbm, up_hbm, down_hbm, after_ref, rows_ref, out_ref, gate, up, down, act, sems):
+def all_in_vmem(kernel, name, inputs, shapes):
+    vmem = pl.BlockSpec(memory_space=pltpu.VMEM)
+    return pl.pallas_call(
+        kernel,
+        in_specs=[vmem] * len(inputs),
+        out_specs=[vmem] * len(shapes),
+        out_shape=[pltpu.VMEM(shape, kind) for shape, kind in shapes],
+        compiler_params=pltpu.CompilerParams(vmem_limit_bytes=8 * MIB),
+        name=name,
+    )(*inputs)
+
+
+def add_kernel(crossed_ref, *refs):
+    at = 0
+    for mine, out in zip(refs[: len(refs) // 2], refs[len(refs) // 2 :]):
+        other = crossed_ref[at : at + mine.shape[0], :]
+        out[...] = (mine[...].astype(jnp.float32) + other.astype(jnp.float32)).astype(out.dtype)
+        at += mine.shape[0]
+
+
+def settle_kernel(mine_ref, crossed_ref, near, line, distant):
+    total = mine_ref[...].astype(jnp.float32) + crossed_ref[...].astype(jnp.float32)
+    rows = near.shape[0]
+    near[...] = total[:rows]
+    line[...] = total[rows : 2 * rows].astype(line.dtype)
+    distant[...] = total[2 * rows :]
+
+
+def merge_near_kernel(near_ref, line_ref, pair_ref, away_terms, own_terms, away, mixed):
+    own = mixed.shape[0]
+    total = near_ref[...] + line_ref[...].astype(jnp.float32)
+    away[...] = (total[:own] + away_terms[...]).astype(away.dtype)
+    mixed[...] = total[own:] + own_terms[...] + pair_ref[own:, :].astype(jnp.float32)
+
+
+def merge_far_kernel(distant_ref, *refs):
+    arrived, outs = refs[:3], refs[3:]
+    total = distant_ref[...]
+    for ref in arrived:
+        total = total + ref[...].astype(jnp.float32)
+    own = outs[0].shape[0]
+    for number, out in enumerate(outs):
+        out[...] = total[number * own : (number + 1) * own].astype(out.dtype)
+
+
+def shared_kernel(gate_hbm, up_hbm, down_hbm, after_ref, rows_ref, *refs):
     del after_ref
+    outs, (gate, up, down, act, sems) = refs[:-5], refs[-5:]
+    rows = outs[0].shape[0]
     units, model = gate.shape
     lots, columns = lots_of(units), 1024
     copies = []
@@ -372,20 +413,22 @@
         act[:, begin : begin + size] = activate(rows_ref[...], gate[lot, :], up[lot, :])
     copies[-1].wait()
     for begin in range(0, model, columns):
-        out_ref[:, begin : begin + columns] = jnp.dot(
+        terms = jnp.dot(
             act[...], down[:, begin : begin + columns], preferred_element_type=jnp.float32
         )
-
-
-def run_shared(after, rows, gate, up, down):
+        for number, out in enumerate(outs):
+            out[:, begin : begin + columns] = terms[number * rows : (number + 1) * rows]
+
+
+def run_shared(after, rows, parts, gate, up, down):
     units, model = gate.shape
     vmem = pl.BlockSpec(memory_space=pltpu.VMEM)
     anywhere = pl.BlockSpec(memory_space=pl.ANY)
     return pl.pallas_call(
         shared_kernel,
         in_specs=[anywhere] * 4 + [vmem],
-        out_specs=vmem,
-        out_shape=pltpu.VMEM((rows.shape[0], model), jnp.float32),
+        out_specs=[vmem] * parts,
+        out_shape=[pltpu.VMEM((rows.shape[0] // parts, model), jnp.float32)] * parts,
         scratch_shapes=[
             pltpu.VMEM(gate.shape, jnp.bfloat16),
             pltpu.VMEM(up.shape, jnp.bfloat16),
@@ -430,50 +473,82 @@
     return jnp.concatenate([high, low], axis=1)
 
 
-def enter(attended, own_rows, routes, route_weight, placement, residual):
+def enter(attended, residual):
     attended = attended.astype(jnp.bfloat16).astype(jnp.float32)
-    hidden = (own_rows(residual).astype(jnp.float32) + attended).astype(jnp.bfloat16)
-    columns = route_columns(own_rows(routes), own_rows(route_weight), placement)
-    return jnp.concatenate([hidden, columns], axis=1), hidden
-
-
-def exchange_experts(swap, block, hidden, slot, weights, shared):
-    own, model = hidden.shape
+    return (residual.astype(jnp.float32) + attended).astype(jnp.bfloat16)
+
+
+def exchange_experts(swap, pair, columns, slot, weights, shared):
+    own, model = pair.shape[0] // 2, pair.shape[1]
     directions = (dict(dx=1), dict(dy=1), dict(dx=1, dy=1))
-    line = [block] + [swap(block, dz=step) for step in (1, 2, 3)]
-    column = jnp.concatenate(line, axis=0)
-    column, slot = lax.optimization_barrier((column, slot))
-    planes = [swap(column, **by) for by in directions]
-    other = swap(column, dc=1)
-    weights, token = stage(column, weights)
-    planes, other, token = lax.optimization_barrier((planes, other, token))
-    first = run_experts(slot, token, *weights, [column, *planes[:2], other])
+    rows = jnp.concatenate([pair, columns], axis=1)
+    line = [swap(rows[own:], dz=step) for step in (3, 2, 1)][::-1]
+    across = swap(rows, dy=1)
+    distant = jnp.concatenate(line, axis=0)
+    distant, slot = lax.optimization_barrier((distant, slot))
+    planes = [swap(distant, **by) for by in directions]
+    early = [rows, across, distant]
+    depth, width = sum(value.shape[0] for value in early), distant.shape[0]
+    weights, token = stage(distant, weights)
+    early += [swap(value, dc=1) for value in early]
+    first = list(run_experts(slot, token, *weights, early, [depth, depth]))
+    *planes, first[0], first[1] = lax.optimization_barrier((*planes, first[0], first[1]))
     others = [swap(plane, dc=1) for plane in planes]
-    last = run_experts(slot, token, *weights, [*others[:2], planes[2], others[2]])
-    kept = [*first[:3], last[2]]
-    crossed = [swap(term, dc=1) for term in (first[3], last[0], last[1], last[3])]
-    sums = [
-        mine.astype(jnp.float32) + term.astype(jnp.float32) for mine, term in zip(kept, crossed)
-    ]
-    returned = [
-        swap(value.astype(jnp.bfloat16), **by) for value, by in zip(sums[1:], directions)
-    ]
-    pair = jnp.concatenate([planes[0][:own, :model], hidden], axis=0)
-    own_terms = run_shared(last[0], pair, *shared)
-    away = swap(own_terms[:own].astype(jnp.bfloat16), dx=1)
-    total = sums[0]
-    for value in returned:
-        total = total + value.astype(jnp.float32)
-    mixed = hidden.astype(jnp.float32) + own_terms[own:] + total[:own]
-    for step in (1, 2, 3):
-        piece = total[step * own : (step + 1) * own].astype(jnp.bfloat16)
-        mixed = mixed + swap(piece, dz=-step).astype(jnp.float32)
-    return mixed, away.astype(jnp.float32)
-
-
-def finish(mixed, norm_gain):
+    last = run_experts(slot, token, *weights, [*planes, *others], [width] * 3 + [3 * width])
+    near, back, distant_sum = all_in_vmem(
+        settle_kernel,
+        "settle",
+        [first[0], swap(first[1], dc=1)],
+        [
+            ((2 * own, model), jnp.float32),
+            ((2 * own, model), jnp.bfloat16),
+            ((width, model), jnp.float32),
+        ],
+    )
+    crossed, back = lax.optimization_barrier((last[3], swap(back, dy=1)))
+    sums = all_in_vmem(
+        add_kernel,
+        "add",
+        [swap(crossed, dc=1), *last[:3]],
+        [((width, model), jnp.bfloat16)] * 3,
+    )
+    returned = [swap(value, **by) for value, by in zip(sums, directions)]
+    away_terms, own_terms = run_shared(sums[0], pair, 2, *shared)
+    away, mixed = all_in_vmem(
+        merge_near_kernel,
+        "merge_near",
+        [near, back, pair, away_terms, own_terms],
+        [((own, model), jnp.bfloat16), ((own, model), jnp.float32)],
+    )
+    pieces = all_in_vmem(
+        merge_far_kernel,
+        "merge_far",
+        [distant_sum, *returned],
+        [((own, model), jnp.bfloat16)] * 3,
+    )
+    pieces = [swap(piece, dz=-step) for step, piece in zip((1, 2, 3), pieces)]
+    return mixed, [*pieces, swap(away, dx=1)]
+
+
+def finish_kernel(mixed_ref, gain_ref, *refs):
+    pieces, out = refs[:-1], refs[-1]
+    mixed = mixed_ref[...]
+    for piece in pieces:
+        mixed = mixed + piece[...].astype(jnp.float32)
     inverse = lax.rsqrt(jnp.mean(mixed * mixed, axis=1, keepdims=True) + EPSILON)
-    return (mixed * inverse * norm_gain).astype(jnp.bfloat16)
+    out[...] = (mixed * inverse * gain_ref[...]).astype(out.dtype)
+
+
+def finish(mixed, norm_gain, pieces=()):
+    vmem = pl.BlockSpec(memory_space=pltpu.VMEM)
+    return pl.pallas_call(
+        finish_kernel,
+        in_specs=[vmem] * (2 + len(pieces)),
+        out_specs=vmem,
+        out_shape=jax.ShapeDtypeStruct(mixed.shape, jnp.bfloat16),
+        compiler_params=pltpu.CompilerParams(vmem_limit_bytes=8 * MIB),
+        name="finish",
+    )(mixed, norm_gain.reshape(1, -1), *pieces)
 
 
 def per_device(
@@ -509,42 +584,44 @@
     up = expert_up[0].T
     down = expert_down[0]
     shared = (shared_gate.T, shared_up.T, shared_down)
-    routing = (routes, route_weight, placement, residual)
-
     if replicas == 2 and groups == 16:
         swap = exchanges(groups, replicas)
+        own_last = lambda value: lax.dynamic_slice_in_dim(
+            jnp.concatenate([value, value], axis=0), (1 - rep) * own, 2 * own, 0
+        )
         away, prepared = attend(1 - rep, heads, *caches)
         arrived = swap(away, dx=1)
         kept, value_up, out_proj = attend_more(
             rep, heads, prepared, query_latent, query_rope, (value_up, out_proj)
         )
-        send, keep = project([arrived, kept], [jnp.bfloat16, jnp.float32], value_up, out_proj)
-        send, routing = lax.optimization_barrier((send, routing))
-        block, hidden = enter(keep + swap(send, dx=1).astype(jnp.float32), own_rows, *routing)
-        total, mixed_shared = exchange_experts(
-            swap, block, hidden, slot, (gate, up, down), shared
-        )
-        return finish(total + mixed_shared, norm_gain)
+        terms = project([arrived, kept], value_up, out_proj)
+        terms, routing = lax.optimization_barrier((terms, (routes, route_weight, residual)))
+        routes, route_weight, residual = routing
+        back = swap(terms, dx=1)
+        columns = own_last(route_columns(routes, route_weight, placement))
+        residual = own_last(residual)
+        back = jnp.concatenate([back[own:], back[:own]], axis=0)
+        pair = enter(terms.astype(jnp.float32) + back.astype(jnp.float32), residual)
+        mixed, pieces = exchange_experts(swap, pair, columns, slot, (gate, up, down), shared)
+        return finish(mixed, norm_gain, pieces)
 
     latents, _ = attend(jnp.int32(0), heads * replicas, *caches)
     latents = lax.all_to_all(latents, "rep", 0, 0, tiled=True)
     latents = latents.reshape(replicas, -1, latents.shape[1])
-    terms = project(
-        [latents[i] for i in range(replicas)], [jnp.bfloat16] * replicas, value_up, out_proj
-    )
-    attended = lax.psum_scatter(
-        jnp.concatenate(terms, axis=0), "rep", scatter_dimension=0, tiled=True
-    )
-    block, hidden = enter(attended, own_rows, *routing)
+    terms = project([latents[i] for i in range(replicas)], value_up, out_proj)
+    attended = lax.psum_scatter(terms, "rep", scatter_dimension=0, tiled=True)
+    hidden = enter(attended, own_rows(residual))
     model = hidden.shape[1]
+    columns = route_columns(own_rows(routes), own_rows(route_weight), placement)
+    block = jnp.concatenate([hidden, columns], axis=1)
     every = lax.all_gather(block, AXES, axis=0, tiled=True)
     lot = min(512, every.shape[0])
     terms = [
-        run_experts(slot, slot, gate, up, down, [every[at : at + lot]])[0]
+        run_experts(slot, slot, gate, up, down, [every[at : at + lot]], [lot])[0]
         for at in range(0, every.shape[0], lot)
     ]
     mine = lax.dynamic_slice_in_dim(every, slot[0] * replicas * own, replicas * own, 0)[:, :model]
-    own_terms = run_shared(mine, mine, *shared).astype(jnp.bfloat16)
+    own_terms = run_shared(mine, mine, 1, *shared)[0].astype(jnp.bfloat16)
     total = lax.psum_scatter(
         jnp.concatenate(terms, axis=0), AXES, scatter_dimension=0, tiled=True
     ).astype(jnp.float32)

time: 71.4 us -> 70 us (0.980)
  waiting for transfers between devices: 25.6 us -> 22.5 us
  starting transfers between devices: 23.8 us -> 25.6 us
  Pallas kernels: 19.7 us -> 21.1 us
  other arithmetic: 1.67 us -> 0.35 us
    ppermute x23 -> x25, waiting for transfers between devices: 25.6 us -> 22.5 us  [exchanges(): return lambda value, **by: lax.ppermute(value, AXES, moves(**by))]
    ppermute x23 -> x25, starting transfers between devices: 23.8 us -> 25.6 us  [exchanges(): return lambda value, **by: lax.ppermute(value, AXES, moves(**by))]
    pallas_call x1 -> x6, Pallas kernels: 0.97 us -> 2.15 us  [the longest x1 0.98 us: project(): pl.pallas_call(project_kernel, in_specs=[vmem] * (2 + len(latents)), out_...]
    convert_element_type x5 -> x1, other arithmetic: 0.94 us -> 0.09 us  [enter(): return (residual.astype(jnp.float32) + attended).astype(jnp.bfloat16)]
  transfers between devices with their start and end apart: 23 -> 25, of which waited for: 15 -> 12; matrix products, arithmetic and copies ran while one was open for 1% -> 0% of each run, Pallas kernels for 19% -> 24%
where the time goes in v3:
time: 70 us; the launch traced here: 69.8 us
  starting transfers between devices  25.6 us (37%)
  waiting for transfers between devices  22.5 us (32%)
  Pallas kernels  21.1 us (30%)
    ppermute x25, starting transfers between devices, exchanges(): return lambda value, **by: lax.ppermute(value, AXES, moves(**by))  25.6 us
    ppermute x25, waiting for transfers between devices, exchanges(): return lambda value, **by: lax.ppermute(value, AXES, moves(**by))  22.5 us
    pallas_call x2, Pallas kernels, run_experts(): pl.pallas_call(functools.partial(expert_kernel, len(inputs)), in_specs=[p...  5.73 us
    pallas_call x1, Pallas kernels, run_shared(): pl.pallas_call(shared_kernel, in_specs=[anywhere] * 4 + [vmem], out_specs...  4.36 us
    pallas_call x1, Pallas kernels, stage(): pl.pallas_call(functools.partial(stage_kernel, len(values)), in_specs=[an...  3.56 us
    pallas_call x1, Pallas kernels, attend(): pl.pallas_call(attend_kernel, in_specs=[pl.BlockSpec(memory_space=pltpu.S...  2.7 us
    pallas_call x1, Pallas kernels, attend_more(): pl.pallas_call(functools.partial(attend_more_kernel, len(values)), in_spe...  2.63 us
  transfers between devices with their start and end apart: 25, of which 12 were waited for; matrix products, arithmetic and copies ran while one was open for 0% of the time, Pallas kernels for 24%

profile of v3, /device:TPU:0, one launch (start us, length us, event | category | flops | bytes accessed | tf_op | source)
XLA Modules:
  0.0 69.8 jit_solution(2519908784760764854)
XLA Ops:
  0.0 2.7 %attend.1 = (bf16[128,512]{1,0:T(8,128)(2,1)S(1)}, bf16[1024,512]{1,0:T(8,128)(2,1)S(1)}, bf16[1024,128]{1,0:T(8,128)(2,1)S(1)}, f32[16,1024]{1,0:T(8,128)S(1)}) custom-call(s32[1]{0:T(128)} %bitcast.1.block_ref, s32[16]{0:T(128)} %lengths_hbm.1, s32[16,9]{1,0:T(8,128)} %table_hbm.1, bf16[16,8192]{1,0:T(8,128)(2,1)} %query_hbm.3, bf16[16,1024]{1,0:T(8,128)(2,1)} %rot_hbm.3, ...), custom_call_target="tpu_custom_call" | custom-call | flops 268435456 | bytes 4194304 | tf_op jit(solution)/shard_map/attend/pallas_call | solution.py:129
  2.7 3.0 %collective-permute-start = (bf16[128,512]{1,0:T(8,128)(2,1)S(1)}, bf16[128,512]{1,0:T(8,128)(2,1)S(1)}, u32[]{:S(2)}, u32[]{:S(2)}) collective-permute-start(bf16[128,512]{1,0:T(8,128)(2,1)S(1)} %get-tuple-element.53), channel_id=1, source_target_pairs={{0,1},{1,0},{2,3},{3,2},{4,5},{5,4},{6,7},{7,6},{8,9},{9,8},{10,11... | collective-permute-start | bytes 393224 | tf_op jit(solution)/shard_map/ppermute | solution.py:461
  5.7 2.6 %attend_more.1 = (bf16[128,512]{1,0:T(8,128)(2,1)S(1)}, bf16[8,512,128]{2,1,0:T(8,128)(2,1)S(1)}, bf16[1024,2048]{1,0:T(8,128)(2,1)S(1)}) custom-call(s32[1]{0:T(128)} %bitcast.block_ref, bf16[1024,512]{1,0:T(8,128)(2,1)S(1)} %get-tuple-element.48.key_lat, bf16[1024,128]{1,0:T(8,128)(2,1)S(1)} %get-tuple-element.49.key_rot, ...), custom_call_target="tpu_custom_call" | custom-call | flops 268435456 | bytes 8388608 | tf_op jit(solution)/shard_map/attend_more/pallas_call | solution.py:191
  10.2 1.8 %collective-permute-start.1 = (bf16[32,2048]{1,0:T(8,128)(2,1)S(1)}, bf16[32,2048]{1,0:T(8,128)(2,1)S(1)}, u32[]{:S(2)}, u32[]{:S(2)}) collective-permute-start(bf16[32,2048]{1,0:T(8,128)(2,1)S(1)} %project.1), channel_id=1, source_target_pairs={{0,1},{1,0},{2,3},{3,2},{4,5},{5,4},{6,7},{7,6},{8,9},{9,8},{10,11... | collective-permute-start | bytes 393224 | tf_op jit(solution)/shard_map/ppermute | solution.py:461
  12.3 2.9 %collective-permute-done.1 = bf16[32,2048]{1,0:T(8,128)(2,1)S(1)} collective-permute-done((bf16[32,2048]{1,0:T(8,128)(2,1)S(1)}, bf16[32,2048]{1,0:T(8,128)(2,1)S(1)}, u32[]{:S(2)}, u32[]{:S(2)}) %collective-permute-start.1) | collective-permute-done | bytes 131104 | tf_op jit(solution)/shard_map/ppermute | solution.py:461
  15.3 3.9 %collective-permute-start.4 = (bf16[16,2176]{1,0:T(8,128)(2,1)S(1)}, bf16[16,2176]{1,0:T(8,128)(2,1)S(1)}, u32[]{:S(2)}, u32[]{:S(2)}) collective-permute-start(bf16[16,2176]{1,0:T(8,128)(2,1)S(1)} %fusion.1), channel_id=1, source_target_pairs={{0,24},{1,25},{2,26},{3,27},{4,28},{5,29},{6,30},{7,31},{8,0},{9,1... | collective-permute-start | bytes 208904 | tf_op jit(solution)/shard_map/ppermute | solution.py:461
  20.2 1.6 %collective-permute-start.8 = (bf16[32,2176]{1,0:T(8,128)(2,1)S(1)}, bf16[32,2176]{1,0:T(8,128)(2,1)S(1)}, u32[]{:S(2)}, u32[]{:S(2)}) collective-permute-start(bf16[32,2176]{1,0:T(8,128)(2,1)S(1)} %pad_maximum_fusion.1.refs_0_), channel_id=1, source_target_pairs={{0,4},{1,5},{2,6},{3,7},{4,0},{5,1},{6,2},{7,3},{8,12},{9,13},{10,... | collective-permute-start | bytes 417800 | tf_op jit(solution)/shard_map/ppermute | solution.py:461
  21.8 2.6 %collective-permute-done.3 = bf16[16,2176]{1,0:T(8,128)(2,1)S(1)} collective-permute-done((bf16[16,2176]{1,0:T(8,128)(2,1)S(1)}, bf16[16,2176]{1,0:T(8,128)(2,1)S(1)}, u32[]{:S(2)}, u32[]{:S(2)}) %collective-permute-start.3) | collective-permute-done | bytes 69664 | tf_op jit(solution)/shard_map/ppermute | solution.py:461
  25.4 1.6 %collective-permute-start.5 = (bf16[48,2176]{1,0:T(8,128)(2,1)S(1)}, bf16[48,2176]{1,0:T(8,128)(2,1)S(1)}, u32[]{:S(2)}, u32[]{:S(2)}) collective-permute-start(bf16[48,2176]{1,0:T(8,128)(2,1)S(1)} %pad_maximum_fusion.after_ref.refs_2_), channel_id=1, source_target_pairs={{0,1},{1,0},{2,3},{3,2},{4,5},{5,4},{6,7},{7,6},{8,9},{9,8},{10,11... | collective-permute-start | bytes 626696 | tf_op jit(solution)/shard_map/ppermute | solution.py:461
  27.0 1.5 %collective-permute-start.6 = (bf16[48,2176]{1,0:T(8,128)(2,1)S(1)}, bf16[48,2176]{1,0:T(8,128)(2,1)S(1)}, u32[]{:S(2)}, u32[]{:S(2)}) collective-permute-start(bf16[48,2176]{1,0:T(8,128)(2,1)S(1)} %pad_maximum_fusion.after_ref.refs_2_), channel_id=1, source_target_pairs={{0,4},{1,5},{2,6},{3,7},{4,0},{5,1},{6,2},{7,3},{8,12},{9,13},{10,... | collective-permute-start | bytes 626696 | tf_op jit(solution)/shard_map/ppermute | solution.py:461
  29.0 3.6 %stage.1 = (bf16[704,2048]{1,0:T(8,128)(2,1)S(1)}, bf16[704,2048]{1,0:T(8,128)(2,1)S(1)}, bf16[704,2048]{1,0:T(8,128)(2,1)S(1)}, f32[8,128]{1,0:T(8,128)S(1)}) custom-call(bf16[48,2176]{1,0:T(8,128)(2,1)S(1)} %pad_maximum_fusion.after_ref.refs_2_, bf16[704,2048]{1,0:T(8,128)(2,1)} %bitcast.14, bf16[704,2048]{1,0:T(8,128)(2,1)} %bitcast.15, ...), custom_call_target="tpu_custom_call" | custom-call | bytes 17301504 | tf_op jit(solution)/shard_map/stage/pallas_call | solution.py:272
  32.6 2.7 %experts.2 = (bf16[112,2048]{1,0:T(8,128)(2,1)S(1)}, bf16[112,2048]{1,0:T(8,128)(2,1)S(1)}) custom-call(s32[1]{0:T(128)} %bitcast.2.slot_ref, f32[8,128]{1,0:T(8,128)S(1)} %get-tuple-element.61.after_ref, bf16[704,2048]{1,0:T(8,128)(2,1)S(1)} %get-tuple-element.62.gate_ref, bf16[704,2048]{1,0:T(8,128)(2,1)S(1)} %get-tuple-element.63.up_ref, ...), custom_call_target="tpu_custom_call" | custom-call | flops 1 | bytes 1 | tf_op jit(solution)/shard_map/experts/pallas_call | solution.py:332
  35.3 3.4 %collective-permute-done.6.refs_1_ = bf16[48,2176]{1,0:T(8,128)(2,1)S(1)} collective-permute-done((bf16[48,2176]{1,0:T(8,128)(2,1)S(1)}, bf16[48,2176]{1,0:T(8,128)(2,1)S(1)}, u32[]{:S(2)}, u32[]{:S(2)}) %collective-permute-start.6) | collective-permute-done | bytes 208928 | tf_op jit(solution)/shard_map/ppermute | solution.py:461
  40.6 1.6 %collective-permute-start.16 = (bf16[32,2048]{1,0:T(8,128)(2,1)S(1)}, bf16[32,2048]{1,0:T(8,128)(2,1)S(1)}, u32[]{:S(2)}, u32[]{:S(2)}) collective-permute-start(bf16[32,2048]{1,0:T(8,128)(2,1)S(1)} %get-tuple-element.74), channel_id=1, source_target_pairs={{0,4},{1,5},{2,6},{3,7},{4,0},{5,1},{6,2},{7,3},{8,12},{9,13},{10,... | collective-permute-start | bytes 393224 | tf_op jit(solution)/shard_map/ppermute | solution.py:461
  42.2 3.1 %experts.3 = (bf16[48,2048]{1,0:T(8,128)(2,1)S(1)}, bf16[48,2048]{1,0:T(8,128)(2,1)S(1)}, bf16[48,2048]{1,0:T(8,128)(2,1)S(1)}, bf16[144,2048]{1,0:T(8,128)(2,1)S(1)}) custom-call(s32[1]{0:T(128)} %bitcast.2.slot_ref, f32[8,128]{1,0:T(8,128)S(1)} %get-tuple-element.61.after_ref, bf16[704,2048]{1,0:T(8,128)(2,1)S(1)} %get-tuple-element.62.gate_ref, ...), custom_call_target="tpu_custom_call" | custom-call | flops 1 | bytes 1 | tf_op jit(solution)/shard_map/experts/pallas_call | solution.py:332
  46.2 2.0 %collective-permute-done.17.crossed_ref = bf16[144,2048]{1,0:T(8,128)(2,1)S(1)} collective-permute-done((bf16[144,2048]{1,0:T(8,128)(2,1)S(1)}, bf16[144,2048]{1,0:T(8,128)(2,1)S(1)}, u32[]{:S(2)}, u32[]{:S(2)}) %collective-permute-start.17) | collective-permute-done | bytes 589856 | tf_op jit(solution)/shard_map/ppermute | solution.py:461
  48.4 1.3 %collective-permute-start.18 = (bf16[48,2048]{1,0:T(8,128)(2,1)S(1)}, bf16[48,2048]{1,0:T(8,128)(2,1)S(1)}, u32[]{:S(2)}, u32[]{:S(2)}) collective-permute-start(bf16[48,2048]{1,0:T(8,128)(2,1)S(1)} %get-tuple-element.80.after_ref), channel_id=1, source_target_pairs={{0,1},{1,0},{2,3},{3,2},{4,5},{5,4},{6,7},{7,6},{8,9},{9,8},{10,11... | collective-permute-start | bytes 589832 | tf_op jit(solution)/shard_map/ppermute | solution.py:461
  50.5 1.4 %collective-permute-start.20 = (bf16[48,2048]{1,0:T(8,128)(2,1)S(1)}, bf16[48,2048]{1,0:T(8,128)(2,1)S(1)}, u32[]{:S(2)}, u32[]{:S(2)}) collective-permute-start(bf16[48,2048]{1,0:T(8,128)(2,1)S(1)} %get-tuple-element.86), channel_id=1, source_target_pairs={{0,5},{1,4},{2,7},{3,6},{4,1},{5,0},{6,3},{7,2},{8,13},{9,12},{10,... | collective-permute-start | bytes 589832 | tf_op jit(solution)/shard_map/ppermute | solution.py:461
  51.9 4.4 %shared.1 = (f32[16,2048]{1,0:T(8,128)S(1)}, f32[16,2048]{1,0:T(8,128)S(1)}) custom-call(bf16[704,2048]{1,0:T(8,128)(2,1)} %bitcast.17, bf16[704,2048]{1,0:T(8,128)(2,1)} %bitcast.18, bf16[704,2048]{1,0:T(8,128)(2,1)} %down_hbm.1, bf16[48,2048]{1,0:T(8,128)(2,1)S(1)} %get-tuple-element.80.after_ref, bf16[32,2048]{1,0:T(8,128)(2,1)S(1)} %add_convert_fusion.rows_ref.pair_ref), custom_call_target="tpu_custom_call" | custom-call | flops 276824064 | bytes 17301504 | tf_op jit(solution)/shard_map/shared/pallas_call | solution.py:427
  56.4 1.3 %collective-permute-start.24 = (bf16[16,2048]{1,0:T(8,128)(2,1)S(1)}, bf16[16,2048]{1,0:T(8,128)(2,1)S(1)}, u32[]{:S(2)}, u32[]{:S(2)}) collective-permute-start(bf16[16,2048]{1,0:T(8,128)(2,1)S(1)} %get-tuple-element.90), channel_id=1, source_target_pairs={{0,1},{1,0},{2,3},{3,2},{4,5},{5,4},{6,7},{7,6},{8,9},{9,8},{10,11... | collective-permute-start | bytes 196616 | tf_op jit(solution)/shard_map/ppermute | solution.py:461
  58.2 3.0 %collective-permute-done.20.refs_2_ = bf16[48,2048]{1,0:T(8,128)(2,1)S(1)} collective-permute-done((bf16[48,2048]{1,0:T(8,128)(2,1)S(1)}, bf16[48,2048]{1,0:T(8,128)(2,1)S(1)}, u32[]{:S(2)}, u32[]{:S(2)}) %collective-permute-start.20) | collective-permute-done | bytes 196640 | tf_op jit(solution)/shard_map/ppermute | solution.py:461
  62.6 1.9 %collective-permute-start.23 = (bf16[16,2048]{1,0:T(8,128)(2,1)S(1)}, bf16[16,2048]{1,0:T(8,128)(2,1)S(1)}, u32[]{:S(2)}, u32[]{:S(2)}) collective-permute-start(bf16[16,2048]{1,0:T(8,128)(2,1)S(1)} %get-tuple-element.89), channel_id=1, source_target_pairs={{0,8},{1,9},{2,10},{3,11},{4,12},{5,13},{6,14},{7,15},{8,16},{9,17... | collective-permute-start | bytes 196616 | tf_op jit(solution)/shard_map/ppermute | solution.py:461
  64.6 1.9 %collective-permute-done.21.refs_0_ = bf16[16,2048]{1,0:T(8,128)(2,1)S(1)} collective-permute-done((bf16[16,2048]{1,0:T(8,128)(2,1)S(1)}, bf16[16,2048]{1,0:T(8,128)(2,1)S(1)}, u32[]{:S(2)}, u32[]{:S(2)}) %collective-permute-start.21) | collective-permute-done | bytes 65568 | tf_op jit(solution)/shard_map/ppermute | solution.py:461
  66.4 2.6 %collective-permute-done.22.refs_1_ = bf16[16,2048]{1,0:T(8,128)(2,1)S(1)} collective-permute-done((bf16[16,2048]{1,0:T(8,128)(2,1)S(1)}, bf16[16,2048]{1,0:T(8,128)(2,1)S(1)}, u32[]{:S(2)}, u32[]{:S(2)}) %collective-permute-start.22) | collective-permute-done | bytes 65568 | tf_op jit(solution)/shard_map/ppermute | solution.py:461
  (59 shorter events, 11.3 us)
Async XLA Ops:
  2.7 6.5 %collective-permute-start = (bf16[128,512]{1,0:T(8,128)(2,1)S(1)}, bf16[128,512]{1,0:T(8,128)(2,1)S(1)}, u32[]{:S(2)}, u32[]{:S(2)}) collective-permute-start(bf16[128,512]{1,0:T(8,128)(2,1)S(1)} %get-tuple-element.53), channel_id=1, source_target_pairs={{0,1},{1,0},{2,3},{3,2},{4,5},{5,4},{6,7},{7,6},{8,9},{9,8},{10,11... | collective-permute-start | bytes 393224 | tf_op jit(solution)/shard_map/ppermute | solution.py:461
  10.2 5.0 %collective-permute-start.1 = (bf16[32,2048]{1,0:T(8,128)(2,1)S(1)}, bf16[32,2048]{1,0:T(8,128)(2,1)S(1)}, u32[]{:S(2)}, u32[]{:S(2)}) collective-permute-start(bf16[32,2048]{1,0:T(8,128)(2,1)S(1)} %project.1), channel_id=1, source_target_pairs={{0,1},{1,0},{2,3},{3,2},{4,5},{5,4},{6,7},{7,6},{8,9},{9,8},{10,11... | collective-permute-start | bytes 393224 | tf_op jit(solution)/shard_map/ppermute | solution.py:461
  15.3 6.5 %collective-permute-start.4 = (bf16[16,2176]{1,0:T(8,128)(2,1)S(1)}, bf16[16,2176]{1,0:T(8,128)(2,1)S(1)}, u32[]{:S(2)}, u32[]{:S(2)}) collective-permute-start(bf16[16,2176]{1,0:T(8,128)(2,1)S(1)} %fusion.1), channel_id=1, source_target_pairs={{0,24},{1,25},{2,26},{3,27},{4,28},{5,29},{6,30},{7,31},{8,0},{9,1... | collective-permute-start | bytes 208904 | tf_op jit(solution)/shard_map/ppermute | solution.py:461
  19.2 5.2 %collective-permute-start.3 = (bf16[16,2176]{1,0:T(8,128)(2,1)S(1)}, bf16[16,2176]{1,0:T(8,128)(2,1)S(1)}, u32[]{:S(2)}, u32[]{:S(2)}) collective-permute-start(bf16[16,2176]{1,0:T(8,128)(2,1)S(1)} %fusion.1), channel_id=1, source_target_pairs={{0,16},{1,17},{2,18},{3,19},{4,20},{5,21},{6,22},{7,23},{8,24},{9,... | collective-permute-start | bytes 208904 | tf_op jit(solution)/shard_map/ppermute | solution.py:461
  19.2 6.1 %collective-permute-start.2 = (bf16[16,2176]{1,0:T(8,128)(2,1)S(1)}, bf16[16,2176]{1,0:T(8,128)(2,1)S(1)}, u32[]{:S(2)}, u32[]{:S(2)}) collective-permute-start(bf16[16,2176]{1,0:T(8,128)(2,1)S(1)} %fusion.1), channel_id=1, source_target_pairs={{0,8},{1,9},{2,10},{3,11},{4,12},{5,13},{6,14},{7,15},{8,16},{9,17... | collective-permute-start | bytes 208904 | tf_op jit(solution)/shard_map/ppermute | solution.py:461
  20.2 8.3 %collective-permute-start.8 = (bf16[32,2176]{1,0:T(8,128)(2,1)S(1)}, bf16[32,2176]{1,0:T(8,128)(2,1)S(1)}, u32[]{:S(2)}, u32[]{:S(2)}) collective-permute-start(bf16[32,2176]{1,0:T(8,128)(2,1)S(1)} %pad_maximum_fusion.1.refs_0_), channel_id=1, source_target_pairs={{0,4},{1,5},{2,6},{3,7},{4,0},{5,1},{6,2},{7,3},{8,12},{9,13},{10,... | collective-permute-start | bytes 417800 | tf_op jit(solution)/shard_map/ppermute | solution.py:461
  21.8 7.2 %collective-permute-start.9 = (bf16[32,2176]{1,0:T(8,128)(2,1)S(1)}, bf16[32,2176]{1,0:T(8,128)(2,1)S(1)}, u32[]{:S(2)}, u32[]{:S(2)}) collective-permute-start(bf16[32,2176]{1,0:T(8,128)(2,1)S(1)} %pad_maximum_fusion.1.refs_0_), channel_id=1, source_target_pairs={{0,2},{1,3},{2,0},{3,1},{4,6},{5,7},{6,4},{7,5},{8,10},{9,11},{10,... | collective-permute-start | bytes 417800 | tf_op jit(solution)/shard_map/ppermute | solution.py:461
  25.4 7.2 %collective-permute-start.11 = (bf16[48,2176]{1,0:T(8,128)(2,1)S(1)}, bf16[48,2176]{1,0:T(8,128)(2,1)S(1)}, u32[]{:S(2)}, u32[]{:S(2)}) collective-permute-start(bf16[48,2176]{1,0:T(8,128)(2,1)S(1)} %pad_maximum_fusion.after_ref.refs_2_), channel_id=1, source_target_pairs={{0,2},{1,3},{2,0},{3,1},{4,6},{5,7},{6,4},{7,5},{8,10},{9,11},{10,... | collective-permute-start | bytes 626696 | tf_op jit(solution)/shard_map/ppermute | solution.py:461
  25.4 9.8 %collective-permute-start.5 = (bf16[48,2176]{1,0:T(8,128)(2,1)S(1)}, bf16[48,2176]{1,0:T(8,128)(2,1)S(1)}, u32[]{:S(2)}, u32[]{:S(2)}) collective-permute-start(bf16[48,2176]{1,0:T(8,128)(2,1)S(1)} %pad_maximum_fusion.after_ref.refs_2_), channel_id=1, source_target_pairs={{0,1},{1,0},{2,3},{3,2},{4,5},{5,4},{6,7},{7,6},{8,9},{9,8},{10,11... | collective-permute-start | bytes 626696 | tf_op jit(solution)/shard_map/ppermute | solution.py:461
  27.0 11.7 %collective-permute-start.6 = (bf16[48,2176]{1,0:T(8,128)(2,1)S(1)}, bf16[48,2176]{1,0:T(8,128)(2,1)S(1)}, u32[]{:S(2)}, u32[]{:S(2)}) collective-permute-start(bf16[48,2176]{1,0:T(8,128)(2,1)S(1)} %pad_maximum_fusion.after_ref.refs_2_), channel_id=1, source_target_pairs={{0,4},{1,5},{2,6},{3,7},{4,0},{5,1},{6,2},{7,3},{8,12},{9,13},{10,... | collective-permute-start | bytes 626696 | tf_op jit(solution)/shard_map/ppermute | solution.py:461
  28.5 10.2 %collective-permute-start.7 = (bf16[48,2176]{1,0:T(8,128)(2,1)S(1)}, bf16[48,2176]{1,0:T(8,128)(2,1)S(1)}, u32[]{:S(2)}, u32[]{:S(2)}) collective-permute-start(bf16[48,2176]{1,0:T(8,128)(2,1)S(1)} %pad_maximum_fusion.after_ref.refs_2_), channel_id=1, source_target_pairs={{0,5},{1,4},{2,7},{3,6},{4,1},{5,0},{6,3},{7,2},{8,13},{9,12},{10,... | collective-permute-start | bytes 626696 | tf_op jit(solution)/shard_map/ppermute | solution.py:461
  29.0 3.6 %collective-permute-start.10 = (bf16[32,2176]{1,0:T(8,128)(2,1)S(1)}, bf16[32,2176]{1,0:T(8,128)(2,1)S(1)}, u32[]{:S(2)}, u32[]{:S(2)}) collective-permute-start(bf16[32,2176]{1,0:T(8,128)(2,1)S(1)} %collective-permute-done.8.refs_1_), channel_id=1, source_target_pairs={{0,2},{1,3},{2,0},{3,1},{4,6},{5,7},{6,4},{7,5},{8,10},{9,11},{10,... | collective-permute-start | bytes 417800 | tf_op jit(solution)/shard_map/ppermute | solution.py:461
  38.7 3.5 %collective-permute-start.13 = (bf16[48,2176]{1,0:T(8,128)(2,1)S(1)}, bf16[48,2176]{1,0:T(8,128)(2,1)S(1)}, u32[]{:S(2)}, u32[]{:S(2)}) collective-permute-start(bf16[48,2176]{1,0:T(8,128)(2,1)S(1)} %collective-permute-done.5.refs_0_), channel_id=1, source_target_pairs={{0,2},{1,3},{2,0},{3,1},{4,6},{5,7},{6,4},{7,5},{8,10},{9,11},{10,... | collective-permute-start | bytes 626696 | tf_op jit(solution)/shard_map/ppermute | solution.py:461
  39.2 3.0 %collective-permute-start.14 = (bf16[48,2176]{1,0:T(8,128)(2,1)S(1)}, bf16[48,2176]{1,0:T(8,128)(2,1)S(1)}, u32[]{:S(2)}, u32[]{:S(2)}) collective-permute-start(bf16[48,2176]{1,0:T(8,128)(2,1)S(1)} %collective-permute-done.6.refs_1_), channel_id=1, source_target_pairs={{0,2},{1,3},{2,0},{3,1},{4,6},{5,7},{6,4},{7,5},{8,10},{9,11},{10,... | collective-permute-start | bytes 626696 | tf_op jit(solution)/shard_map/ppermute | solution.py:461
  39.2 3.0 %collective-permute-start.15 = (bf16[48,2176]{1,0:T(8,128)(2,1)S(1)}, bf16[48,2176]{1,0:T(8,128)(2,1)S(1)}, u32[]{:S(2)}, u32[]{:S(2)}) collective-permute-start(bf16[48,2176]{1,0:T(8,128)(2,1)S(1)} %collective-permute-done.7.refs_2_), channel_id=1, source_target_pairs={{0,2},{1,3},{2,0},{3,1},{4,6},{5,7},{6,4},{7,5},{8,10},{9,11},{10,... | collective-permute-start | bytes 626696 | tf_op jit(solution)/shard_map/ppermute | solution.py:461
  40.6 5.6 %collective-permute-start.16 = (bf16[32,2048]{1,0:T(8,128)(2,1)S(1)}, bf16[32,2048]{1,0:T(8,128)(2,1)S(1)}, u32[]{:S(2)}, u32[]{:S(2)}) collective-permute-start(bf16[32,2048]{1,0:T(8,128)(2,1)S(1)} %get-tuple-element.74), channel_id=1, source_target_pairs={{0,4},{1,5},{2,6},{3,7},{4,0},{5,1},{6,2},{7,3},{8,12},{9,13},{10,... | collective-permute-start | bytes 393224 | tf_op jit(solution)/shard_map/ppermute | solution.py:461
  46.2 2.0 %collective-permute-start.17 = (bf16[144,2048]{1,0:T(8,128)(2,1)S(1)}, bf16[144,2048]{1,0:T(8,128)(2,1)S(1)}, u32[]{:S(2)}, u32[]{:S(2)}) collective-permute-start(bf16[144,2048]{1,0:T(8,128)(2,1)S(1)} %get-tuple-element.76), channel_id=1, source_target_pairs={{0,2},{1,3},{2,0},{3,1},{4,6},{5,7},{6,4},{7,5},{8,10},{9,11},{10,... | collective-permute-start | bytes 1769480 | tf_op jit(solution)/shard_map/ppermute | solution.py:461
  48.4 9.3 %collective-permute-start.18 = (bf16[48,2048]{1,0:T(8,128)(2,1)S(1)}, bf16[48,2048]{1,0:T(8,128)(2,1)S(1)}, u32[]{:S(2)}, u32[]{:S(2)}) collective-permute-start(bf16[48,2048]{1,0:T(8,128)(2,1)S(1)} %get-tuple-element.80.after_ref), channel_id=1, source_target_pairs={{0,1},{1,0},{2,3},{3,2},{4,5},{5,4},{6,7},{7,6},{8,9},{9,8},{10,11... | collective-permute-start | bytes 589832 | tf_op jit(solution)/shard_map/ppermute | solution.py:461
  49.7 8.5 %collective-permute-start.19 = (bf16[48,2048]{1,0:T(8,128)(2,1)S(1)}, bf16[48,2048]{1,0:T(8,128)(2,1)S(1)}, u32[]{:S(2)}, u32[]{:S(2)}) collective-permute-start(bf16[48,2048]{1,0:T(8,128)(2,1)S(1)} %get-tuple-element.85), channel_id=1, source_target_pairs={{0,4},{1,5},{2,6},{3,7},{4,0},{5,1},{6,2},{7,3},{8,12},{9,13},{10,... | collective-permute-start | bytes 589832 | tf_op jit(solution)/shard_map/ppermute | solution.py:461
  50.5 10.8 %collective-permute-start.20 = (bf16[48,2048]{1,0:T(8,128)(2,1)S(1)}, bf16[48,2048]{1,0:T(8,128)(2,1)S(1)}, u32[]{:S(2)}, u32[]{:S(2)}) collective-permute-start(bf16[48,2048]{1,0:T(8,128)(2,1)S(1)} %get-tuple-element.86), channel_id=1, source_target_pairs={{0,5},{1,4},{2,7},{3,6},{4,1},{5,0},{6,3},{7,2},{8,13},{9,12},{10,... | collective-permute-start | bytes 589832 | tf_op jit(solution)/shard_map/ppermute | solution.py:461
  56.4 8.2 %collective-permute-start.24 = (bf16[16,2048]{1,0:T(8,128)(2,1)S(1)}, bf16[16,2048]{1,0:T(8,128)(2,1)S(1)}, u32[]{:S(2)}, u32[]{:S(2)}) collective-permute-start(bf16[16,2048]{1,0:T(8,128)(2,1)S(1)} %get-tuple-element.90), channel_id=1, source_target_pairs={{0,1},{1,0},{2,3},{3,2},{4,5},{5,4},{6,7},{7,6},{8,9},{9,8},{10,11... | collective-permute-start | bytes 196616 | tf_op jit(solution)/shard_map/ppermute | solution.py:461
  61.4 5.1 %collective-permute-start.21 = (bf16[16,2048]{1,0:T(8,128)(2,1)S(1)}, bf16[16,2048]{1,0:T(8,128)(2,1)S(1)}, u32[]{:S(2)}, u32[]{:S(2)}) collective-permute-start(bf16[16,2048]{1,0:T(8,128)(2,1)S(1)} %get-tuple-element.87), channel_id=1, source_target_pairs={{0,24},{1,25},{2,26},{3,27},{4,28},{5,29},{6,30},{7,31},{8,0},{9,1... | collective-permute-start | bytes 196616 | tf_op jit(solution)/shard_map/ppermute | solution.py:461
  62.4 6.6 %collective-permute-start.22 = (bf16[16,2048]{1,0:T(8,128)(2,1)S(1)}, bf16[16,2048]{1,0:T(8,128)(2,1)S(1)}, u32[]{:S(2)}, u32[]{:S(2)}) collective-permute-start(bf16[16,2048]{1,0:T(8,128)(2,1)S(1)} %get-tuple-element.88), channel_id=1, source_target_pairs={{0,16},{1,17},{2,18},{3,19},{4,20},{5,21},{6,22},{7,23},{8,24},{9,... | collective-permute-start | bytes 196616 | tf_op jit(solution)/shard_map/ppermute | solution.py:461
  62.6 6.5 %collective-permute-start.23 = (bf16[16,2048]{1,0:T(8,128)(2,1)S(1)}, bf16[16,2048]{1,0:T(8,128)(2,1)S(1)}, u32[]{:S(2)}, u32[]{:S(2)}) collective-permute-start(bf16[16,2048]{1,0:T(8,128)(2,1)S(1)} %get-tuple-element.89), channel_id=1, source_target_pairs={{0,8},{1,9},{2,10},{3,11},{4,12},{5,13},{6,14},{7,15},{8,16},{9,17... | collective-permute-start | bytes 196616 | tf_op jit(solution)/shard_map/ppermute | solution.py:461
  (6 other events, 35.7 us)

commit v4 on v3

--- a/solution.py
+++ b/solution.py
@@ -303,11 +303,12 @@
     units, model = gate_ref.shape
     columns = 512
     slot = slot_ref[0]
+    tails = min(ref.shape[1] for ref in inputs) - model
     weights, at = [], 0
     for ref in inputs:
         rows[at : at + ref.shape[0], :] = ref[:, :model]
         at += ref.shape[0]
-        tail = ref[:, model:].astype(jnp.float32)
+        tail = ref[:, model : model + tails].astype(jnp.float32)
         lane = lax.broadcasted_iota(jnp.int32, tail.shape, 1)
         mine = (lane == slot) | (lane == slot + tail.shape[1] // 2)
         weights.append(jnp.sum(jnp.where(mine, tail, 0.0), axis=1, keepdims=True))
@@ -361,7 +362,10 @@
     at = 0
     for mine, out in zip(refs[: len(refs) // 2], refs[len(refs) // 2 :]):
         other = crossed_ref[at : at + mine.shape[0], :]
-        out[...] = (mine[...].astype(jnp.float32) + other.astype(jnp.float32)).astype(out.dtype)
+        total = mine[...].astype(jnp.float32) + other.astype(jnp.float32)
+        out[:, : total.shape[1]] = total.astype(out.dtype)
+        if out.shape[1] > total.shape[1]:
+            out[:, total.shape[1] :] = jnp.zeros((out.shape[0], LANES), out.dtype)
         at += mine.shape[0]
 
 
@@ -384,7 +388,7 @@
     arrived, outs = refs[:3], refs[3:]
     total = distant_ref[...]
     for ref in arrived:
-        total = total + ref[...].astype(jnp.float32)
+        total = total + ref[:, : total.shape[1]].astype(jnp.float32)
     own = outs[0].shape[0]
     for number, out in enumerate(outs):
         out[...] = total[number * own : (number + 1) * own].astype(out.dtype)
@@ -485,8 +489,10 @@
     line = [swap(rows[own:], dz=step) for step in (3, 2, 1)][::-1]
     across = swap(rows, dy=1)
     distant = jnp.concatenate(line, axis=0)
-    distant, slot = lax.optimization_barrier((distant, slot))
-    planes = [swap(distant, **by) for by in directions]
+    wide = jnp.concatenate([distant, jnp.zeros((distant.shape[0], LANES), distant.dtype)], axis=1)
+    distant, wide, slot = lax.optimization_barrier((distant, wide, slot))
+    sent = (distant, distant, wide)
+    planes = [swap(value, **by) for value, by in zip(sent, directions)]
     early = [rows, across, distant]
     depth, width = sum(value.shape[0] for value in early), distant.shape[0]
     weights, token = stage(distant, weights)
@@ -510,7 +516,7 @@
         add_kernel,
         "add",
         [swap(crossed, dc=1), *last[:3]],
-        [((width, model), jnp.bfloat16)] * 3,
+        [((width, model + more), jnp.bfloat16) for more in (0, 0, 0)],
     )
     returned = [swap(value, **by) for value, by in zip(sums, directions)]
     away_terms, own_terms = run_shared(sums[0], pair, 2, *shared)

time: 70 us -> 68.5 us (0.979)
  waiting for transfers between devices: 22.5 us -> 19.1 us
  starting transfers between devices: 25.6 us -> 27.5 us
    ppermute x25, waiting for transfers between devices: 22.5 us -> 19.1 us  [exchanges(): return lambda value, **by: lax.ppermute(value, AXES, moves(**by))]
    ppermute x25, starting transfers between devices: 25.6 us -> 27.5 us  [exchanges(): return lambda value, **by: lax.ppermute(value, AXES, moves(**by))]
  transfers between devices with their start and end apart: 25 -> 25, of which waited for: 12 -> 13; matrix products, arithmetic and copies ran while one was open for 0% -> 1% of each run, Pallas kernels for 24% -> 24%
where the time goes in v4:
time: 68.5 us; the launch traced here: 68.4 us
  starting transfers between devices  27.5 us (40%)
  Pallas kernels  21.1 us (31%)
  waiting for transfers between devices  19.1 us (28%)
    ppermute x25, starting transfers between devices, exchanges(): return lambda value, **by: lax.ppermute(value, AXES, moves(**by))  27.5 us
    ppermute x25, waiting for transfers between devices, exchanges(): return lambda value, **by: lax.ppermute(value, AXES, moves(**by))  19.1 us
    pallas_call x2, Pallas kernels, run_experts(): pl.pallas_call(functools.partial(expert_kernel, len(inputs)), in_specs=[p...  5.73 us
    pallas_call x1, Pallas kernels, run_shared(): pl.pallas_call(shared_kernel, in_specs=[anywhere] * 4 + [vmem], out_specs...  4.35 us
    pallas_call x1, Pallas kernels, stage(): pl.pallas_call(functools.partial(stage_kernel, len(values)), in_specs=[an...  3.56 us
    pallas_call x1, Pallas kernels, attend(): pl.pallas_call(attend_kernel, in_specs=[pl.BlockSpec(memory_space=pltpu.S...  2.7 us
    pallas_call x1, Pallas kernels, attend_more(): pl.pallas_call(functools.partial(attend_more_kernel, len(values)), in_spe...  2.63 us
  transfers between devices with their start and end apart: 25, of which 13 were waited for; matrix products, arithmetic and copies ran while one was open for 1% of the time, Pallas kernels for 24%

profile of v4, /device:TPU:0, one launch (start us, length us, event | category | flops | bytes accessed | tf_op | source)
XLA Modules:
  0.0 68.4 jit_solution(11943171623740192390)
XLA Ops:
  0.0 2.7 %attend.1 = (bf16[128,512]{1,0:T(8,128)(2,1)S(1)}, bf16[1024,512]{1,0:T(8,128)(2,1)S(1)}, bf16[1024,128]{1,0:T(8,128)(2,1)S(1)}, f32[16,1024]{1,0:T(8,128)S(1)}) custom-call(s32[1]{0:T(128)} %bitcast.1.block_ref, s32[16]{0:T(128)} %lengths_hbm.1, s32[16,9]{1,0:T(8,128)} %table_hbm.1, bf16[16,8192]{1,0:T(8,128)(2,1)} %query_hbm.3, bf16[16,1024]{1,0:T(8,128)(2,1)} %rot_hbm.3, ...), custom_call_target="tpu_custom_call" | custom-call | flops 268435456 | bytes 4194304 | tf_op jit(solution)/shard_map/attend/pallas_call | solution.py:129
  2.7 3.0 %collective-permute-start = (bf16[128,512]{1,0:T(8,128)(2,1)S(1)}, bf16[128,512]{1,0:T(8,128)(2,1)S(1)}, u32[]{:S(2)}, u32[]{:S(2)}) collective-permute-start(bf16[128,512]{1,0:T(8,128)(2,1)S(1)} %get-tuple-element.54), channel_id=1, source_target_pairs={{0,1},{1,0},{2,3},{3,2},{4,5},{5,4},{6,7},{7,6},{8,9},{9,8},{10,11... | collective-permute-start | bytes 393224 | tf_op jit(solution)/shard_map/ppermute | solution.py:465
  5.7 2.6 %attend_more.1 = (bf16[128,512]{1,0:T(8,128)(2,1)S(1)}, bf16[8,512,128]{2,1,0:T(8,128)(2,1)S(1)}, bf16[1024,2048]{1,0:T(8,128)(2,1)S(1)}) custom-call(s32[1]{0:T(128)} %bitcast.block_ref, bf16[1024,512]{1,0:T(8,128)(2,1)S(1)} %get-tuple-element.49.key_lat, bf16[1024,128]{1,0:T(8,128)(2,1)S(1)} %get-tuple-element.50.key_rot, ...), custom_call_target="tpu_custom_call" | custom-call | flops 268435456 | bytes 8388608 | tf_op jit(solution)/shard_map/attend_more/pallas_call | solution.py:191
  10.2 1.8 %collective-permute-start.1 = (bf16[32,2048]{1,0:T(8,128)(2,1)S(1)}, bf16[32,2048]{1,0:T(8,128)(2,1)S(1)}, u32[]{:S(2)}, u32[]{:S(2)}) collective-permute-start(bf16[32,2048]{1,0:T(8,128)(2,1)S(1)} %project.1), channel_id=1, source_target_pairs={{0,1},{1,0},{2,3},{3,2},{4,5},{5,4},{6,7},{7,6},{8,9},{9,8},{10,11... | collective-permute-start | bytes 393224 | tf_op jit(solution)/shard_map/ppermute | solution.py:465
  12.3 2.9 %collective-permute-done.1 = bf16[32,2048]{1,0:T(8,128)(2,1)S(1)} collective-permute-done((bf16[32,2048]{1,0:T(8,128)(2,1)S(1)}, bf16[32,2048]{1,0:T(8,128)(2,1)S(1)}, u32[]{:S(2)}, u32[]{:S(2)}) %collective-permute-start.1) | collective-permute-done | bytes 131104 | tf_op jit(solution)/shard_map/ppermute | solution.py:465
  15.3 1.9 %collective-permute-start.2 = (bf16[16,2176]{1,0:T(8,128)(2,1)S(1)}, bf16[16,2176]{1,0:T(8,128)(2,1)S(1)}, u32[]{:S(2)}, u32[]{:S(2)}) collective-permute-start(bf16[16,2176]{1,0:T(8,128)(2,1)S(1)} %fusion.1), channel_id=1, source_target_pairs={{0,8},{1,9},{2,10},{3,11},{4,12},{5,13},{6,14},{7,15},{8,16},{9,17... | collective-permute-start | bytes 208904 | tf_op jit(solution)/shard_map/ppermute | solution.py:465
  17.2 2.6 %collective-permute-start.3 = (bf16[16,2176]{1,0:T(8,128)(2,1)S(1)}, bf16[16,2176]{1,0:T(8,128)(2,1)S(1)}, u32[]{:S(2)}, u32[]{:S(2)}) collective-permute-start(bf16[16,2176]{1,0:T(8,128)(2,1)S(1)} %fusion.1), channel_id=1, source_target_pairs={{0,16},{1,17},{2,18},{3,19},{4,20},{5,21},{6,22},{7,23},{8,24},{9,... | collective-permute-start | bytes 208904 | tf_op jit(solution)/shard_map/ppermute | solution.py:465
  19.8 1.3 %collective-permute-start.4 = (bf16[16,2176]{1,0:T(8,128)(2,1)S(1)}, bf16[16,2176]{1,0:T(8,128)(2,1)S(1)}, u32[]{:S(2)}, u32[]{:S(2)}) collective-permute-start(bf16[16,2176]{1,0:T(8,128)(2,1)S(1)} %fusion.1), channel_id=1, source_target_pairs={{0,24},{1,25},{2,26},{3,27},{4,28},{5,29},{6,30},{7,31},{8,0},{9,1... | collective-permute-start | bytes 208904 | tf_op jit(solution)/shard_map/ppermute | solution.py:465
  21.1 1.6 %collective-permute-start.8 = (bf16[32,2176]{1,0:T(8,128)(2,1)S(1)}, bf16[32,2176]{1,0:T(8,128)(2,1)S(1)}, u32[]{:S(2)}, u32[]{:S(2)}) collective-permute-start(bf16[32,2176]{1,0:T(8,128)(2,1)S(1)} %pad_maximum_fusion.refs_0_), channel_id=1, source_target_pairs={{0,4},{1,5},{2,6},{3,7},{4,0},{5,1},{6,2},{7,3},{8,12},{9,13},{10,... | collective-permute-start | bytes 417800 | tf_op jit(solution)/shard_map/ppermute | solution.py:465
  24.1 2.5 %collective-permute-start.7 = (bf16[48,2304]{1,0:T(8,128)(2,1)S(1)}, bf16[48,2304]{1,0:T(8,128)(2,1)S(1)}, u32[]{:S(2)}, u32[]{:S(2)}) collective-permute-start(bf16[48,2304]{1,0:T(8,128)(2,1)S(1)} %concatenate.27), channel_id=1, source_target_pairs={{0,5},{1,4},{2,7},{3,6},{4,1},{5,0},{6,3},{7,2},{8,13},{9,12},{10,... | collective-permute-start | bytes 663560 | tf_op jit(solution)/shard_map/ppermute | solution.py:465
  27.7 2.4 %collective-permute-start.6 = (bf16[48,2176]{1,0:T(8,128)(2,1)S(1)}, bf16[48,2176]{1,0:T(8,128)(2,1)S(1)}, u32[]{:S(2)}, u32[]{:S(2)}) collective-permute-start(bf16[48,2176]{1,0:T(8,128)(2,1)S(1)} %constant_dynamic-update-slice_fusion.after_ref.refs_2_), channel_id=1, source_target_pairs={{0,4},{1,5},{2,6},{3,7},{4,0},{5,1},{6,2},{7,3},{8,12},{9,13},{10,... | collective-permute-start | bytes 626696 | tf_op jit(solution)/shard_map/ppermute | solution.py:465
  30.2 3.6 %stage.1 = (bf16[704,2048]{1,0:T(8,128)(2,1)S(1)}, bf16[704,2048]{1,0:T(8,128)(2,1)S(1)}, bf16[704,2048]{1,0:T(8,128)(2,1)S(1)}, f32[8,128]{1,0:T(8,128)S(1)}) custom-call(bf16[48,2176]{1,0:T(8,128)(2,1)S(1)} %constant_dynamic-update-slice_fusion.after_ref.refs_2_, bf16[704,2048]{1,0:T(8,128)(2,1)} %bitcast.14, bf16[704,2048]{1,0:T(8,128)(2,1)} %bitcast.15, ...), custom_call_target="tpu_custom_call" | custom-call | bytes 17301504 | tf_op jit(solution)/shard_map/stage/pallas_call | solution.py:272
  33.8 2.7 %experts.2 = (bf16[112,2048]{1,0:T(8,128)(2,1)S(1)}, bf16[112,2048]{1,0:T(8,128)(2,1)S(1)}) custom-call(s32[1]{0:T(128)} %bitcast.2.slot_ref, f32[8,128]{1,0:T(8,128)S(1)} %get-tuple-element.63.after_ref, bf16[704,2048]{1,0:T(8,128)(2,1)S(1)} %get-tuple-element.64.gate_ref, bf16[704,2048]{1,0:T(8,128)(2,1)S(1)} %get-tuple-element.65.up_ref, ...), custom_call_target="tpu_custom_call" | custom-call | flops 1 | bytes 1 | tf_op jit(solution)/shard_map/experts/pallas_call | solution.py:333
  39.4 3.1 %experts.3 = (bf16[48,2048]{1,0:T(8,128)(2,1)S(1)}, bf16[48,2048]{1,0:T(8,128)(2,1)S(1)}, bf16[48,2048]{1,0:T(8,128)(2,1)S(1)}, bf16[144,2048]{1,0:T(8,128)(2,1)S(1)}) custom-call(s32[1]{0:T(128)} %bitcast.2.slot_ref, f32[8,128]{1,0:T(8,128)S(1)} %get-tuple-element.63.after_ref, bf16[704,2048]{1,0:T(8,128)(2,1)S(1)} %get-tuple-element.64.gate_ref, ...), custom_call_target="tpu_custom_call" | custom-call | flops 1 | bytes 1 | tf_op jit(solution)/shard_map/experts/pallas_call | solution.py:333
  42.5 2.0 %collective-permute-done.16.line_ref = bf16[32,2048]{1,0:T(8,128)(2,1)S(1)} collective-permute-done((bf16[32,2048]{1,0:T(8,128)(2,1)S(1)}, bf16[32,2048]{1,0:T(8,128)(2,1)S(1)}, u32[]{:S(2)}, u32[]{:S(2)}) %collective-permute-start.16) | collective-permute-done | bytes 131104 | tf_op jit(solution)/shard_map/ppermute | solution.py:465
  44.4 2.0 %collective-permute-done.17.crossed_ref = bf16[144,2048]{1,0:T(8,128)(2,1)S(1)} collective-permute-done((bf16[144,2048]{1,0:T(8,128)(2,1)S(1)}, bf16[144,2048]{1,0:T(8,128)(2,1)S(1)}, u32[]{:S(2)}, u32[]{:S(2)}) %collective-permute-start.17) | collective-permute-done | bytes 589856 | tf_op jit(solution)/shard_map/ppermute | solution.py:465
  46.6 1.6 %collective-permute-start.18 = (bf16[48,2048]{1,0:T(8,128)(2,1)S(1)}, bf16[48,2048]{1,0:T(8,128)(2,1)S(1)}, u32[]{:S(2)}, u32[]{:S(2)}) collective-permute-start(bf16[48,2048]{1,0:T(8,128)(2,1)S(1)} %get-tuple-element.82.after_ref), channel_id=1, source_target_pairs={{0,1},{1,0},{2,3},{3,2},{4,5},{5,4},{6,7},{7,6},{8,9},{9,8},{10,11... | collective-permute-start | bytes 589832 | tf_op jit(solution)/shard_map/ppermute | solution.py:465
  48.4 1.7 %collective-permute-start.20 = (bf16[48,2048]{1,0:T(8,128)(2,1)S(1)}, bf16[48,2048]{1,0:T(8,128)(2,1)S(1)}, u32[]{:S(2)}, u32[]{:S(2)}) collective-permute-start(bf16[48,2048]{1,0:T(8,128)(2,1)S(1)} %get-tuple-element.88), channel_id=1, source_target_pairs={{0,5},{1,4},{2,7},{3,6},{4,1},{5,0},{6,3},{7,2},{8,13},{9,12},{10,... | collective-permute-start | bytes 589832 | tf_op jit(solution)/shard_map/ppermute | solution.py:465
  50.1 4.4 %shared.1 = (f32[16,2048]{1,0:T(8,128)S(1)}, f32[16,2048]{1,0:T(8,128)S(1)}) custom-call(bf16[704,2048]{1,0:T(8,128)(2,1)} %bitcast.17, bf16[704,2048]{1,0:T(8,128)(2,1)} %bitcast.18, bf16[704,2048]{1,0:T(8,128)(2,1)} %down_hbm.1, bf16[48,2048]{1,0:T(8,128)(2,1)S(1)} %get-tuple-element.82.after_ref, bf16[32,2048]{1,0:T(8,128)(2,1)S(1)} %add_convert_fusion.rows_ref.pair_ref), custom_call_target="tpu_custom_call" | custom-call | flops 276824064 | bytes 17301504 | tf_op jit(solution)/shard_map/shared/pallas_call | solution.py:431
  54.5 1.6 %collective-permute-start.24 = (bf16[16,2048]{1,0:T(8,128)(2,1)S(1)}, bf16[16,2048]{1,0:T(8,128)(2,1)S(1)}, u32[]{:S(2)}, u32[]{:S(2)}) collective-permute-start(bf16[16,2048]{1,0:T(8,128)(2,1)S(1)} %get-tuple-element.92), channel_id=1, source_target_pairs={{0,1},{1,0},{2,3},{3,2},{4,5},{5,4},{6,7},{7,6},{8,9},{9,8},{10,11... | collective-permute-start | bytes 196616 | tf_op jit(solution)/shard_map/ppermute | solution.py:465
  56.1 2.9 %collective-permute-done.19.refs_1_ = bf16[48,2048]{1,0:T(8,128)(2,1)S(1)} collective-permute-done((bf16[48,2048]{1,0:T(8,128)(2,1)S(1)}, bf16[48,2048]{1,0:T(8,128)(2,1)S(1)}, u32[]{:S(2)}, u32[]{:S(2)}) %collective-permute-start.19) | collective-permute-done | bytes 196640 | tf_op jit(solution)/shard_map/ppermute | solution.py:465
  59.1 2.4 %collective-permute-start.21 = (bf16[16,2048]{1,0:T(8,128)(2,1)S(1)}, bf16[16,2048]{1,0:T(8,128)(2,1)S(1)}, u32[]{:S(2)}, u32[]{:S(2)}) collective-permute-start(bf16[16,2048]{1,0:T(8,128)(2,1)S(1)} %get-tuple-element.89), channel_id=1, source_target_pairs={{0,24},{1,25},{2,26},{3,27},{4,28},{5,29},{6,30},{7,31},{8,0},{9,1... | collective-permute-start | bytes 196616 | tf_op jit(solution)/shard_map/ppermute | solution.py:465
  62.2 1.4 %collective-permute-done.21.refs_0_ = bf16[16,2048]{1,0:T(8,128)(2,1)S(1)} collective-permute-done((bf16[16,2048]{1,0:T(8,128)(2,1)S(1)}, bf16[16,2048]{1,0:T(8,128)(2,1)S(1)}, u32[]{:S(2)}, u32[]{:S(2)}) %collective-permute-start.21) | collective-permute-done | bytes 65568 | tf_op jit(solution)/shard_map/ppermute | solution.py:465
  63.6 3.1 %collective-permute-done.22.refs_1_ = bf16[16,2048]{1,0:T(8,128)(2,1)S(1)} collective-permute-done((bf16[16,2048]{1,0:T(8,128)(2,1)S(1)}, bf16[16,2048]{1,0:T(8,128)(2,1)S(1)}, u32[]{:S(2)}, u32[]{:S(2)}) %collective-permute-start.22) | collective-permute-done | bytes 65568 | tf_op jit(solution)/shard_map/ppermute | solution.py:465
  (62 shorter events, 10.5 us)
Async XLA Ops:
  2.7 6.5 %collective-permute-start = (bf16[128,512]{1,0:T(8,128)(2,1)S(1)}, bf16[128,512]{1,0:T(8,128)(2,1)S(1)}, u32[]{:S(2)}, u32[]{:S(2)}) collective-permute-start(bf16[128,512]{1,0:T(8,128)(2,1)S(1)} %get-tuple-element.54), channel_id=1, source_target_pairs={{0,1},{1,0},{2,3},{3,2},{4,5},{5,4},{6,7},{7,6},{8,9},{9,8},{10,11... | collective-permute-start | bytes 393224 | tf_op jit(solution)/shard_map/ppermute | solution.py:465
  10.2 5.0 %collective-permute-start.1 = (bf16[32,2048]{1,0:T(8,128)(2,1)S(1)}, bf16[32,2048]{1,0:T(8,128)(2,1)S(1)}, u32[]{:S(2)}, u32[]{:S(2)}) collective-permute-start(bf16[32,2048]{1,0:T(8,128)(2,1)S(1)} %project.1), channel_id=1, source_target_pairs={{0,1},{1,0},{2,3},{3,2},{4,5},{5,4},{6,7},{7,6},{8,9},{9,8},{10,11... | collective-permute-start | bytes 393224 | tf_op jit(solution)/shard_map/ppermute | solution.py:465
  15.3 7.4 %collective-permute-start.2 = (bf16[16,2176]{1,0:T(8,128)(2,1)S(1)}, bf16[16,2176]{1,0:T(8,128)(2,1)S(1)}, u32[]{:S(2)}, u32[]{:S(2)}) collective-permute-start(bf16[16,2176]{1,0:T(8,128)(2,1)S(1)} %fusion.1), channel_id=1, source_target_pairs={{0,8},{1,9},{2,10},{3,11},{4,12},{5,13},{6,14},{7,15},{8,16},{9,17... | collective-permute-start | bytes 208904 | tf_op jit(solution)/shard_map/ppermute | solution.py:465
  17.2 5.6 %collective-permute-start.3 = (bf16[16,2176]{1,0:T(8,128)(2,1)S(1)}, bf16[16,2176]{1,0:T(8,128)(2,1)S(1)}, u32[]{:S(2)}, u32[]{:S(2)}) collective-permute-start(bf16[16,2176]{1,0:T(8,128)(2,1)S(1)} %fusion.1), channel_id=1, source_target_pairs={{0,16},{1,17},{2,18},{3,19},{4,20},{5,21},{6,22},{7,23},{8,24},{9,... | collective-permute-start | bytes 208904 | tf_op jit(solution)/shard_map/ppermute | solution.py:465
  19.8 4.3 %collective-permute-start.4 = (bf16[16,2176]{1,0:T(8,128)(2,1)S(1)}, bf16[16,2176]{1,0:T(8,128)(2,1)S(1)}, u32[]{:S(2)}, u32[]{:S(2)}) collective-permute-start(bf16[16,2176]{1,0:T(8,128)(2,1)S(1)} %fusion.1), channel_id=1, source_target_pairs={{0,24},{1,25},{2,26},{3,27},{4,28},{5,29},{6,30},{7,31},{8,0},{9,1... | collective-permute-start | bytes 208904 | tf_op jit(solution)/shard_map/ppermute | solution.py:465
  21.1 6.6 %collective-permute-start.8 = (bf16[32,2176]{1,0:T(8,128)(2,1)S(1)}, bf16[32,2176]{1,0:T(8,128)(2,1)S(1)}, u32[]{:S(2)}, u32[]{:S(2)}) collective-permute-start(bf16[32,2176]{1,0:T(8,128)(2,1)S(1)} %pad_maximum_fusion.refs_0_), channel_id=1, source_target_pairs={{0,4},{1,5},{2,6},{3,7},{4,0},{5,1},{6,2},{7,3},{8,12},{9,13},{10,... | collective-permute-start | bytes 417800 | tf_op jit(solution)/shard_map/ppermute | solution.py:465
  22.7 7.4 %collective-permute-start.9 = (bf16[32,2176]{1,0:T(8,128)(2,1)S(1)}, bf16[32,2176]{1,0:T(8,128)(2,1)S(1)}, u32[]{:S(2)}, u32[]{:S(2)}) collective-permute-start(bf16[32,2176]{1,0:T(8,128)(2,1)S(1)} %pad_maximum_fusion.refs_0_), channel_id=1, source_target_pairs={{0,2},{1,3},{2,0},{3,1},{4,6},{5,7},{6,4},{7,5},{8,10},{9,11},{10,... | collective-permute-start | bytes 417800 | tf_op jit(solution)/shard_map/ppermute | solution.py:465
  24.1 12.3 %collective-permute-start.7 = (bf16[48,2304]{1,0:T(8,128)(2,1)S(1)}, bf16[48,2304]{1,0:T(8,128)(2,1)S(1)}, u32[]{:S(2)}, u32[]{:S(2)}) collective-permute-start(bf16[48,2304]{1,0:T(8,128)(2,1)S(1)} %concatenate.27), channel_id=1, source_target_pairs={{0,5},{1,4},{2,7},{3,6},{4,1},{5,0},{6,3},{7,2},{8,13},{9,12},{10,... | collective-permute-start | bytes 663560 | tf_op jit(solution)/shard_map/ppermute | solution.py:465
  26.6 7.1 %collective-permute-start.11 = (bf16[48,2176]{1,0:T(8,128)(2,1)S(1)}, bf16[48,2176]{1,0:T(8,128)(2,1)S(1)}, u32[]{:S(2)}, u32[]{:S(2)}) collective-permute-start(bf16[48,2176]{1,0:T(8,128)(2,1)S(1)} %constant_dynamic-update-slice_fusion.after_ref.refs_2_), channel_id=1, source_target_pairs={{0,2},{1,3},{2,0},{3,1},{4,6},{5,7},{6,4},{7,5},{8,10},{9,11},{10,... | collective-permute-start | bytes 626696 | tf_op jit(solution)/shard_map/ppermute | solution.py:465
  26.6 9.8 %collective-permute-start.5 = (bf16[48,2176]{1,0:T(8,128)(2,1)S(1)}, bf16[48,2176]{1,0:T(8,128)(2,1)S(1)}, u32[]{:S(2)}, u32[]{:S(2)}) collective-permute-start(bf16[48,2176]{1,0:T(8,128)(2,1)S(1)} %constant_dynamic-update-slice_fusion.after_ref.refs_2_), channel_id=1, source_target_pairs={{0,1},{1,0},{2,3},{3,2},{4,5},{5,4},{6,7},{7,6},{8,9},{9,8},{10,11... | collective-permute-start | bytes 626696 | tf_op jit(solution)/shard_map/ppermute | solution.py:465
  27.7 8.7 %collective-permute-start.6 = (bf16[48,2176]{1,0:T(8,128)(2,1)S(1)}, bf16[48,2176]{1,0:T(8,128)(2,1)S(1)}, u32[]{:S(2)}, u32[]{:S(2)}) collective-permute-start(bf16[48,2176]{1,0:T(8,128)(2,1)S(1)} %constant_dynamic-update-slice_fusion.after_ref.refs_2_), channel_id=1, source_target_pairs={{0,4},{1,5},{2,6},{3,7},{4,0},{5,1},{6,2},{7,3},{8,12},{9,13},{10,... | collective-permute-start | bytes 626696 | tf_op jit(solution)/shard_map/ppermute | solution.py:465
  30.2 3.6 %collective-permute-start.10 = (bf16[32,2176]{1,0:T(8,128)(2,1)S(1)}, bf16[32,2176]{1,0:T(8,128)(2,1)S(1)}, u32[]{:S(2)}, u32[]{:S(2)}) collective-permute-start(bf16[32,2176]{1,0:T(8,128)(2,1)S(1)} %collective-permute-done.8.refs_1_), channel_id=1, source_target_pairs={{0,2},{1,3},{2,0},{3,1},{4,6},{5,7},{6,4},{7,5},{8,10},{9,11},{10,... | collective-permute-start | bytes 417800 | tf_op jit(solution)/shard_map/ppermute | solution.py:465
  36.5 2.0 %collective-permute-start.12 = (bf16[112,2048]{1,0:T(8,128)(2,1)S(1)}, bf16[112,2048]{1,0:T(8,128)(2,1)S(1)}, u32[]{:S(2)}, u32[]{:S(2)}) collective-permute-start(bf16[112,2048]{1,0:T(8,128)(2,1)S(1)} %get-tuple-element.70), channel_id=1, source_target_pairs={{0,2},{1,3},{2,0},{3,1},{4,6},{5,7},{6,4},{7,5},{8,10},{9,11},{10,... | collective-permute-start | bytes 1376264 | tf_op jit(solution)/shard_map/ppermute | solution.py:465
  37.0 2.4 %collective-permute-start.15 = (bf16[48,2304]{1,0:T(8,128)(2,1)S(1)}, bf16[48,2304]{1,0:T(8,128)(2,1)S(1)}, u32[]{:S(2)}, u32[]{:S(2)}) collective-permute-start(bf16[48,2304]{1,0:T(8,128)(2,1)S(1)} %collective-permute-done.7.refs_2_), channel_id=1, source_target_pairs={{0,2},{1,3},{2,0},{3,1},{4,6},{5,7},{6,4},{7,5},{8,10},{9,11},{10,... | collective-permute-start | bytes 663560 | tf_op jit(solution)/shard_map/ppermute | solution.py:465
  37.1 2.0 %collective-permute-start.13 = (bf16[48,2176]{1,0:T(8,128)(2,1)S(1)}, bf16[48,2176]{1,0:T(8,128)(2,1)S(1)}, u32[]{:S(2)}, u32[]{:S(2)}) collective-permute-start(bf16[48,2176]{1,0:T(8,128)(2,1)S(1)} %collective-permute-done.5.refs_0_), channel_id=1, source_target_pairs={{0,2},{1,3},{2,0},{3,1},{4,6},{5,7},{6,4},{7,5},{8,10},{9,11},{10,... | collective-permute-start | bytes 626696 | tf_op jit(solution)/shard_map/ppermute | solution.py:465
  38.6 5.8 %collective-permute-start.16 = (bf16[32,2048]{1,0:T(8,128)(2,1)S(1)}, bf16[32,2048]{1,0:T(8,128)(2,1)S(1)}, u32[]{:S(2)}, u32[]{:S(2)}) collective-permute-start(bf16[32,2048]{1,0:T(8,128)(2,1)S(1)} %get-tuple-element.76), channel_id=1, source_target_pairs={{0,4},{1,5},{2,6},{3,7},{4,0},{5,1},{6,2},{7,3},{8,12},{9,13},{10,... | collective-permute-start | bytes 393224 | tf_op jit(solution)/shard_map/ppermute | solution.py:465
  44.4 2.0 %collective-permute-start.17 = (bf16[144,2048]{1,0:T(8,128)(2,1)S(1)}, bf16[144,2048]{1,0:T(8,128)(2,1)S(1)}, u32[]{:S(2)}, u32[]{:S(2)}) collective-permute-start(bf16[144,2048]{1,0:T(8,128)(2,1)S(1)} %get-tuple-element.78), channel_id=1, source_target_pairs={{0,2},{1,3},{2,0},{3,1},{4,6},{5,7},{6,4},{7,5},{8,10},{9,11},{10,... | collective-permute-start | bytes 1769480 | tf_op jit(solution)/shard_map/ppermute | solution.py:465
  46.6 9.5 %collective-permute-start.18 = (bf16[48,2048]{1,0:T(8,128)(2,1)S(1)}, bf16[48,2048]{1,0:T(8,128)(2,1)S(1)}, u32[]{:S(2)}, u32[]{:S(2)}) collective-permute-start(bf16[48,2048]{1,0:T(8,128)(2,1)S(1)} %get-tuple-element.82.after_ref), channel_id=1, source_target_pairs={{0,1},{1,0},{2,3},{3,2},{4,5},{5,4},{6,7},{7,6},{8,9},{9,8},{10,11... | collective-permute-start | bytes 589832 | tf_op jit(solution)/shard_map/ppermute | solution.py:465
  48.1 10.9 %collective-permute-start.19 = (bf16[48,2048]{1,0:T(8,128)(2,1)S(1)}, bf16[48,2048]{1,0:T(8,128)(2,1)S(1)}, u32[]{:S(2)}, u32[]{:S(2)}) collective-permute-start(bf16[48,2048]{1,0:T(8,128)(2,1)S(1)} %get-tuple-element.87), channel_id=1, source_target_pairs={{0,4},{1,5},{2,6},{3,7},{4,0},{5,1},{6,2},{7,3},{8,12},{9,13},{10,... | collective-permute-start | bytes 589832 | tf_op jit(solution)/shard_map/ppermute | solution.py:465
  48.4 10.6 %collective-permute-start.20 = (bf16[48,2048]{1,0:T(8,128)(2,1)S(1)}, bf16[48,2048]{1,0:T(8,128)(2,1)S(1)}, u32[]{:S(2)}, u32[]{:S(2)}) collective-permute-start(bf16[48,2048]{1,0:T(8,128)(2,1)S(1)} %get-tuple-element.88), channel_id=1, source_target_pairs={{0,5},{1,4},{2,7},{3,6},{4,1},{5,0},{6,3},{7,2},{8,13},{9,12},{10,... | collective-permute-start | bytes 589832 | tf_op jit(solution)/shard_map/ppermute | solution.py:465
  54.5 7.7 %collective-permute-start.24 = (bf16[16,2048]{1,0:T(8,128)(2,1)S(1)}, bf16[16,2048]{1,0:T(8,128)(2,1)S(1)}, u32[]{:S(2)}, u32[]{:S(2)}) collective-permute-start(bf16[16,2048]{1,0:T(8,128)(2,1)S(1)} %get-tuple-element.92), channel_id=1, source_target_pairs={{0,1},{1,0},{2,3},{3,2},{4,5},{5,4},{6,7},{7,6},{8,9},{9,8},{10,11... | collective-permute-start | bytes 196616 | tf_op jit(solution)/shard_map/ppermute | solution.py:465
  59.1 4.5 %collective-permute-start.21 = (bf16[16,2048]{1,0:T(8,128)(2,1)S(1)}, bf16[16,2048]{1,0:T(8,128)(2,1)S(1)}, u32[]{:S(2)}, u32[]{:S(2)}) collective-permute-start(bf16[16,2048]{1,0:T(8,128)(2,1)S(1)} %get-tuple-element.89), channel_id=1, source_target_pairs={{0,24},{1,25},{2,26},{3,27},{4,28},{5,29},{6,30},{7,31},{8,0},{9,1... | collective-permute-start | bytes 196616 | tf_op jit(solution)/shard_map/ppermute | solution.py:465
  61.5 5.2 %collective-permute-start.22 = (bf16[16,2048]{1,0:T(8,128)(2,1)S(1)}, bf16[16,2048]{1,0:T(8,128)(2,1)S(1)}, u32[]{:S(2)}, u32[]{:S(2)}) collective-permute-start(bf16[16,2048]{1,0:T(8,128)(2,1)S(1)} %get-tuple-element.90), channel_id=1, source_target_pairs={{0,16},{1,17},{2,18},{3,19},{4,20},{5,21},{6,22},{7,23},{8,24},{9,... | collective-permute-start | bytes 196616 | tf_op jit(solution)/shard_map/ppermute | solution.py:465
  61.5 6.1 %collective-permute-start.23 = (bf16[16,2048]{1,0:T(8,128)(2,1)S(1)}, bf16[16,2048]{1,0:T(8,128)(2,1)S(1)}, u32[]{:S(2)}, u32[]{:S(2)}) collective-permute-start(bf16[16,2048]{1,0:T(8,128)(2,1)S(1)} %get-tuple-element.91), channel_id=1, source_target_pairs={{0,8},{1,9},{2,10},{3,11},{4,12},{5,13},{6,14},{7,15},{8,16},{9,17... | collective-permute-start | bytes 196616 | tf_op jit(solution)/shard_map/ppermute | solution.py:465
  (6 other events, 36.1 us)

commit v5 on v4

--- a/solution.py
+++ b/solution.py
@@ -380,7 +380,8 @@
 def merge_near_kernel(near_ref, line_ref, pair_ref, away_terms, own_terms, away, mixed):
     own = mixed.shape[0]
     total = near_ref[...] + line_ref[...].astype(jnp.float32)
-    away[...] = (total[:own] + away_terms[...]).astype(away.dtype)
+    away[:, : total.shape[1]] = (total[:own] + away_terms[...]).astype(away.dtype)
+    away[:, total.shape[1] :] = jnp.zeros((own, away.shape[1] - total.shape[1]), away.dtype)
     mixed[...] = total[own:] + own_terms[...] + pair_ref[own:, :].astype(jnp.float32)
 
 
@@ -391,7 +392,10 @@
         total = total + ref[:, : total.shape[1]].astype(jnp.float32)
     own = outs[0].shape[0]
     for number, out in enumerate(outs):
-        out[...] = total[number * own : (number + 1) * own].astype(out.dtype)
+        piece = total[number * own : (number + 1) * own].astype(out.dtype)
+        out[:, : piece.shape[1]] = piece
+        if out.shape[1] > piece.shape[1]:
+            out[:, piece.shape[1] :] = jnp.zeros((own, out.shape[1] - piece.shape[1]), out.dtype)
 
 
 def shared_kernel(gate_hbm, up_hbm, down_hbm, after_ref, rows_ref, *refs):
@@ -451,13 +455,13 @@
 
 
 def exchanges(groups, replicas):
-    lines, depth = replicas, groups // (2 * replicas)
+    lines = replicas
 
     def moves(dz=0, dy=0, dc=0, dx=0):
         pairs = []
         for group in range(groups):
             z, y, core = group // (2 * lines), group // 2 % lines, group % 2
-            other = ((z + dz) % depth * lines + (y ^ dy)) * 2 + (core ^ dc)
+            other = ((z ^ dz) * lines + (y ^ dy)) * 2 + (core ^ dc)
             for rep in range(replicas):
                 pairs.append((group * replicas + rep, other * replicas + (rep ^ dx)))
         return pairs
@@ -511,28 +515,31 @@
             ((width, model), jnp.float32),
         ],
     )
-    crossed, back = lax.optimization_barrier((last[3], swap(back, dy=1)))
+    crossed, back = last[3], swap(back, dy=1)
     sums = all_in_vmem(
         add_kernel,
         "add",
         [swap(crossed, dc=1), *last[:3]],
-        [((width, model + more), jnp.bfloat16) for more in (0, 0, 0)],
+        [((width, model + more), jnp.bfloat16) for more in (0, LANES, 0)],
     )
     returned = [swap(value, **by) for value, by in zip(sums, directions)]
     away_terms, own_terms = run_shared(sums[0], pair, 2, *shared)
+    *returned, away_terms, own_terms = lax.optimization_barrier(
+        (*returned, away_terms, own_terms)
+    )
     away, mixed = all_in_vmem(
         merge_near_kernel,
         "merge_near",
         [near, back, pair, away_terms, own_terms],
-        [((own, model), jnp.bfloat16), ((own, model), jnp.float32)],
+        [((own, model + LANES), jnp.bfloat16), ((own, model), jnp.float32)],
     )
     pieces = all_in_vmem(
         merge_far_kernel,
         "merge_far",
         [distant_sum, *returned],
-        [((own, model), jnp.bfloat16)] * 3,
-    )
-    pieces = [swap(piece, dz=-step) for step, piece in zip((1, 2, 3), pieces)]
+        [((own, model + more), jnp.bfloat16) for more in (0, 2 * LANES, 2 * LANES)],
+    )
+    pieces = [swap(piece, dz=step) for step, piece in zip((1, 2, 3), pieces)]
     return mixed, [*pieces, swap(away, dx=1)]
 
 
@@ -540,7 +547,7 @@
     pieces, out = refs[:-1], refs[-1]
     mixed = mixed_ref[...]
     for piece in pieces:
-        mixed = mixed + piece[...].astype(jnp.float32)
+        mixed = mixed + piece[:, : mixed.shape[1]].astype(jnp.float32)
     inverse = lax.rsqrt(jnp.mean(mixed * mixed, axis=1, keepdims=True) + EPSILON)
     out[...] = (mixed * inverse * gain_ref[...]).astype(out.dtype)
 

time: 68.5 us -> 66.8 us (0.975)
  starting transfers between devices: 27.5 us -> 26.1 us
    ppermute x25, starting transfers between devices: 27.5 us -> 26.1 us  [exchanges(): return lambda value, **by: lax.ppermute(value, AXES, moves(**by))]
  transfers between devices with their start and end apart: 25 -> 25, of which waited for: 13 -> 11; matrix products, arithmetic and copies ran while one was open for 1% -> 1% of each run, Pallas kernels for 24% -> 20%
where the time goes in v5:
time: 66.8 us; the launch traced here: 66.7 us
  starting transfers between devices  26.1 us (39%)
  Pallas kernels  21.1 us (32%)
  waiting for transfers between devices  18.8 us (28%)
    ppermute x25, starting transfers between devices, exchanges(): return lambda value, **by: lax.ppermute(value, AXES, moves(**by))  26.1 us
    ppermute x25, waiting for transfers between devices, exchanges(): return lambda value, **by: lax.ppermute(value, AXES, moves(**by))  18.8 us
    pallas_call x2, Pallas kernels, run_experts(): pl.pallas_call(functools.partial(expert_kernel, len(inputs)), in_specs=[p...  5.74 us
    pallas_call x1, Pallas kernels, run_shared(): pl.pallas_call(shared_kernel, in_specs=[anywhere] * 4 + [vmem], out_specs...  4.36 us
    pallas_call x1, Pallas kernels, stage(): pl.pallas_call(functools.partial(stage_kernel, len(values)), in_specs=[an...  3.56 us
    pallas_call x1, Pallas kernels, attend(): pl.pallas_call(attend_kernel, in_specs=[pl.BlockSpec(memory_space=pltpu.S...  2.7 us
    pallas_call x1, Pallas kernels, attend_more(): pl.pallas_call(functools.partial(attend_more_kernel, len(values)), in_spe...  2.63 us
  transfers between devices with their start and end apart: 25, of which 11 were waited for; matrix products, arithmetic and copies ran while one was open for 1% of the time, Pallas kernels for 20%

profile of v5, /device:TPU:0, one launch (start us, length us, event | category | flops | bytes accessed | tf_op | source)
XLA Modules:
  0.0 66.7 jit_solution(6089715706964292353)
XLA Ops:
  0.0 2.7 %attend.1 = (bf16[128,512]{1,0:T(8,128)(2,1)S(1)}, bf16[1024,512]{1,0:T(8,128)(2,1)S(1)}, bf16[1024,128]{1,0:T(8,128)(2,1)S(1)}, f32[16,1024]{1,0:T(8,128)S(1)}) custom-call(s32[1]{0:T(128)} %bitcast.1.block_ref, s32[16]{0:T(128)} %lengths_hbm.1, s32[16,9]{1,0:T(8,128)} %table_hbm.1, bf16[16,8192]{1,0:T(8,128)(2,1)} %query_hbm.3, bf16[16,1024]{1,0:T(8,128)(2,1)} %rot_hbm.3, ...), custom_call_target="tpu_custom_call" | custom-call | flops 268435456 | bytes 4194304 | tf_op jit(solution)/shard_map/attend/pallas_call | solution.py:129
  2.7 3.0 %collective-permute-start = (bf16[128,512]{1,0:T(8,128)(2,1)S(1)}, bf16[128,512]{1,0:T(8,128)(2,1)S(1)}, u32[]{:S(2)}, u32[]{:S(2)}) collective-permute-start(bf16[128,512]{1,0:T(8,128)(2,1)S(1)} %get-tuple-element.57), channel_id=1, source_target_pairs={{0,1},{1,0},{2,3},{3,2},{4,5},{5,4},{6,7},{7,6},{8,9},{9,8},{10,11... | collective-permute-start | bytes 393224 | tf_op jit(solution)/shard_map/ppermute | solution.py:469
  5.7 2.6 %attend_more.1 = (bf16[128,512]{1,0:T(8,128)(2,1)S(1)}, bf16[8,512,128]{2,1,0:T(8,128)(2,1)S(1)}, bf16[1024,2048]{1,0:T(8,128)(2,1)S(1)}) custom-call(s32[1]{0:T(128)} %bitcast.block_ref, bf16[1024,512]{1,0:T(8,128)(2,1)S(1)} %get-tuple-element.52.key_lat, bf16[1024,128]{1,0:T(8,128)(2,1)S(1)} %get-tuple-element.53.key_rot, ...), custom_call_target="tpu_custom_call" | custom-call | flops 268435456 | bytes 8388608 | tf_op jit(solution)/shard_map/attend_more/pallas_call | solution.py:191
  10.2 1.8 %collective-permute-start.1 = (bf16[32,2048]{1,0:T(8,128)(2,1)S(1)}, bf16[32,2048]{1,0:T(8,128)(2,1)S(1)}, u32[]{:S(2)}, u32[]{:S(2)}) collective-permute-start(bf16[32,2048]{1,0:T(8,128)(2,1)S(1)} %project.1), channel_id=1, source_target_pairs={{0,1},{1,0},{2,3},{3,2},{4,5},{5,4},{6,7},{7,6},{8,9},{9,8},{10,11... | collective-permute-start | bytes 393224 | tf_op jit(solution)/shard_map/ppermute | solution.py:469
  12.3 2.9 %collective-permute-done.1 = bf16[32,2048]{1,0:T(8,128)(2,1)S(1)} collective-permute-done((bf16[32,2048]{1,0:T(8,128)(2,1)S(1)}, bf16[32,2048]{1,0:T(8,128)(2,1)S(1)}, u32[]{:S(2)}, u32[]{:S(2)}) %collective-permute-start.1) | collective-permute-done | bytes 131104 | tf_op jit(solution)/shard_map/ppermute | solution.py:469
  15.3 1.9 %collective-permute-start.2 = (bf16[16,2176]{1,0:T(8,128)(2,1)S(1)}, bf16[16,2176]{1,0:T(8,128)(2,1)S(1)}, u32[]{:S(2)}, u32[]{:S(2)}) collective-permute-start(bf16[16,2176]{1,0:T(8,128)(2,1)S(1)} %fusion.1), channel_id=1, source_target_pairs={{0,8},{1,9},{2,10},{3,11},{4,12},{5,13},{6,14},{7,15},{8,0},{9,1},... | collective-permute-start | bytes 208904 | tf_op jit(solution)/shard_map/ppermute | solution.py:469
  17.2 2.6 %collective-permute-start.3 = (bf16[16,2176]{1,0:T(8,128)(2,1)S(1)}, bf16[16,2176]{1,0:T(8,128)(2,1)S(1)}, u32[]{:S(2)}, u32[]{:S(2)}) collective-permute-start(bf16[16,2176]{1,0:T(8,128)(2,1)S(1)} %fusion.1), channel_id=1, source_target_pairs={{0,16},{1,17},{2,18},{3,19},{4,20},{5,21},{6,22},{7,23},{8,24},{9,... | collective-permute-start | bytes 208904 | tf_op jit(solution)/shard_map/ppermute | solution.py:469
  19.8 1.8 %collective-permute-start.8 = (bf16[32,2176]{1,0:T(8,128)(2,1)S(1)}, bf16[32,2176]{1,0:T(8,128)(2,1)S(1)}, u32[]{:S(2)}, u32[]{:S(2)}) collective-permute-start(bf16[32,2176]{1,0:T(8,128)(2,1)S(1)} %pad_maximum_fusion.refs_0_), channel_id=1, source_target_pairs={{0,4},{1,5},{2,6},{3,7},{4,0},{5,1},{6,2},{7,3},{8,12},{9,13},{10,... | collective-permute-start | bytes 417800 | tf_op jit(solution)/shard_map/ppermute | solution.py:469
  21.6 2.2 %collective-permute-done.3 = bf16[16,2176]{1,0:T(8,128)(2,1)S(1)} collective-permute-done((bf16[16,2176]{1,0:T(8,128)(2,1)S(1)}, bf16[16,2176]{1,0:T(8,128)(2,1)S(1)}, u32[]{:S(2)}, u32[]{:S(2)}) %collective-permute-start.3) | collective-permute-done | bytes 69664 | tf_op jit(solution)/shard_map/ppermute | solution.py:469
  23.8 2.1 %collective-permute-done.4 = bf16[16,2176]{1,0:T(8,128)(2,1)S(1)} collective-permute-done((bf16[16,2176]{1,0:T(8,128)(2,1)S(1)}, bf16[16,2176]{1,0:T(8,128)(2,1)S(1)}, u32[]{:S(2)}, u32[]{:S(2)}) %collective-permute-start.4) | collective-permute-done | bytes 69664 | tf_op jit(solution)/shard_map/ppermute | solution.py:469
  25.9 2.5 %collective-permute-start.7 = (bf16[48,2304]{1,0:T(8,128)(2,1)S(1)}, bf16[48,2304]{1,0:T(8,128)(2,1)S(1)}, u32[]{:S(2)}, u32[]{:S(2)}) collective-permute-start(bf16[48,2304]{1,0:T(8,128)(2,1)S(1)} %concatenate.27), channel_id=1, source_target_pairs={{0,5},{1,4},{2,7},{3,6},{4,1},{5,0},{6,3},{7,2},{8,13},{9,12},{10,... | collective-permute-start | bytes 663560 | tf_op jit(solution)/shard_map/ppermute | solution.py:469
  29.5 3.6 %stage.1 = (bf16[704,2048]{1,0:T(8,128)(2,1)S(1)}, bf16[704,2048]{1,0:T(8,128)(2,1)S(1)}, bf16[704,2048]{1,0:T(8,128)(2,1)S(1)}, f32[8,128]{1,0:T(8,128)S(1)}) custom-call(bf16[48,2176]{1,0:T(8,128)(2,1)S(1)} %constant_dynamic-update-slice_fusion.after_ref.refs_2_, bf16[704,2048]{1,0:T(8,128)(2,1)} %bitcast.14, bf16[704,2048]{1,0:T(8,128)(2,1)} %bitcast.15, ...), custom_call_target="tpu_custom_call" | custom-call | bytes 17301504 | tf_op jit(solution)/shard_map/stage/pallas_call | solution.py:272
  33.1 2.7 %experts.2 = (bf16[112,2048]{1,0:T(8,128)(2,1)S(1)}, bf16[112,2048]{1,0:T(8,128)(2,1)S(1)}) custom-call(s32[1]{0:T(128)} %bitcast.2.slot_ref, f32[8,128]{1,0:T(8,128)S(1)} %get-tuple-element.66.after_ref, bf16[704,2048]{1,0:T(8,128)(2,1)S(1)} %get-tuple-element.67.gate_ref, bf16[704,2048]{1,0:T(8,128)(2,1)S(1)} %get-tuple-element.68.up_ref, ...), custom_call_target="tpu_custom_call" | custom-call | flops 1 | bytes 1 | tf_op jit(solution)/shard_map/experts/pallas_call | solution.py:333
  35.8 1.6 %collective-permute-done.5.refs_0_ = bf16[48,2176]{1,0:T(8,128)(2,1)S(1)} collective-permute-done((bf16[48,2176]{1,0:T(8,128)(2,1)S(1)}, bf16[48,2176]{1,0:T(8,128)(2,1)S(1)}, u32[]{:S(2)}, u32[]{:S(2)}) %collective-permute-start.5) | collective-permute-done | bytes 208928 | tf_op jit(solution)/shard_map/ppermute | solution.py:469
  39.6 3.1 %experts.3 = (bf16[48,2048]{1,0:T(8,128)(2,1)S(1)}, bf16[48,2048]{1,0:T(8,128)(2,1)S(1)}, bf16[48,2048]{1,0:T(8,128)(2,1)S(1)}, bf16[144,2048]{1,0:T(8,128)(2,1)S(1)}) custom-call(s32[1]{0:T(128)} %bitcast.2.slot_ref, f32[8,128]{1,0:T(8,128)S(1)} %get-tuple-element.66.after_ref, bf16[704,2048]{1,0:T(8,128)(2,1)S(1)} %get-tuple-element.67.gate_ref, ...), custom_call_target="tpu_custom_call" | custom-call | flops 1 | bytes 1 | tf_op jit(solution)/shard_map/experts/pallas_call | solution.py:333
  43.2 1.5 %collective-permute-done.17.crossed_ref = bf16[144,2048]{1,0:T(8,128)(2,1)S(1)} collective-permute-done((bf16[144,2048]{1,0:T(8,128)(2,1)S(1)}, bf16[144,2048]{1,0:T(8,128)(2,1)S(1)}, u32[]{:S(2)}, u32[]{:S(2)}) %collective-permute-start.17) | collective-permute-done | bytes 589856 | tf_op jit(solution)/shard_map/ppermute | solution.py:469
  44.8 1.4 %collective-permute-start.19 = (bf16[48,2176]{1,0:T(8,128)(2,1)S(1)}, bf16[48,2176]{1,0:T(8,128)(2,1)S(1)}, u32[]{:S(2)}, u32[]{:S(2)}) collective-permute-start(bf16[48,2176]{1,0:T(8,128)(2,1)S(1)} %get-tuple-element.84), channel_id=1, source_target_pairs={{0,4},{1,5},{2,6},{3,7},{4,0},{5,1},{6,2},{7,3},{8,12},{9,13},{10,... | collective-permute-start | bytes 626696 | tf_op jit(solution)/shard_map/ppermute | solution.py:469
  46.3 1.6 %collective-permute-start.18 = (bf16[48,2048]{1,0:T(8,128)(2,1)S(1)}, bf16[48,2048]{1,0:T(8,128)(2,1)S(1)}, u32[]{:S(2)}, u32[]{:S(2)}) collective-permute-start(bf16[48,2048]{1,0:T(8,128)(2,1)S(1)} %get-tuple-element.83.after_ref), channel_id=1, source_target_pairs={{0,1},{1,0},{2,3},{3,2},{4,5},{5,4},{6,7},{7,6},{8,9},{9,8},{10,11... | collective-permute-start | bytes 589832 | tf_op jit(solution)/shard_map/ppermute | solution.py:469
  48.5 1.4 %collective-permute-start.13 = (bf16[32,2048]{1,0:T(8,128)(2,1)S(1)}, bf16[32,2048]{1,0:T(8,128)(2,1)S(1)}, u32[]{:S(2)}, u32[]{:S(2)}) collective-permute-start(bf16[32,2048]{1,0:T(8,128)(2,1)S(1)} %get-tuple-element.75), channel_id=1, source_target_pairs={{0,4},{1,5},{2,6},{3,7},{4,0},{5,1},{6,2},{7,3},{8,12},{9,13},{10,... | collective-permute-start | bytes 393224 | tf_op jit(solution)/shard_map/ppermute | solution.py:469
  49.9 4.4 %shared.1 = (f32[16,2048]{1,0:T(8,128)S(1)}, f32[16,2048]{1,0:T(8,128)S(1)}) custom-call(bf16[704,2048]{1,0:T(8,128)(2,1)} %bitcast.17, bf16[704,2048]{1,0:T(8,128)(2,1)} %bitcast.18, bf16[704,2048]{1,0:T(8,128)(2,1)} %down_hbm.1, bf16[48,2048]{1,0:T(8,128)(2,1)S(1)} %get-tuple-element.83.after_ref, bf16[32,2048]{1,0:T(8,128)(2,1)S(1)} %add_convert_fusion.rows_ref.pair_ref), custom_call_target="tpu_custom_call" | custom-call | flops 276824064 | bytes 17301504 | tf_op jit(solution)/shard_map/shared/pallas_call | solution.py:435
  54.3 3.3 %collective-permute-done.20.refs_2_ = bf16[48,2048]{1,0:T(8,128)(2,1)S(1)} collective-permute-done((bf16[48,2048]{1,0:T(8,128)(2,1)S(1)}, bf16[48,2048]{1,0:T(8,128)(2,1)S(1)}, u32[]{:S(2)}, u32[]{:S(2)}) %collective-permute-start.20) | collective-permute-done | bytes 196640 | tf_op jit(solution)/shard_map/ppermute | solution.py:469
  59.6 1.7 %collective-permute-start.24 = (bf16[16,2176]{1,0:T(8,128)(2,1)S(1)}, bf16[16,2176]{1,0:T(8,128)(2,1)S(1)}, u32[]{:S(2)}, u32[]{:S(2)}) collective-permute-start(bf16[16,2176]{1,0:T(8,128)(2,1)S(1)} %get-tuple-element.98), channel_id=1, source_target_pairs={{0,1},{1,0},{2,3},{3,2},{4,5},{5,4},{6,7},{7,6},{8,9},{9,8},{10,11... | collective-permute-start | bytes 208904 | tf_op jit(solution)/shard_map/ppermute | solution.py:469
  61.3 1.9 %collective-permute-start.21 = (bf16[16,2048]{1,0:T(8,128)(2,1)S(1)}, bf16[16,2048]{1,0:T(8,128)(2,1)S(1)}, u32[]{:S(2)}, u32[]{:S(2)}) collective-permute-start(bf16[16,2048]{1,0:T(8,128)(2,1)S(1)} %get-tuple-element.95), channel_id=1, source_target_pairs={{0,8},{1,9},{2,10},{3,11},{4,12},{5,13},{6,14},{7,15},{8,0},{9,1},... | collective-permute-start | bytes 196616 | tf_op jit(solution)/shard_map/ppermute | solution.py:469
  63.1 2.7 %collective-permute-done.21.refs_0_ = bf16[16,2048]{1,0:T(8,128)(2,1)S(1)} collective-permute-done((bf16[16,2048]{1,0:T(8,128)(2,1)S(1)}, bf16[16,2048]{1,0:T(8,128)(2,1)S(1)}, u32[]{:S(2)}, u32[]{:S(2)}) %collective-permute-start.21) | collective-permute-done | bytes 65568 | tf_op jit(solution)/shard_map/ppermute | solution.py:469
  (62 shorter events, 9.6 us)
Async XLA Ops:
  2.7 6.5 %collective-permute-start = (bf16[128,512]{1,0:T(8,128)(2,1)S(1)}, bf16[128,512]{1,0:T(8,128)(2,1)S(1)}, u32[]{:S(2)}, u32[]{:S(2)}) collective-permute-start(bf16[128,512]{1,0:T(8,128)(2,1)S(1)} %get-tuple-element.57), channel_id=1, source_target_pairs={{0,1},{1,0},{2,3},{3,2},{4,5},{5,4},{6,7},{7,6},{8,9},{9,8},{10,11... | collective-permute-start | bytes 393224 | tf_op jit(solution)/shard_map/ppermute | solution.py:469
  10.2 5.0 %collective-permute-start.1 = (bf16[32,2048]{1,0:T(8,128)(2,1)S(1)}, bf16[32,2048]{1,0:T(8,128)(2,1)S(1)}, u32[]{:S(2)}, u32[]{:S(2)}) collective-permute-start(bf16[32,2048]{1,0:T(8,128)(2,1)S(1)} %project.1), channel_id=1, source_target_pairs={{0,1},{1,0},{2,3},{3,2},{4,5},{5,4},{6,7},{7,6},{8,9},{9,8},{10,11... | collective-permute-start | bytes 393224 | tf_op jit(solution)/shard_map/ppermute | solution.py:469
  15.3 6.3 %collective-permute-start.2 = (bf16[16,2176]{1,0:T(8,128)(2,1)S(1)}, bf16[16,2176]{1,0:T(8,128)(2,1)S(1)}, u32[]{:S(2)}, u32[]{:S(2)}) collective-permute-start(bf16[16,2176]{1,0:T(8,128)(2,1)S(1)} %fusion.1), channel_id=1, source_target_pairs={{0,8},{1,9},{2,10},{3,11},{4,12},{5,13},{6,14},{7,15},{8,0},{9,1},... | collective-permute-start | bytes 208904 | tf_op jit(solution)/shard_map/ppermute | solution.py:469
  17.2 6.6 %collective-permute-start.3 = (bf16[16,2176]{1,0:T(8,128)(2,1)S(1)}, bf16[16,2176]{1,0:T(8,128)(2,1)S(1)}, u32[]{:S(2)}, u32[]{:S(2)}) collective-permute-start(bf16[16,2176]{1,0:T(8,128)(2,1)S(1)} %fusion.1), channel_id=1, source_target_pairs={{0,16},{1,17},{2,18},{3,19},{4,20},{5,21},{6,22},{7,23},{8,24},{9,... | collective-permute-start | bytes 208904 | tf_op jit(solution)/shard_map/ppermute | solution.py:469
  19.8 6.1 %collective-permute-start.4 = (bf16[16,2176]{1,0:T(8,128)(2,1)S(1)}, bf16[16,2176]{1,0:T(8,128)(2,1)S(1)}, u32[]{:S(2)}, u32[]{:S(2)}) collective-permute-start(bf16[16,2176]{1,0:T(8,128)(2,1)S(1)} %fusion.1), channel_id=1, source_target_pairs={{0,24},{1,25},{2,26},{3,27},{4,28},{5,29},{6,30},{7,31},{8,16},{9,... | collective-permute-start | bytes 208904 | tf_op jit(solution)/shard_map/ppermute | solution.py:469
  19.8 9.2 %collective-permute-start.8 = (bf16[32,2176]{1,0:T(8,128)(2,1)S(1)}, bf16[32,2176]{1,0:T(8,128)(2,1)S(1)}, u32[]{:S(2)}, u32[]{:S(2)}) collective-permute-start(bf16[32,2176]{1,0:T(8,128)(2,1)S(1)} %pad_maximum_fusion.refs_0_), channel_id=1, source_target_pairs={{0,4},{1,5},{2,6},{3,7},{4,0},{5,1},{6,2},{7,3},{8,12},{9,13},{10,... | collective-permute-start | bytes 417800 | tf_op jit(solution)/shard_map/ppermute | solution.py:469
  21.6 7.9 %collective-permute-start.9 = (bf16[32,2176]{1,0:T(8,128)(2,1)S(1)}, bf16[32,2176]{1,0:T(8,128)(2,1)S(1)}, u32[]{:S(2)}, u32[]{:S(2)}) collective-permute-start(bf16[32,2176]{1,0:T(8,128)(2,1)S(1)} %pad_maximum_fusion.refs_0_), channel_id=1, source_target_pairs={{0,2},{1,3},{2,0},{3,1},{4,6},{5,7},{6,4},{7,5},{8,10},{9,11},{10,... | collective-permute-start | bytes 417800 | tf_op jit(solution)/shard_map/ppermute | solution.py:469
  25.9 11.5 %collective-permute-start.7 = (bf16[48,2304]{1,0:T(8,128)(2,1)S(1)}, bf16[48,2304]{1,0:T(8,128)(2,1)S(1)}, u32[]{:S(2)}, u32[]{:S(2)}) collective-permute-start(bf16[48,2304]{1,0:T(8,128)(2,1)S(1)} %concatenate.27), channel_id=1, source_target_pairs={{0,5},{1,4},{2,7},{3,6},{4,1},{5,0},{6,3},{7,2},{8,13},{9,12},{10,... | collective-permute-start | bytes 663560 | tf_op jit(solution)/shard_map/ppermute | solution.py:469
  28.4 4.6 %collective-permute-start.11 = (bf16[48,2176]{1,0:T(8,128)(2,1)S(1)}, bf16[48,2176]{1,0:T(8,128)(2,1)S(1)}, u32[]{:S(2)}, u32[]{:S(2)}) collective-permute-start(bf16[48,2176]{1,0:T(8,128)(2,1)S(1)} %constant_dynamic-update-slice_fusion.after_ref.refs_2_), channel_id=1, source_target_pairs={{0,2},{1,3},{2,0},{3,1},{4,6},{5,7},{6,4},{7,5},{8,10},{9,11},{10,... | collective-permute-start | bytes 626696 | tf_op jit(solution)/shard_map/ppermute | solution.py:469
  28.4 8.9 %collective-permute-start.5 = (bf16[48,2176]{1,0:T(8,128)(2,1)S(1)}, bf16[48,2176]{1,0:T(8,128)(2,1)S(1)}, u32[]{:S(2)}, u32[]{:S(2)}) collective-permute-start(bf16[48,2176]{1,0:T(8,128)(2,1)S(1)} %constant_dynamic-update-slice_fusion.after_ref.refs_2_), channel_id=1, source_target_pairs={{0,1},{1,0},{2,3},{3,2},{4,5},{5,4},{6,7},{7,6},{8,9},{9,8},{10,11... | collective-permute-start | bytes 626696 | tf_op jit(solution)/shard_map/ppermute | solution.py:469
  29.0 8.5 %collective-permute-start.6 = (bf16[48,2176]{1,0:T(8,128)(2,1)S(1)}, bf16[48,2176]{1,0:T(8,128)(2,1)S(1)}, u32[]{:S(2)}, u32[]{:S(2)}) collective-permute-start(bf16[48,2176]{1,0:T(8,128)(2,1)S(1)} %constant_dynamic-update-slice_fusion.after_ref.refs_2_), channel_id=1, source_target_pairs={{0,4},{1,5},{2,6},{3,7},{4,0},{5,1},{6,2},{7,3},{8,12},{9,13},{10,... | collective-permute-start | bytes 626696 | tf_op jit(solution)/shard_map/ppermute | solution.py:469
  29.5 3.6 %collective-permute-start.10 = (bf16[32,2176]{1,0:T(8,128)(2,1)S(1)}, bf16[32,2176]{1,0:T(8,128)(2,1)S(1)}, u32[]{:S(2)}, u32[]{:S(2)}) collective-permute-start(bf16[32,2176]{1,0:T(8,128)(2,1)S(1)} %collective-permute-done.8.refs_1_), channel_id=1, source_target_pairs={{0,2},{1,3},{2,0},{3,1},{4,6},{5,7},{6,4},{7,5},{8,10},{9,11},{10,... | collective-permute-start | bytes 417800 | tf_op jit(solution)/shard_map/ppermute | solution.py:469
  37.5 2.1 %collective-permute-start.16 = (bf16[48,2304]{1,0:T(8,128)(2,1)S(1)}, bf16[48,2304]{1,0:T(8,128)(2,1)S(1)}, u32[]{:S(2)}, u32[]{:S(2)}) collective-permute-start(bf16[48,2304]{1,0:T(8,128)(2,1)S(1)} %collective-permute-done.7.refs_2_), channel_id=1, source_target_pairs={{0,2},{1,3},{2,0},{3,1},{4,6},{5,7},{6,4},{7,5},{8,10},{9,11},{10,... | collective-permute-start | bytes 663560 | tf_op jit(solution)/shard_map/ppermute | solution.py:469
  37.5 1.8 %collective-permute-start.14 = (bf16[48,2176]{1,0:T(8,128)(2,1)S(1)}, bf16[48,2176]{1,0:T(8,128)(2,1)S(1)}, u32[]{:S(2)}, u32[]{:S(2)}) collective-permute-start(bf16[48,2176]{1,0:T(8,128)(2,1)S(1)} %collective-permute-done.5.refs_0_), channel_id=1, source_target_pairs={{0,2},{1,3},{2,0},{3,1},{4,6},{5,7},{6,4},{7,5},{8,10},{9,11},{10,... | collective-permute-start | bytes 626696 | tf_op jit(solution)/shard_map/ppermute | solution.py:469
  42.6 2.1 %collective-permute-start.17 = (bf16[144,2048]{1,0:T(8,128)(2,1)S(1)}, bf16[144,2048]{1,0:T(8,128)(2,1)S(1)}, u32[]{:S(2)}, u32[]{:S(2)}) collective-permute-start(bf16[144,2048]{1,0:T(8,128)(2,1)S(1)} %get-tuple-element.79), channel_id=1, source_target_pairs={{0,2},{1,3},{2,0},{3,1},{4,6},{5,7},{6,4},{7,5},{8,10},{9,11},{10,... | collective-permute-start | bytes 1769480 | tf_op jit(solution)/shard_map/ppermute | solution.py:469
  42.9 5.5 %collective-permute-start.12 = (bf16[112,2048]{1,0:T(8,128)(2,1)S(1)}, bf16[112,2048]{1,0:T(8,128)(2,1)S(1)}, u32[]{:S(2)}, u32[]{:S(2)}) collective-permute-start(bf16[112,2048]{1,0:T(8,128)(2,1)S(1)} %get-tuple-element.73), channel_id=1, source_target_pairs={{0,2},{1,3},{2,0},{3,1},{4,6},{5,7},{6,4},{7,5},{8,10},{9,11},{10,... | collective-permute-start | bytes 1376264 | tf_op jit(solution)/shard_map/ppermute | solution.py:469
  44.8 12.8 %collective-permute-start.19 = (bf16[48,2176]{1,0:T(8,128)(2,1)S(1)}, bf16[48,2176]{1,0:T(8,128)(2,1)S(1)}, u32[]{:S(2)}, u32[]{:S(2)}) collective-permute-start(bf16[48,2176]{1,0:T(8,128)(2,1)S(1)} %get-tuple-element.84), channel_id=1, source_target_pairs={{0,4},{1,5},{2,6},{3,7},{4,0},{5,1},{6,2},{7,3},{8,12},{9,13},{10,... | collective-permute-start | bytes 626696 | tf_op jit(solution)/shard_map/ppermute | solution.py:469
  46.3 8.0 %collective-permute-start.18 = (bf16[48,2048]{1,0:T(8,128)(2,1)S(1)}, bf16[48,2048]{1,0:T(8,128)(2,1)S(1)}, u32[]{:S(2)}, u32[]{:S(2)}) collective-permute-start(bf16[48,2048]{1,0:T(8,128)(2,1)S(1)} %get-tuple-element.83.after_ref), channel_id=1, source_target_pairs={{0,1},{1,0},{2,3},{3,2},{4,5},{5,4},{6,7},{7,6},{8,9},{9,8},{10,11... | collective-permute-start | bytes 589832 | tf_op jit(solution)/shard_map/ppermute | solution.py:469
  47.9 9.7 %collective-permute-start.20 = (bf16[48,2048]{1,0:T(8,128)(2,1)S(1)}, bf16[48,2048]{1,0:T(8,128)(2,1)S(1)}, u32[]{:S(2)}, u32[]{:S(2)}) collective-permute-start(bf16[48,2048]{1,0:T(8,128)(2,1)S(1)} %get-tuple-element.85), channel_id=1, source_target_pairs={{0,5},{1,4},{2,7},{3,6},{4,1},{5,0},{6,3},{7,2},{8,13},{9,12},{10,... | collective-permute-start | bytes 589832 | tf_op jit(solution)/shard_map/ppermute | solution.py:469
  48.5 11.0 %collective-permute-start.13 = (bf16[32,2048]{1,0:T(8,128)(2,1)S(1)}, bf16[32,2048]{1,0:T(8,128)(2,1)S(1)}, u32[]{:S(2)}, u32[]{:S(2)}) collective-permute-start(bf16[32,2048]{1,0:T(8,128)(2,1)S(1)} %get-tuple-element.75), channel_id=1, source_target_pairs={{0,4},{1,5},{2,6},{3,7},{4,0},{5,1},{6,2},{7,3},{8,12},{9,13},{10,... | collective-permute-start | bytes 393224 | tf_op jit(solution)/shard_map/ppermute | solution.py:469
  57.7 8.1 %collective-permute-start.22 = (bf16[16,2304]{1,0:T(8,128)(2,1)S(1)}, bf16[16,2304]{1,0:T(8,128)(2,1)S(1)}, u32[]{:S(2)}, u32[]{:S(2)}) collective-permute-start(bf16[16,2304]{1,0:T(8,128)(2,1)S(1)} %get-tuple-element.96), channel_id=1, source_target_pairs={{0,16},{1,17},{2,18},{3,19},{4,20},{5,21},{6,22},{7,23},{8,24},{9,... | collective-permute-start | bytes 221192 | tf_op jit(solution)/shard_map/ppermute | solution.py:469
  58.1 7.8 %collective-permute-start.23 = (bf16[16,2304]{1,0:T(8,128)(2,1)S(1)}, bf16[16,2304]{1,0:T(8,128)(2,1)S(1)}, u32[]{:S(2)}, u32[]{:S(2)}) collective-permute-start(bf16[16,2304]{1,0:T(8,128)(2,1)S(1)} %get-tuple-element.97), channel_id=1, source_target_pairs={{0,24},{1,25},{2,26},{3,27},{4,28},{5,29},{6,30},{7,31},{8,16},{9,... | collective-permute-start | bytes 221192 | tf_op jit(solution)/shard_map/ppermute | solution.py:469
  59.6 6.3 %collective-permute-start.24 = (bf16[16,2176]{1,0:T(8,128)(2,1)S(1)}, bf16[16,2176]{1,0:T(8,128)(2,1)S(1)}, u32[]{:S(2)}, u32[]{:S(2)}) collective-permute-start(bf16[16,2176]{1,0:T(8,128)(2,1)S(1)} %get-tuple-element.98), channel_id=1, source_target_pairs={{0,1},{1,0},{2,3},{3,2},{4,5},{5,4},{6,7},{7,6},{8,9},{9,8},{10,11... | collective-permute-start | bytes 208904 | tf_op jit(solution)/shard_map/ppermute | solution.py:469
  61.3 4.6 %collective-permute-start.21 = (bf16[16,2048]{1,0:T(8,128)(2,1)S(1)}, bf16[16,2048]{1,0:T(8,128)(2,1)S(1)}, u32[]{:S(2)}, u32[]{:S(2)}) collective-permute-start(bf16[16,2048]{1,0:T(8,128)(2,1)S(1)} %get-tuple-element.95), channel_id=1, source_target_pairs={{0,8},{1,9},{2,10},{3,11},{4,12},{5,13},{6,14},{7,15},{8,0},{9,1},... | collective-permute-start | bytes 196616 | tf_op jit(solution)/shard_map/ppermute | solution.py:469
  (6 other events, 34.3 us)
